TPU v7x, 256 devices: a whole 4x4x8 slice. The times are simulated.
256 devices in a mesh: blk: 64 (over z, x_hi, y), rep: 4 (over x_lo, core).
Axes of the slice: x: 4 (x_hi: 2, x_lo: 2; x = x_hi * 2 + x_lo), y: 4, z: 8, core: 2. Of those that a mesh axis runs over, the one named last changes fastest.
Arguments:
- node_feats: bfloat16 [65536, 256], P(('blk', 'rep')), may hold values from -6 to 6
- tile_vals: bfloat16 [64, 4, 128, 128, 128], P('blk', 'rep'), may hold values from -0.0625 to 0.0625
- tile_row: int32 [64, 4, 128], P('blk', 'rep'), may hold values from 0 to 7
- tile_col: int32 [64, 4, 128], P('blk', 'rep'), may hold values from 0 to 127, as said below
- tile_count: int32 [64, 4], P('blk', 'rep'), may hold values from 16 to 128, as said below
- w_agg: bfloat16 [256, 256], replicated, may hold values from -0.375 to 0.375
- w_self: bfloat16 [256, 256], replicated, may hold values from -0.375 to 0.375
- bias: float32 [256], replicated, may hold values from -1 to 1
- cotangent: bfloat16 [65536, 256], P(('blk', 'rep')), may hold values from -6 to 6
Outputs:
- updated: bfloat16 [65536, 256], P(('blk', 'rep'))
- feat_grad: bfloat16 [65536, 256], P(('blk', 'rep'))
- tile_grads: bfloat16 [64, 4, 128, 128, 128], P('blk', 'rep')
- weight_grads: float32 [2, 256, 256], replicated
Inputs may be any that keep to these rules, and one draw needn't show every extreme that they name: `tile_col`: each slot names a column tile of a row group at most 2 cycle steps away or a power of two steps away around the closed cycle of 64 groups. `tile_count`: one of 128, 64, 32 or 16; some (g, r) has exactly 128.
All inputs are finite; a program needn't handle non-finite values.
Results may differ from a plain program's by a relative error of at most 0.0059.
Values may be sent and summed in bfloat16 or wider, within the bound.
No kernel may reach another device: no remote copies, remote signals or barrier semaphores. Data moves between devices by JAX's collectives and lax.ppermute only.
A program may use at most 128 MiB of HBM per device.

v0:
```python
import math

import jax
import jax.numpy as jnp
from jax import lax
from jax.sharding import PartitionSpec as P


def local(node_feats, tile_vals, tile_row, tile_col, tile_count, w_agg, w_self, bias, cotangent):
    high = lax.Precision.HIGHEST
    n_rep = lax.axis_size("rep")
    n_blk = lax.axis_size("blk")
    tile_size = tile_vals.shape[-1]
    feat_width = node_feats.shape[1]
    own_rows = node_feats.shape[0]
    own_tiles = own_rows // tile_size
    row_tiles = n_rep * own_tiles
    values = tile_vals[0, 0]
    row_index = tile_row[0, 0]
    col_index = tile_col[0, 0]
    live_count = tile_count[0, 0]
    slots = values.shape[0]
    live_mask = (jnp.arange(slots, dtype=jnp.int32) < live_count).astype(jnp.float32)
    table_tiles = n_blk * own_tiles
    gathered = lax.all_gather(node_feats, "blk", axis=0, tiled=True)
    col_table = gathered.reshape(table_tiles, tile_size, feat_width)
    col_blocks = col_table[col_index]
    products = jnp.einsum("kij,kjd->kid", values, col_blocks, preferred_element_type=jnp.float32)
    row_hot = (row_index[:, None] == jnp.arange(row_tiles, dtype=jnp.int32)).astype(
        jnp.float32
    ) * live_mask[:, None]
    partial_sum = jnp.einsum("kq,kid->qid", row_hot, products, precision=high).reshape(
        row_tiles * tile_size, feat_width
    )
    aggregate = lax.psum_scatter(partial_sum, "rep", scatter_dimension=0, tiled=True)
    agg_b = aggregate.astype(jnp.bfloat16)
    preact = (
        jnp.dot(agg_b, w_agg, preferred_element_type=jnp.float32)
        + jnp.dot(node_feats, w_self, preferred_element_type=jnp.float32)
        + bias
    )
    updated = (node_feats.astype(jnp.float32) + jax.nn.silu(preact)).astype(jnp.bfloat16)
    sigmoid_pre = jax.nn.sigmoid(preact)
    silu_slope = sigmoid_pre * (1.0 + preact * (1.0 - sigmoid_pre))
    dpre = (cotangent.astype(jnp.float32) * silu_slope).astype(jnp.bfloat16)
    contract_rows = (((0,), (0,)), ((), ()))
    local_agg = lax.dot_general(agg_b, dpre, contract_rows, preferred_element_type=jnp.float32)
    local_self = lax.dot_general(
        node_feats, dpre, contract_rows, preferred_element_type=jnp.float32
    )
    grad_sums = lax.psum((local_agg, local_self), ("blk", "rep"))
    grad_scale = 1.0 / math.sqrt(own_rows * n_blk * n_rep)
    weight_grads = jnp.stack([grad_sums[0], grad_sums[1]]) * grad_scale
    contract_cols = (((1,), (1,)), ((), ()))
    dagg = lax.dot_general(dpre, w_agg, contract_cols, preferred_element_type=jnp.float32).astype(
        jnp.bfloat16
    )
    group_rows = lax.all_gather(dagg, "rep", axis=0, tiled=True)
    row_blocks = group_rows.reshape(row_tiles, tile_size, feat_width)[row_index]
    tile_scale = live_mask / math.sqrt(feat_width)
    grads_now = jnp.einsum(
        "kid,kjd->kij", row_blocks, col_blocks, preferred_element_type=jnp.float32
    )
    tile_grads = (
        (grads_now * tile_scale[:, None, None])
        .astype(jnp.bfloat16)
        .reshape(1, 1, slots, tile_size, tile_size)
    )
    contrib = jnp.einsum("kij,kid->kjd", values, row_blocks, preferred_element_type=jnp.float32)
    col_hot = (col_index[:, None] == jnp.arange(table_tiles, dtype=jnp.int32)).astype(
        jnp.float32
    ) * live_mask[:, None]
    col_term = jnp.einsum("kc,kjd->cjd", col_hot, contrib, precision=high).reshape(
        table_tiles * tile_size, feat_width
    )
    backward = lax.psum_scatter(col_term, "blk", scatter_dimension=0, tiled=True)
    feat_grad = (
        cotangent.astype(jnp.float32)
        + lax.dot_general(dpre, w_self, contract_cols, preferred_element_type=jnp.float32)
        + backward
    )
    return (updated, feat_grad.astype(jnp.bfloat16), tile_grads, weight_grads)


def solution(mesh):
    in_specs = (
        P(("blk", "rep"), None),
        P("blk", "rep", None, None, None),
        P("blk", "rep", None),
        P("blk", "rep", None),
        P("blk", "rep"),
        P(),
        P(),
        P(),
        P(("blk", "rep"), None),
    )
    out_specs = (
        P(("blk", "rep"), None),
        P(("blk", "rep"), None),
        P("blk", "rep", None, None, None),
        P(),
    )
    return jax.shard_map(local, mesh=mesh, in_specs=in_specs, out_specs=out_specs, check_vma=False)
```

profile of v0, /device:TPU:0, one launch (start us, length us, event | category | flops | bytes accessed | tf_op | source)
XLA Modules:
  0.0 948.3 jit_solution(16624627091089157657)
XLA Ops:
  7.2 0.7 all-gather.2.cloned.1.call-update
  8.6 0.7 fusion.26
  9.3 154.0 %all-gather.2.cloned.1.call-done = bf16[16384,256]{1,0:T(8,128)(2,1)} async-done(((bf16[256,256]{1,0:T(8,128)(2,1)}), bf16[16384,256]{1,0:T(8,128)(2,1)}) %all-gather.2.cloned.1.call-update) | async-done | bytes 8388624 | tf_op jit(solution)/shard_map/all_gather | solution.py:25
  163.3 9.9 %gather_fusion = bf16[128,128,256]{2,1,0:T(8,128)(2,1)} fusion(bf16[128,128,256]{2,1,0:T(8,128)(2,1)} %bitcast.58, s32[1024]{0:T(1024)S(1)} %pad_clamp_fusion.1), kind=kCustom, calls=%fused_computation | custom fusion | bytes 16777728 | tf_op jit(solution)/shard_map/gather | solution.py:27
  173.2 12.7 %fusion.7 = f32[128,256,128]{2,1,0:T(8,128)} fusion(bf16[128,128,256]{2,1,0:T(8,128)(2,1)} %gather_fusion, bf16[1,1,128,128,128]{4,3,2,1,0:T(8,128)(2,1)} %param.10), kind=kOutput, calls=%fused_computation.10 | convolution fusion | flops 1073741824 | bytes 29360128 | tf_op jit(solution)/shard_map/kij,kjd->kid/dot_general | solution.py:28
  185.9 17.7 %copy.18 = f32[128,256,128]{1,0,2:T(8,128)} copy(f32[128,256,128]{2,1,0:T(8,128)} %fusion.7) | data formatting | bytes 33554432 | tf_op jit(solution)/shard_map/kij,kjd->kid/dot_general | solution.py:28
  203.6 10.9 %fusion.2 = f32[8,128,256]{2,0,1:T(8,128)S(1)} fusion(f32[128,256,128]{1,0,2:T(8,128)} %copy.18, f32[128]{0:T(128)S(1)} %compare_convert_fusion, s32[128]{0:T(128)S(1)} %bitcast.60), kind=kOutput, calls=%fused_computation.4 | convolution fusion | flops 402655232 | bytes 17826816 | tf_op jit(solution)/shard_map/kq,kid->qid/dot_general | solution.py:32
  214.5 1.3 copy.15
  215.9 19.9 %reduce-scatter.3.cloned.1.call-done = f32[256,256]{1,0:T(8,128)} async-done(((f32[1024,256]{1,0:T(8,128)}), f32[256,256]{1,0:T(8,128)}) %reduce-scatter.3.cloned.1.call-update) | async-done | bytes 262160 | tf_op jit(solution)/shard_map/reduce_scatter | solution.py:35
  235.8 1.1 fusion.16
  237.0 1.0 fusion.12
  238.2 0.9 convolution_bitcast_fusion
  239.1 7.2 all_gather.7
  246.4 6.5 gather_fusion.1
  252.9 12.7 %fusion.5 = f32[128,256,128]{2,1,0:T(8,128)} fusion(bf16[128,128,256]{2,1,0:T(8,128)(2,1)} %gather_fusion.1, bf16[1,1,128,128,128]{4,3,2,1,0:T(8,128)(2,1)} %param.10), kind=kOutput, calls=%fused_computation.8 | convolution fusion | flops 1073741824 | bytes 29360128 | tf_op jit(solution)/shard_map/kij,kid->kjd/dot_general | solution.py:69
  265.6 17.7 %copy.19 = f32[128,256,128]{1,0,2:T(8,128)} copy(f32[128,256,128]{2,1,0:T(8,128)} %fusion.5) | data formatting | bytes 33554432 | tf_op jit(solution)/shard_map/kij,kid->kjd/dot_general | solution.py:69
  283.3 0.9 convolution_bitcast_fusion.1
  284.3 21.9 %fusion = f32[128,128,256]{2,0,1:T(8,128)} fusion(f32[128,256,128]{1,0,2:T(8,128)} %copy.19, f32[128]{0:T(128)S(1)} %compare_convert_fusion, s32[128]{0:T(128)S(1)} %bitcast.61), kind=kOutput, calls=%fused_computation.2 | convolution fusion | flops 6442483712 | bytes 33555456 | tf_op jit(solution)/shard_map/kc,kjd->cjd/dot_general | solution.py:73
  306.2 17.7 %copy.16 = f32[128,128,256]{2,1,0:T(8,128)} copy(f32[128,128,256]{2,0,1:T(8,128)} %fusion) | data formatting | bytes 33554432 | tf_op jit(solution)/shard_map/kc,kjd->cjd/dot_general | solution.py:73
  324.0 10.2 %fusion.4 = bf16[1,1,128,128,128]{4,3,2,1,0:T(8,128)(2,1)} fusion(f32[128]{0:T(128)S(1)} %compare_select_fusion.2, bf16[128,128,256]{2,1,0:T(8,128)(2,1)} %gather_fusion.1, bf16[128,128,256]{2,1,0:T(8,128)(2,1)} %gather_fusion), kind=kOutput, calls=%fused_computation.7 | convolution fusion | flops 1077936128 | bytes 20972032 | tf_op jit(solution)/shard_map/kid,kjd->kij/dot_general | solution.py:61
  334.2 203.7 %all-reduce.3.cloned.1.call-done = (f32[1,256,256]{2,1,0:T(8,128)}, f32[1,256,256]{2,1,0:T(8,128)}) async-done(((f32[1,256,256]{2,1,0:T(8,128)}, f32[1,256,256]{2,1,0:T(8,128)}), (f32[1,256,256]{2,1,0:T(8,128)}, f32[1,256,256]{2,1,0:T(8,128)})) %all-reduce.3.cloned.1.call-update) | async-done | bytes 524304 | tf_op jit(solution)/shard_map/psum | solution.py:51
  537.8 1.9 maximum_multiply_fusion
  539.7 400.2 %reduce-scatter.5.cloned.1.call-done = f32[256,256]{1,0:T(8,128)} async-done(((f32[16384,256]{1,0:T(8,128)}), f32[256,256]{1,0:T(8,128)}) %reduce-scatter.5.cloned.1.call-update) | async-done | bytes 262160 | tf_op jit(solution)/shard_map/reduce_scatter | solution.py:76
  939.9 1.8 fusion.11
  (29 shorter events, 0.5 us)
Async XLA Ops:
  7.2 229.8 %copy-start = (bf16[256,256]{1,0:T(8,128)(2,1)S(1)}, bf16[256,256]{1,0:T(8,128)(2,1)}, u32[]{:S(2)}) copy-start(bf16[256,256]{1,0:T(8,128)(2,1)} %param.15) | copy-start | bytes 393220
  7.2 156.1 %all-gather.2.cloned.1.call-start = ((), (), s32[]{:S(2)}) async-start(), calls=%async_computation.2 | async-start | bytes 8519680 | tf_op jit(solution)/shard_map/all_gather | solution.py:25
  7.9 227.9 %reduce-scatter.3.cloned.1.call-start = ((), (), s32[]{:S(2)}) async-start(), calls=%async_computation.3 | async-start | bytes 1310720 | tf_op jit(solution)/shard_map/reduce_scatter | solution.py:35
  185.9 17.7 %copy-start.5 = (s32[1,1,128]{2,1,0:T(1,128)S(1)}, s32[1,1,128]{2,1,0:T(1,128)}, u32[]{:S(2)}) copy-start(s32[1,1,128]{2,1,0:T(1,128)} %param.11) | copy-start | bytes 1540
  203.6 32.3 %copy-start.2 = (bf16[256,256]{1,0:T(8,128)(2,1)S(1)}, bf16[256,256]{1,0:T(8,128)(2,1)}, u32[]{:S(2)}) copy-start(bf16[256,256]{1,0:T(8,128)(2,1)} %param.14) | copy-start | bytes 393220
  203.6 33.4 %copy-start.3 = (bf16[256,256]{1,0:T(8,128)(2,1)S(1)}, bf16[256,256]{1,0:T(8,128)(2,1)}, u32[]{:S(2)}) copy-start(bf16[256,256]{1,0:T(8,128)(2,1)} %param.9) | copy-start | bytes 393220
  203.6 33.4 %copy-start.4 = (bf16[256,256]{1,0:T(8,128)(2,1)S(1)}, bf16[256,256]{1,0:T(8,128)(2,1)}, u32[]{:S(2)}) copy-start(bf16[256,256]{1,0:T(8,128)(2,1)} %param.17) | copy-start | bytes 393220
  203.6 33.4 %copy-start.7 = (f32[256]{0:T(256)S(1)}, f32[256]{0:T(256)}, u32[]{:S(2)}) copy-start(f32[256]{0:T(256)} %param.16) | copy-start | bytes 3076
  215.8 322.0 %all-reduce.3.cloned.1.call-start = ((), (), s32[]{:S(2)}) async-start(), calls=%async_computation.5 | async-start | bytes 1048576 | tf_op jit(solution)/shard_map/psum | solution.py:51
  265.6 17.7 %copy-start.1 = (f32[256,256]{1,0:T(8,128)S(1)}, f32[256,256]{1,0:T(8,128)}, u32[]{:S(2)}) copy-start(f32[256,256]{1,0:T(8,128)} %reduce-scatter.3.cloned.1.call-done) | copy-start | bytes 786436
  265.6 18.7 %copy-start.6 = (s32[1,1,128]{2,1,0:T(1,128)S(1)}, s32[1,1,128]{2,1,0:T(1,128)}, u32[]{:S(2)}) copy-start(s32[1,1,128]{2,1,0:T(1,128)} %param.12) | copy-start | bytes 1540
  284.3 655.7 %reduce-scatter.5.cloned.1.call-start = ((), (), s32[]{:S(2)}) async-start(), calls=%async_computation.4 | async-start | bytes 17039360 | tf_op jit(solution)/shard_map/reduce_scatter | solution.py:76
Sparse Core Ops, SparseCore 0:
  11.5 151.7 all-gather.1
  215.9 19.8 reduce-scatter.2
  284.4 253.4 all-reduce.2
  540.4 399.4 reduce-scatter.4
where the time goes:
time: 949 us; the launch traced here: 948 us
  waiting for transfers between devices  779 us (82%)
  matrix products  74.4 us (8%)
  local copies, waits for them, and re-layouts  70.9 us (7%)
  between operations  14.5 us (2%)
    reduce_scatter x1, waiting for transfers between devices, local(): lax.psum_scatter(col_term, 'blk', scatter_dimension=0, tiled=True)  400 us
    psum x1, waiting for transfers between devices, local(): grad_sums = lax.psum((local_agg, local_self), ('blk', 'rep'))  204 us
    all_gather x1, waiting for transfers between devices, local(): gathered = lax.all_gather(node_feats, 'blk', axis=0, tiled=True)  154 us
    dot_general x1, matrix products, local(): jnp.einsum('kc,kjd->cjd', col_hot, contrib, precision=high)  21.9 us
    reduce_scatter x1, waiting for transfers between devices, local(): lax.psum_scatter(partial_sum, 'rep', scatter_dimension=0, tiled=True)  19.9 us
  transfers between devices with their start and end apart: 4, of which 4 were waited for; matrix products, arithmetic and copies ran while one was open for 6% of the time, Pallas kernels for 0%

commit v1 on v0

v1 whole, which is shorter than its diff:
```python
import math

import jax
import jax.numpy as jnp
from jax import lax
from jax.experimental import pallas as pl
from jax.experimental.pallas import tpu as pltpu
from jax.sharding import PartitionSpec as P

DISTANCES = (0, 1, 2, 4, 8, 16, 32, 48, 56, 60, 62, 63)
VMEM = pl.BlockSpec(memory_space=pltpu.VMEM)
SMEM = pl.BlockSpec(memory_space=pltpu.SMEM)
ANY = pl.BlockSpec(memory_space=pl.ANY)
LIMIT = 40 * 1024 * 1024


def params():
    return pltpu.CompilerParams(vmem_limit_bytes=LIMIT)


def dot_nt(a, b):
    return lax.dot_general(a, b, (((1,), (1,)), ((), ())), preferred_element_type=jnp.float32)


def dot_tn(a, b):
    return lax.dot_general(a, b, (((0,), (0,)), ((), ())), preferred_element_type=jnp.float32)


def build_kernel(row_ref, loc_ref, count_ref, vals_ref, dense_ref, acc_ref):
    col_tiles = dense_ref.shape[1] // 128
    row_tiles = dense_ref.shape[0] // 128

    def clear(i, c):
        acc_ref[i] = jnp.zeros((128, 128), jnp.float32)
        return c

    lax.fori_loop(0, row_tiles * col_tiles, clear, 0)

    def add(k, c):
        at = row_ref[k] * col_tiles + loc_ref[k]
        acc_ref[at] = acc_ref[at] + vals_ref[k].astype(jnp.float32)
        return c

    lax.fori_loop(0, count_ref[0], add, 0)

    def cast(q, c):
        rows = pl.ds(pl.multiple_of(q * 128, 128), 128)
        for t in range(col_tiles):
            dense_ref[rows, t * 128 : (t + 1) * 128] = acc_ref[q * col_tiles + t].astype(jnp.bfloat16)
        return c

    lax.fori_loop(0, row_tiles, cast, 0)


def load_blocks(rep, dense_ref, buf, sems):
    copies = []
    for k in range(4):
        rows = pl.ds(pl.multiple_of((rep ^ k) * 256, 256), 256)
        copies.append(pltpu.make_async_copy(dense_ref.at[rows], buf.at[k], sems.at[k]))
    for copy in copies:
        copy.start()
    return copies


def forward_kernel(rep_ref, dense_ref, *refs):
    feats, outs, (buf, sems) = refs[:12], refs[12:16], refs[16:]
    copies = load_blocks(rep_ref[0], dense_ref, buf, sems)
    for k in (3, 2, 1, 0):
        copies[k].wait()
        total = jnp.zeros((256, 256), jnp.float32)
        for o in range(12):
            total = total + jnp.dot(
                buf[k, :, o * 256 : (o + 1) * 256], feats[o][...], preferred_element_type=jnp.float32
            )
        outs[k][...] = total.astype(outs[k].dtype)


def update_kernel(p0, p1, p2, p3, x_ref, cot_ref, wa_ref, ws_ref, b_ref, upd_ref, dagg_ref, base_ref, grads_ref):
    agg = p0[...] + p1[...].astype(jnp.float32) + p2[...].astype(jnp.float32) + p3[...].astype(jnp.float32)
    agg_b = agg.astype(jnp.bfloat16)
    x = x_ref[...]
    pre = (
        jnp.dot(agg_b, wa_ref[...], preferred_element_type=jnp.float32)
        + jnp.dot(x, ws_ref[...], preferred_element_type=jnp.float32)
        + b_ref[...]
    )
    s = 1.0 / (1.0 + jnp.exp(-pre))
    upd_ref[...] = (x.astype(jnp.float32) + pre * s).astype(jnp.bfloat16)
    cot = cot_ref[...].astype(jnp.float32)
    dpre = (cot * (s * (1.0 + pre * (1.0 - s)))).astype(jnp.bfloat16)
    dagg_ref[...] = dot_nt(dpre, wa_ref[...]).astype(jnp.bfloat16)
    base_ref[...] = cot + dot_nt(dpre, ws_ref[...])
    scale = 1.0 / 256.0
    for i, a in enumerate((agg_b, x)):
        total = dot_tn(a, dpre) * scale
        grads_ref[2 * i] = total[:, :128]
        grads_ref[2 * i + 1] = total[:, 128:]


def scatter_kernel(rep_ref, dense_ref, d0, d1, d2, d3, *refs):
    outs, (buf, sems) = refs[:12], refs[12:]
    copies = load_blocks(rep_ref[0], dense_ref, buf, sems)
    turned = [d[...].T for d in (d0, d1, d2, d3)]
    for copy in copies:
        copy.wait()
    for o in range(12):
        total = jnp.zeros((256, 256), jnp.float32)
        for k in range(4):
            total = total + jnp.dot(
                turned[k], buf[k, :, o * 256 : (o + 1) * 256], preferred_element_type=jnp.float32
            )
        outs[o][...] = total.astype(outs[o].dtype)


def tile_grads_kernel(rep_ref, row_ref, loc_ref, count_ref, d0, d1, d2, d3, *refs):
    feats, out_ref, (grid_ref, zero_ref, sem) = refs[:12], refs[12], refs[13:]
    daggs = (d0, d1, d2, d3)
    rep = rep_ref[0]
    zero_ref[...] = jnp.zeros_like(zero_ref)
    slots = out_ref.shape[0]
    for k in range(4):
        first = (rep ^ k) * 2
        for o in range(12):
            block = (dot_nt(daggs[k][...], feats[o][...]) * (1.0 / 16.0)).astype(jnp.bfloat16)
            for a in range(2):
                for b in range(2):
                    grid_ref[(first + a) * 24 + 2 * o + b] = block[
                        a * 128 : (a + 1) * 128, b * 128 : (b + 1) * 128
                    ]

    def send(k, c):
        pltpu.make_async_copy(grid_ref.at[row_ref[k] * 24 + loc_ref[k]], out_ref.at[k], sem).start()
        return c

    def blank(k, c):
        pltpu.make_async_copy(zero_ref, out_ref.at[k], sem).start()
        return c

    lax.fori_loop(0, count_ref[0], send, 0)
    lax.fori_loop(count_ref[0], slots, blank, 0)

    def wait(k, c):
        pltpu.make_async_copy(zero_ref, out_ref.at[k], sem).wait()
        return c

    lax.fori_loop(0, slots, wait, 0)


def finish_kernel(base_ref, own_ref, *refs):
    terms, out_ref = refs[:-1], refs[-1]
    total = own_ref[...]
    for t in terms:
        total = total + t[...].astype(jnp.float32)
    out_ref[...] = (base_ref[...] + total.T).astype(jnp.bfloat16)


def local(node_feats, tile_vals, tile_row, tile_col, tile_count, w_agg, w_self, bias, cotangent):
    n_blk = lax.axis_size("blk")
    group = lax.axis_index("blk")
    rep = lax.axis_index("rep").reshape(1).astype(jnp.int32)
    row = tile_row[0, 0]
    count = tile_count[0]
    away = (lax.div(tile_col[0, 0], 2) - group + n_blk) & (n_blk - 1)
    loc = lax.rem(tile_col[0, 0], 2)
    for d in DISTANCES[1:]:
        loc = loc + 2 * (away >= d).astype(jnp.int32)
    loc = loc.astype(jnp.int32)

    def shape(s, t=jnp.bfloat16):
        return jax.ShapeDtypeStruct(s, t)

    def from_blk(x, d):
        return lax.ppermute(x, "blk", [(i, (i - d) % n_blk) for i in range(n_blk)])

    def to_rep(x, k):
        return lax.ppermute(x, "rep", [(i, i ^ k) for i in range(4)])

    feats = [node_feats] + [from_blk(node_feats, d) for d in DISTANCES[1:]]
    dense = pl.pallas_call(
        build_kernel,
        out_shape=shape((1024, 3072)),
        in_specs=[SMEM, SMEM, SMEM, VMEM],
        out_specs=VMEM,
        scratch_shapes=[pltpu.VMEM((192, 128, 128), jnp.float32)],
        compiler_params=params(),
        cost_estimate=pl.CostEstimate(flops=0, bytes_accessed=10 << 20, transcendentals=0),
        name="build",
    )(row, loc, count, tile_vals[0, 0])

    block = (256, 256)
    blocks = [pltpu.VMEM((4, 256, 3072), jnp.bfloat16), pltpu.SemaphoreType.DMA((4,))]
    parts = pl.pallas_call(
        forward_kernel,
        out_shape=[shape(block, jnp.float32)] + [shape(block)] * 3,
        in_specs=[SMEM, ANY] + [VMEM] * 12,
        out_specs=[VMEM] * 4,
        scratch_shapes=blocks,
        compiler_params=params(),
        cost_estimate=pl.CostEstimate(flops=2 * 1024 * 3072 * 256, bytes_accessed=8 << 20, transcendentals=0),
        name="forward",
    )(rep, dense, *feats)
    swapped = [parts[0]] + [to_rep(parts[k], k) for k in (1, 2, 3)]

    updated, dagg, base, grads = pl.pallas_call(
        update_kernel,
        out_shape=[shape(block), shape(block), shape(block, jnp.float32), shape((4, 256, 128), jnp.float32)],
        in_specs=[VMEM] * 9,
        out_specs=[VMEM] * 4,
        compiler_params=params(),
        cost_estimate=pl.CostEstimate(flops=12 * 256**3, bytes_accessed=2 << 20, transcendentals=65536),
        name="update",
    )(*swapped, node_feats, cotangent, w_agg, w_self, bias.reshape(1, 256))

    daggs = [dagg] + [to_rep(dagg, k) for k in (1, 2, 3)]
    terms = pl.pallas_call(
        scatter_kernel,
        out_shape=[shape(block, jnp.float32)] + [shape(block)] * 11,
        in_specs=[SMEM, ANY] + [VMEM] * 4,
        out_specs=[VMEM] * 12,
        scratch_shapes=blocks,
        compiler_params=params(),
        cost_estimate=pl.CostEstimate(flops=2 * 1024 * 3072 * 256, bytes_accessed=8 << 20, transcendentals=0),
        name="scatter",
    )(rep, dense, *daggs)
    arrived = [from_blk(t, -d) for t, d in zip(terms[1:], DISTANCES[1:])]

    tile_grads = pl.pallas_call(
        tile_grads_kernel,
        out_shape=shape((128, 128, 128)),
        in_specs=[SMEM] * 4 + [VMEM] * 16,
        out_specs=ANY,
        scratch_shapes=[
            pltpu.VMEM((192, 128, 128), jnp.bfloat16),
            pltpu.VMEM((128, 128), jnp.bfloat16),
            pltpu.SemaphoreType.DMA,
        ],
        compiler_params=params(),
        cost_estimate=pl.CostEstimate(flops=2 * 1024 * 3072 * 256, bytes_accessed=8 << 20, transcendentals=0),
        name="tile_grads",
    )(rep, row, loc, count, *daggs, *feats)

    feat_grad = pl.pallas_call(
        finish_kernel,
        out_shape=shape(block),
        in_specs=[VMEM] * 13,
        out_specs=VMEM,
        compiler_params=params(),
        cost_estimate=pl.CostEstimate(flops=0, bytes_accessed=2 << 20, transcendentals=0),
        name="finish",
    )(base, *terms[:1], *arrived)

    quarter = jnp.sum(lax.all_to_all(grads, "rep", 0, 0, tiled=True), axis=0)
    piece = jnp.sum(lax.all_to_all(quarter.reshape(n_blk, 4, 128), "blk", 0, 0, tiled=True), axis=0)
    whole = lax.all_to_all(jnp.broadcast_to(piece[None], (n_blk, 4, 128)), "blk", 0, 0, tiled=True)
    quarters = lax.all_to_all(jnp.broadcast_to(whole.reshape(1, 256, 128), (4, 256, 128)), "rep", 0, 0, tiled=True)
    weight_grads = jnp.stack(
        [jnp.concatenate([quarters[2 * i], quarters[2 * i + 1]], axis=1) for i in range(2)]
    )
    return updated, feat_grad, tile_grads.reshape(1, 1, 128, 128, 128), weight_grads


def solution(mesh):
    in_specs = (
        P(("blk", "rep"), None),
        P("blk", "rep", None, None, None),
        P("blk", "rep", None),
        P("blk", "rep", None),
        P("blk", "rep"),
        P(),
        P(),
        P(),
        P(("blk", "rep"), None),
    )
    out_specs = (
        P(("blk", "rep"), None),
        P(("blk", "rep"), None),
        P("blk", "rep", None, None, None),
        P(),
    )
    return jax.shard_map(local, mesh=mesh, in_specs=in_specs, out_specs=out_specs, check_vma=False)
```

time: 949 us -> 156 us (0.16)
  the two profiles are of different devices: /device:TPU:0 before, /device:TPU:60 now
where the time goes in v1:
time: 156 us
  starting transfers between devices  68.8 us (44%)
  waiting for transfers between devices  42.7 us (27%)
  Pallas kernels  16.7 us (11%)
  local copies, waits for them, and re-layouts  11.8 us (8%)
  blocking collectives  11.6 us (7%)
  other arithmetic  2.3 us (1%)
  between operations  1.56 us (1%)
    ppermute x22, starting transfers between devices, from_blk(): return lax.ppermute(x, 'blk', [(i, (i - d) % n_blk) for i in range(n_blk)])  38.3 us
    ppermute x22, waiting for transfers between devices, from_blk(): return lax.ppermute(x, 'blk', [(i, (i - d) % n_blk) for i in range(n_blk)])  30.5 us
    all_to_all x1, starting transfers between devices, local(): lax.all_to_all(quarter.reshape(n_blk, 4, 128), 'blk', 0, 0, tiled=True)  12.2 us
    all_to_all x1, blocking collectives, local(): quarter = jnp.sum(lax.all_to_all(grads, 'rep', 0, 0, tiled=True), axis=0)  11.6 us
    all_to_all x1, starting transfers between devices, local(): lax.all_to_all(jnp.broadcast_to(piece[None], (n_blk, 4, 128)), 'blk', 0,...  10.3 us
    unnamed x28, local copies, waits for them, and re-layouts  8.24 us
    ppermute x6, waiting for transfers between devices, to_rep(): return lax.ppermute(x, 'rep', [(i, i ^ k) for i in range(4)])  6.41 us
    all_to_all x1, waiting for transfers between devices, local(): lax.all_to_all(quarter.reshape(n_blk, 4, 128), 'blk', 0, 0, tiled=True)  5.81 us
  transfers between devices with their start and end apart: 31, of which 10 were waited for; matrix products, arithmetic and copies ran while one was open for 2% of the time, Pallas kernels for 7%

profile of v1, /device:TPU:60, one launch (start us, length us, event | category | flops | bytes accessed | tf_op | source)
XLA Modules:
  0.0 155.5 jit_solution(11856179277022925647)
XLA Ops:
  2.2 2.6 %collective-permute-start.9 = (bf16[256,256]{1,0:T(8,128)(2,1)}, bf16[256,256]{1,0:T(8,128)(2,1)S(1)}, u32[]{:S(2)}, u32[]{:S(2)}) collective-permute-start(bf16[256,256]{1,0:T(8,128)(2,1)} %refs_0_.3), channel_id=1, source_target_pairs={{0,8},{4,12},{8,16},{12,20},{16,24},{20,28},{24,32},{28,36},{32,40... | collective-permute-start | bytes 393224 | tf_op jit(solution)/shard_map/ppermute | solution.py:173
  4.8 3.0 %collective-permute-start.8 = (bf16[256,256]{1,0:T(8,128)(2,1)}, bf16[256,256]{1,0:T(8,128)(2,1)S(1)}, u32[]{:S(2)}, u32[]{:S(2)}) collective-permute-start(bf16[256,256]{1,0:T(8,128)(2,1)} %refs_0_.3), channel_id=1, source_target_pairs={{0,16},{4,20},{8,24},{12,28},{16,32},{20,36},{24,40},{28,44},{32,4... | collective-permute-start | bytes 393224 | tf_op jit(solution)/shard_map/ppermute | solution.py:173
  9.8 3.6 %collective-permute-start.6 = (bf16[256,256]{1,0:T(8,128)(2,1)}, bf16[256,256]{1,0:T(8,128)(2,1)S(1)}, u32[]{:S(2)}, u32[]{:S(2)}) collective-permute-start(bf16[256,256]{1,0:T(8,128)(2,1)} %refs_0_.3), channel_id=1, source_target_pairs={{0,64},{4,68},{8,72},{12,76},{16,80},{20,84},{24,88},{28,92},{32,9... | collective-permute-start | bytes 393224 | tf_op jit(solution)/shard_map/ppermute | solution.py:173
  14.9 4.2 %collective-permute-start.4 = (bf16[256,256]{1,0:T(8,128)(2,1)}, bf16[256,256]{1,0:T(8,128)(2,1)S(1)}, u32[]{:S(2)}, u32[]{:S(2)}) collective-permute-start(bf16[256,256]{1,0:T(8,128)(2,1)} %refs_0_.3), channel_id=1, source_target_pairs={{0,192},{4,196},{8,200},{12,204},{16,208},{20,212},{24,216},{28,22... | collective-permute-start | bytes 393224 | tf_op jit(solution)/shard_map/ppermute | solution.py:173
  20.7 7.1 %collective-permute-done.6.refs_7_ = bf16[256,256]{1,0:T(8,128)(2,1)S(1)} collective-permute-done((bf16[256,256]{1,0:T(8,128)(2,1)}, bf16[256,256]{1,0:T(8,128)(2,1)S(1)}, u32[]{:S(2)}, u32[]{:S(2)}) %collective-permute-start.6) | collective-permute-done | bytes 131104 | tf_op jit(solution)/shard_map/ppermute | solution.py:173
  31.9 3.3 %build.1.dense_ref = bf16[1024,3072]{1,0:T(8,128)(2,1)S(1)} custom-call(s32[128]{0:T(128)S(1)} %bitcast.33, s32[128]{0:T(128)S(1)} %fusion.10.loc_ref, s32[1]{0:T(128)} %bitcast.30.count_ref, bf16[128,128,128]{2,1,0:T(8,128)(2,1)S(1)} %bitcast.32), custom_call_target="tpu_custom_call" | custom-call | bytes 10485760 | tf_op jit(solution)/shard_map/build/pallas_call | solution.py:179
  35.3 2.8 %collective-permute-done.1.refs_2_ = bf16[256,256]{1,0:T(8,128)(2,1)S(1)} collective-permute-done((bf16[256,256]{1,0:T(8,128)(2,1)}, bf16[256,256]{1,0:T(8,128)(2,1)S(1)}, u32[]{:S(2)}, u32[]{:S(2)}) %collective-permute-start.1) | collective-permute-done | bytes 131104 | tf_op jit(solution)/shard_map/ppermute | solution.py:173
  38.1 2.5 %collective-permute-done.refs_1_ = bf16[256,256]{1,0:T(8,128)(2,1)S(1)} collective-permute-done((bf16[256,256]{1,0:T(8,128)(2,1)}, bf16[256,256]{1,0:T(8,128)(2,1)S(1)}, u32[]{:S(2)}, u32[]{:S(2)}) %collective-permute-start) | collective-permute-done | bytes 131104 | tf_op jit(solution)/shard_map/ppermute | solution.py:173
  40.6 4.3 %forward.1 = (f32[256,256]{1,0:T(8,128)S(1)}, bf16[256,256]{1,0:T(8,128)(2,1)S(1)}, bf16[256,256]{1,0:T(8,128)(2,1)S(1)}, bf16[256,256]{1,0:T(8,128)(2,1)S(1)}) custom-call(s32[1]{0:T(128)} %bitcast.rep_ref, bf16[1024,3072]{1,0:T(8,128)(2,1)S(1)} %build.1.dense_ref, bf16[256,256]{1,0:T(8,128)(2,1)S(1)} %copy-done.3, ...), custom_call_target="tpu_custom_call" | custom-call | flops 1610612736 | bytes 8388608 | tf_op jit(solution)/shard_map/forward/pallas_call | solution.py:192
  46.9 4.4 %collective-permute-done.12.p2 = bf16[256,256]{1,0:T(8,128)(2,1)S(1)} collective-permute-done((bf16[256,256]{1,0:T(8,128)(2,1)S(1)}, bf16[256,256]{1,0:T(8,128)(2,1)S(1)}, u32[]{:S(2)}, u32[]{:S(2)}) %collective-permute-start.12) | collective-permute-done | bytes 131104 | tf_op jit(solution)/shard_map/ppermute | solution.py:176
  54.4 11.6 %all_to_all.20 = f32[4,256,128]{2,1,0:T(8,128)S(1)} all-to-all(f32[4,256,128]{2,1,0:T(8,128)S(1)} %get-tuple-element.43), channel_id=1, replica_groups=mesh['blk'=64,'rep'=4] {'rep'}, dimensions={0} | all-to-all | bytes 1048576 | tf_op jit(solution)/shard_map/all_to_all | solution.py:252
  66.7 12.2 %all-to-all-start.1 = ((f32[64,4,128]{2,1,0:T(4,128)}), f32[64,4,128]{2,1,0:T(4,128)S(1)}, u32[]{:S(2)}, u32[]{:S(2)}) async-start(f32[64,4,128]{2,1,0:T(4,128)} %bitcast.7), calls=%async_computation.1 | async-start | bytes 262144 | tf_op jit(solution)/shard_map/all_to_all | solution.py:253
  80.8 5.8 %all-to-all-done.1 = f32[64,4,128]{2,1,0:T(4,128)S(1)} async-done(((f32[64,4,128]{2,1,0:T(4,128)}), f32[64,4,128]{2,1,0:T(4,128)S(1)}, u32[]{:S(2)}, u32[]{:S(2)}) %all-to-all-start.1) | async-done | bytes 131104 | tf_op jit(solution)/shard_map/all_to_all | solution.py:253
  87.4 10.3 %all-to-all-start.2 = ((f32[64,4,128]{2,1,0:T(4,128)}), f32[64,4,128]{2,1,0:T(4,128)}, u32[]{:S(2)}, u32[]{:S(2)}) async-start(f32[64,4,128]{2,1,0:T(4,128)} %broadcast_in_dim.6), calls=%async_computation.2 | async-start | bytes 262144 | tf_op jit(solution)/shard_map/all_to_all | solution.py:254
  97.7 2.8 %copy-done.1 = bf16[1024,3072]{1,0:T(8,128)(2,1)S(1)} copy-done((bf16[1024,3072]{1,0:T(8,128)(2,1)S(1)}, bf16[1024,3072]{1,0:T(8,128)(2,1)}, u32[]{:S(2)}) %copy-start.1) | copy-done | bytes 6291480
  100.5 2.8 %scatter.1 = (f32[256,256]{1,0:T(8,128)S(1)}, bf16[256,256]{1,0:T(8,128)(2,1)}, bf16[256,256]{1,0:T(8,128)(2,1)S(1)}, bf16[256,256]{1,0:T(8,128)(2,1)S(1)}, bf16...) custom-call(s32[1]{0:T(128)} %bitcast.rep_ref, ...), custom_call_target="tpu_custom_call" | custom-call | flops 1610612736 | bytes 8388608 | tf_op jit(solution)/shard_map/scatter/pallas_call | solution.py:215
  109.1 4.1 %all-to-all-start.3 = ((f32[4,256,128]{2,1,0:T(8,128)}), f32[4,256,128]{2,1,0:T(8,128)}, u32[]{:S(2)}, u32[]{:S(2)}) async-start(f32[4,256,128]{2,1,0:T(8,128)} %broadcast_in_dim.15), calls=%async_computation.3 | async-start | bytes 1048576 | tf_op jit(solution)/shard_map/all_to_all | solution.py:255
  113.3 2.7 %collective-permute-start.18 = (bf16[256,256]{1,0:T(8,128)(2,1)}, bf16[256,256]{1,0:T(8,128)(2,1)S(1)}, u32[]{:S(2)}, u32[]{:S(2)}) collective-permute-start(bf16[256,256]{1,0:T(8,128)(2,1)} %copy-done.13), channel_id=1, source_target_pairs={{0,8},{4,12},{8,16},{12,20},{16,24},{20,28},{24,32},{28,36},{32,40... | collective-permute-start | bytes 393224 | tf_op jit(solution)/shard_map/ppermute | solution.py:173
  116.0 2.7 %collective-permute-start.19 = (bf16[256,256]{1,0:T(8,128)(2,1)}, bf16[256,256]{1,0:T(8,128)(2,1)S(1)}, u32[]{:S(2)}, u32[]{:S(2)}) collective-permute-start(bf16[256,256]{1,0:T(8,128)(2,1)} %copy-done.12), channel_id=1, source_target_pairs={{0,16},{4,20},{8,24},{12,28},{16,32},{20,36},{24,40},{28,44},{32,4... | collective-permute-start | bytes 393224 | tf_op jit(solution)/shard_map/ppermute | solution.py:173
  120.3 2.8 %collective-permute-start.21 = (bf16[256,256]{1,0:T(8,128)(2,1)}, bf16[256,256]{1,0:T(8,128)(2,1)S(1)}, u32[]{:S(2)}, u32[]{:S(2)}) collective-permute-start(bf16[256,256]{1,0:T(8,128)(2,1)} %copy-done.10), channel_id=1, source_target_pairs={{0,64},{4,68},{8,72},{12,76},{16,80},{20,84},{24,88},{28,92},{32,9... | collective-permute-start | bytes 393224 | tf_op jit(solution)/shard_map/ppermute | solution.py:173
  124.3 3.0 %collective-permute-start.23 = (bf16[256,256]{1,0:T(8,128)(2,1)S(1)}, bf16[256,256]{1,0:T(8,128)(2,1)S(1)}, u32[]{:S(2)}, u32[]{:S(2)}) collective-permute-start(bf16[256,256]{1,0:T(8,128)(2,1)S(1)} %get-tuple-element.38), channel_id=1, source_target_pairs={{0,192},{4,196},{8,200},{12,204},{16,208},{20,212},{24,216},{28,22... | collective-permute-start | bytes 393224 | tf_op jit(solution)/shard_map/ppermute | solution.py:173
  129.9 10.0 %collective-permute-done.21.refs_4_ = bf16[256,256]{1,0:T(8,128)(2,1)S(1)} collective-permute-done((bf16[256,256]{1,0:T(8,128)(2,1)}, bf16[256,256]{1,0:T(8,128)(2,1)S(1)}, u32[]{:S(2)}, u32[]{:S(2)}) %collective-permute-start.21) | collective-permute-done | bytes 131104 | tf_op jit(solution)/shard_map/ppermute | solution.py:173
  140.9 4.3 %tile_grads.1 = bf16[128,128,128]{2,1,0:T(8,128)(2,1)} custom-call(s32[1]{0:T(128)} %bitcast.rep_ref, s32[128]{0:T(128)S(1)} %bitcast.34, s32[128]{0:T(128)S(1)} %fusion.10.loc_ref, s32[1]{0:T(128)} %bitcast.31.count_ref, bf16[256,256]{1,0:T(8,128)(2,1)S(1)} %get-tuple-element.30.d0, bf16[256,256]{1,0:T(8,128)(2,1)S(1)} %collective-permute-done.14.d1, ...), custom_call_target="tpu_custom_call" | custom-call | flops 1610612736 | bytes 8388608 | tf_op jit(solution)/shard_map/tile_grads/pallas_call | solution.py:227
  145.3 5.1 %collective-permute-done.26.refs_9_ = bf16[256,256]{1,0:T(8,128)(2,1)S(1)} collective-permute-done((bf16[256,256]{1,0:T(8,128)(2,1)S(1)}, bf16[256,256]{1,0:T(8,128)(2,1)S(1)}, u32[]{:S(2)}, u32[]{:S(2)}) %collective-permute-start.26) | collective-permute-done | bytes 131104 | tf_op jit(solution)/shard_map/ppermute | solution.py:173
  (81 shorter events, 35.9 us)
Async XLA Ops:
  0.6 12.7 %collective-permute-start.10 = (bf16[256,256]{1,0:T(8,128)(2,1)}, bf16[256,256]{1,0:T(8,128)(2,1)S(1)}, u32[]{:S(2)}, u32[]{:S(2)}) collective-permute-start(bf16[256,256]{1,0:T(8,128)(2,1)} %refs_0_.3), channel_id=1, source_target_pairs={{0,4},{4,8},{8,12},{12,16},{16,20},{20,24},{24,28},{28,32},{32,36}... | collective-permute-start | bytes 393224 | tf_op jit(solution)/shard_map/ppermute | solution.py:173
  2.2 12.7 %collective-permute-start.9 = (bf16[256,256]{1,0:T(8,128)(2,1)}, bf16[256,256]{1,0:T(8,128)(2,1)S(1)}, u32[]{:S(2)}, u32[]{:S(2)}) collective-permute-start(bf16[256,256]{1,0:T(8,128)(2,1)} %refs_0_.3), channel_id=1, source_target_pairs={{0,8},{4,12},{8,16},{12,20},{16,24},{20,28},{24,32},{28,36},{32,40... | collective-permute-start | bytes 393224 | tf_op jit(solution)/shard_map/ppermute | solution.py:173
  4.8 14.3 %collective-permute-start.8 = (bf16[256,256]{1,0:T(8,128)(2,1)}, bf16[256,256]{1,0:T(8,128)(2,1)S(1)}, u32[]{:S(2)}, u32[]{:S(2)}) collective-permute-start(bf16[256,256]{1,0:T(8,128)(2,1)} %refs_0_.3), channel_id=1, source_target_pairs={{0,16},{4,20},{8,24},{12,28},{16,32},{20,36},{24,40},{28,44},{32,4... | collective-permute-start | bytes 393224 | tf_op jit(solution)/shard_map/ppermute | solution.py:173
  7.8 12.3 %collective-permute-start.7 = (bf16[256,256]{1,0:T(8,128)(2,1)}, bf16[256,256]{1,0:T(8,128)(2,1)S(1)}, u32[]{:S(2)}, u32[]{:S(2)}) collective-permute-start(bf16[256,256]{1,0:T(8,128)(2,1)} %refs_0_.3), channel_id=1, source_target_pairs={{0,32},{4,36},{8,40},{12,44},{16,48},{20,52},{24,56},{28,60},{32,6... | collective-permute-start | bytes 393224 | tf_op jit(solution)/shard_map/ppermute | solution.py:173
  9.8 18.0 %collective-permute-start.6 = (bf16[256,256]{1,0:T(8,128)(2,1)}, bf16[256,256]{1,0:T(8,128)(2,1)S(1)}, u32[]{:S(2)}, u32[]{:S(2)}) collective-permute-start(bf16[256,256]{1,0:T(8,128)(2,1)} %refs_0_.3), channel_id=1, source_target_pairs={{0,64},{4,68},{8,72},{12,76},{16,80},{20,84},{24,88},{28,92},{32,9... | collective-permute-start | bytes 393224 | tf_op jit(solution)/shard_map/ppermute | solution.py:173
  13.3 14.4 %collective-permute-start.5 = (bf16[256,256]{1,0:T(8,128)(2,1)}, bf16[256,256]{1,0:T(8,128)(2,1)S(1)}, u32[]{:S(2)}, u32[]{:S(2)}) collective-permute-start(bf16[256,256]{1,0:T(8,128)(2,1)} %refs_0_.3), channel_id=1, source_target_pairs={{0,128},{4,132},{8,136},{12,140},{16,144},{20,148},{24,152},{28,15... | collective-permute-start | bytes 393224 | tf_op jit(solution)/shard_map/ppermute | solution.py:173
  14.9 20.3 %collective-permute-start.4 = (bf16[256,256]{1,0:T(8,128)(2,1)}, bf16[256,256]{1,0:T(8,128)(2,1)S(1)}, u32[]{:S(2)}, u32[]{:S(2)}) collective-permute-start(bf16[256,256]{1,0:T(8,128)(2,1)} %refs_0_.3), channel_id=1, source_target_pairs={{0,192},{4,196},{8,200},{12,204},{16,208},{20,212},{24,216},{28,22... | collective-permute-start | bytes 393224 | tf_op jit(solution)/shard_map/ppermute | solution.py:173
  19.1 16.1 %collective-permute-start.3 = (bf16[256,256]{1,0:T(8,128)(2,1)}, bf16[256,256]{1,0:T(8,128)(2,1)S(1)}, u32[]{:S(2)}, u32[]{:S(2)}) collective-permute-start(bf16[256,256]{1,0:T(8,128)(2,1)} %refs_0_.3), channel_id=1, source_target_pairs={{0,224},{4,228},{8,232},{12,236},{16,240},{20,244},{24,248},{28,25... | collective-permute-start | bytes 393224 | tf_op jit(solution)/shard_map/ppermute | solution.py:173
  20.1 15.1 %collective-permute-start.2 = (bf16[256,256]{1,0:T(8,128)(2,1)}, bf16[256,256]{1,0:T(8,128)(2,1)S(1)}, u32[]{:S(2)}, u32[]{:S(2)}) collective-permute-start(bf16[256,256]{1,0:T(8,128)(2,1)} %refs_0_.3), channel_id=1, source_target_pairs={{0,240},{4,244},{8,248},{12,252},{16,0},{20,4},{24,8},{28,12},{32,... | collective-permute-start | bytes 393224 | tf_op jit(solution)/shard_map/ppermute | solution.py:173
  27.8 12.8 %collective-permute-start = (bf16[256,256]{1,0:T(8,128)(2,1)}, bf16[256,256]{1,0:T(8,128)(2,1)S(1)}, u32[]{:S(2)}, u32[]{:S(2)}) collective-permute-start(bf16[256,256]{1,0:T(8,128)(2,1)} %refs_0_.3), channel_id=1, source_target_pairs={{0,252},{4,0},{8,4},{12,8},{16,12},{20,16},{24,20},{28,24},{32,28}... | collective-permute-start | bytes 393224 | tf_op jit(solution)/shard_map/ppermute | solution.py:173
  66.7 19.9 %all-to-all-start.1 = ((f32[64,4,128]{2,1,0:T(4,128)}), f32[64,4,128]{2,1,0:T(4,128)S(1)}, u32[]{:S(2)}, u32[]{:S(2)}) async-start(f32[64,4,128]{2,1,0:T(4,128)} %bitcast.7), calls=%async_computation.1 | async-start | bytes 262144 | tf_op jit(solution)/shard_map/all_to_all | solution.py:253
  78.9 18.8 %collective-permute-start.16 = (bf16[256,256]{1,0:T(8,128)(2,1)S(1)}, bf16[256,256]{1,0:T(8,128)(2,1)S(1)}, u32[]{:S(2)}, u32[]{:S(2)}) collective-permute-start(bf16[256,256]{1,0:T(8,128)(2,1)S(1)} %get-tuple-element.30.d0), channel_id=1, source_target_pairs={{0,3},{1,2},{2,1},{3,0},{4,7},{5,6},{6,5},{7,4},{8,11},{9,10},{10,... | collective-permute-start | bytes 393224 | tf_op jit(solution)/shard_map/ppermute | solution.py:176
  79.0 18.7 %collective-permute-start.15 = (bf16[256,256]{1,0:T(8,128)(2,1)S(1)}, bf16[256,256]{1,0:T(8,128)(2,1)S(1)}, u32[]{:S(2)}, u32[]{:S(2)}) collective-permute-start(bf16[256,256]{1,0:T(8,128)(2,1)S(1)} %get-tuple-element.30.d0), channel_id=1, source_target_pairs={{0,2},{1,3},{2,0},{3,1},{4,6},{5,7},{6,4},{7,5},{8,10},{9,11},{10,... | collective-permute-start | bytes 393224 | tf_op jit(solution)/shard_map/ppermute | solution.py:176
  79.5 18.2 %collective-permute-start.14 = (bf16[256,256]{1,0:T(8,128)(2,1)S(1)}, bf16[256,256]{1,0:T(8,128)(2,1)S(1)}, u32[]{:S(2)}, u32[]{:S(2)}) collective-permute-start(bf16[256,256]{1,0:T(8,128)(2,1)S(1)} %get-tuple-element.30.d0), channel_id=1, source_target_pairs={{0,1},{1,0},{2,3},{3,2},{4,5},{5,4},{6,7},{7,6},{8,9},{9,8},{10,11... | collective-permute-start | bytes 393224 | tf_op jit(solution)/shard_map/ppermute | solution.py:176
  87.4 20.0 %all-to-all-start.2 = ((f32[64,4,128]{2,1,0:T(4,128)}), f32[64,4,128]{2,1,0:T(4,128)}, u32[]{:S(2)}, u32[]{:S(2)}) async-start(f32[64,4,128]{2,1,0:T(4,128)} %broadcast_in_dim.6), calls=%async_computation.2 | async-start | bytes 262144 | tf_op jit(solution)/shard_map/all_to_all | solution.py:254
  105.9 17.1 %collective-permute-start.17 = (bf16[256,256]{1,0:T(8,128)(2,1)}, bf16[256,256]{1,0:T(8,128)(2,1)S(1)}, u32[]{:S(2)}, u32[]{:S(2)}) collective-permute-start(bf16[256,256]{1,0:T(8,128)(2,1)} %get-tuple-element.32), channel_id=1, source_target_pairs={{0,4},{4,8},{8,12},{12,16},{16,20},{20,24},{24,28},{28,32},{32,36}... | collective-permute-start | bytes 393224 | tf_op jit(solution)/shard_map/ppermute | solution.py:173
  109.1 44.4 %all-to-all-start.3 = ((f32[4,256,128]{2,1,0:T(8,128)}), f32[4,256,128]{2,1,0:T(8,128)}, u32[]{:S(2)}, u32[]{:S(2)}) async-start(f32[4,256,128]{2,1,0:T(8,128)} %broadcast_in_dim.15), calls=%async_computation.3 | async-start | bytes 1048576 | tf_op jit(solution)/shard_map/all_to_all | solution.py:255
  116.0 12.0 %collective-permute-start.19 = (bf16[256,256]{1,0:T(8,128)(2,1)}, bf16[256,256]{1,0:T(8,128)(2,1)S(1)}, u32[]{:S(2)}, u32[]{:S(2)}) collective-permute-start(bf16[256,256]{1,0:T(8,128)(2,1)} %copy-done.12), channel_id=1, source_target_pairs={{0,16},{4,20},{8,24},{12,28},{16,32},{20,36},{24,40},{28,44},{32,4... | collective-permute-start | bytes 393224 | tf_op jit(solution)/shard_map/ppermute | solution.py:173
  120.3 19.6 %collective-permute-start.21 = (bf16[256,256]{1,0:T(8,128)(2,1)}, bf16[256,256]{1,0:T(8,128)(2,1)S(1)}, u32[]{:S(2)}, u32[]{:S(2)}) collective-permute-start(bf16[256,256]{1,0:T(8,128)(2,1)} %copy-done.10), channel_id=1, source_target_pairs={{0,64},{4,68},{8,72},{12,76},{16,80},{20,84},{24,88},{28,92},{32,9... | collective-permute-start | bytes 393224 | tf_op jit(solution)/shard_map/ppermute | solution.py:173
  123.0 16.8 %collective-permute-start.22 = (bf16[256,256]{1,0:T(8,128)(2,1)S(1)}, bf16[256,256]{1,0:T(8,128)(2,1)S(1)}, u32[]{:S(2)}, u32[]{:S(2)}) collective-permute-start(bf16[256,256]{1,0:T(8,128)(2,1)S(1)} %get-tuple-element.37), channel_id=1, source_target_pairs={{0,128},{4,132},{8,136},{12,140},{16,144},{20,148},{24,152},{28,15... | collective-permute-start | bytes 393224 | tf_op jit(solution)/shard_map/ppermute | solution.py:173
  124.3 21.0 %collective-permute-start.23 = (bf16[256,256]{1,0:T(8,128)(2,1)S(1)}, bf16[256,256]{1,0:T(8,128)(2,1)S(1)}, u32[]{:S(2)}, u32[]{:S(2)}) collective-permute-start(bf16[256,256]{1,0:T(8,128)(2,1)S(1)} %get-tuple-element.38), channel_id=1, source_target_pairs={{0,192},{4,196},{8,200},{12,204},{16,208},{20,212},{24,216},{28,22... | collective-permute-start | bytes 393224 | tf_op jit(solution)/shard_map/ppermute | solution.py:173
  128.1 17.2 %collective-permute-start.24 = (bf16[256,256]{1,0:T(8,128)(2,1)S(1)}, bf16[256,256]{1,0:T(8,128)(2,1)S(1)}, u32[]{:S(2)}, u32[]{:S(2)}) collective-permute-start(bf16[256,256]{1,0:T(8,128)(2,1)S(1)} %get-tuple-element.39), channel_id=1, source_target_pairs={{0,224},{4,228},{8,232},{12,236},{16,240},{20,244},{24,248},{28,25... | collective-permute-start | bytes 393224 | tf_op jit(solution)/shard_map/ppermute | solution.py:173
  128.7 16.6 %collective-permute-start.25 = (bf16[256,256]{1,0:T(8,128)(2,1)S(1)}, bf16[256,256]{1,0:T(8,128)(2,1)S(1)}, u32[]{:S(2)}, u32[]{:S(2)}) collective-permute-start(bf16[256,256]{1,0:T(8,128)(2,1)S(1)} %get-tuple-element.40), channel_id=1, source_target_pairs={{0,240},{4,244},{8,248},{12,252},{16,0},{20,4},{24,8},{28,12},{32,... | collective-permute-start | bytes 393224 | tf_op jit(solution)/shard_map/ppermute | solution.py:173
  139.9 12.7 %collective-permute-start.27 = (bf16[256,256]{1,0:T(8,128)(2,1)S(1)}, bf16[256,256]{1,0:T(8,128)(2,1)S(1)}, u32[]{:S(2)}, u32[]{:S(2)}) collective-permute-start(bf16[256,256]{1,0:T(8,128)(2,1)S(1)} %get-tuple-element.42), channel_id=1, source_target_pairs={{0,252},{4,0},{8,4},{12,8},{16,12},{20,16},{24,20},{28,24},{32,28}... | collective-permute-start | bytes 393224 | tf_op jit(solution)/shard_map/ppermute | solution.py:173
  (21 other events, 218.7 us)

commit v2 on v1

v2 whole, which is shorter than its diff:
```python
import functools

import jax
import jax.numpy as jnp
from jax import lax
from jax.experimental import pallas as pl
from jax.experimental.pallas import tpu as pltpu
from jax.sharding import PartitionSpec as P

DISTANCES = (0, 1, 2, 4, 8, 16, 32, 48, 56, 60, 62, 63)
VMEM = pl.BlockSpec(memory_space=pltpu.VMEM)
SMEM = pl.BlockSpec(memory_space=pltpu.SMEM)
ANY = pl.BlockSpec(memory_space=pl.ANY)
HBM = pl.BlockSpec(memory_space=pltpu.HBM)


def dot_nt(a, b):
    return lax.dot_general(a, b, (((1,), (1,)), ((), ())), preferred_element_type=jnp.float32)


def dot_tn(a, b):
    return lax.dot_general(a, b, (((0,), (0,)), ((), ())), preferred_element_type=jnp.float32)


def build_kernel(row_ref, loc_ref, count_ref, vals_ref, dense_ref, acc_ref, held_ref, sems):
    parts = sems.shape[0]
    share = held_ref.shape[0] // parts
    copies = [
        pltpu.make_async_copy(
            vals_ref.at[pl.ds(p * share, share)], held_ref.at[pl.ds(p * share, share)], sems.at[p]
        )
        for p in range(parts)
    ]
    for copy in copies:
        copy.start()
    col_tiles = dense_ref.shape[1] // 128
    row_tiles = dense_ref.shape[0] // 128

    def clear(i, c):
        acc_ref[i] = jnp.zeros((128, 128), jnp.float32)
        return c

    lax.fori_loop(0, row_tiles * col_tiles, clear, 0)

    def add(k, c):
        at = row_ref[k] * col_tiles + loc_ref[k]
        acc_ref[at] = acc_ref[at] + held_ref[k].astype(jnp.float32)
        return c

    for p, copy in enumerate(copies):
        copy.wait()
        lax.fori_loop(p * share, jnp.minimum((p + 1) * share, count_ref[0]), add, 0)

    def cast(q, c):
        rows = pl.ds(pl.multiple_of(q * 128, 128), 128)
        for t in range(col_tiles):
            dense_ref[rows, t * 128 : (t + 1) * 128] = acc_ref[q * col_tiles + t].astype(jnp.bfloat16)
        return c

    lax.fori_loop(0, row_tiles, cast, 0)


def group_rows(rep, k):
    return pl.ds(pl.multiple_of((rep ^ k) * 256, 256), 256)


def forward_kernel(ks, rep_ref, dense_ref, *refs):
    feats, outs = refs[:12], refs[12:]
    for k, out in zip(ks, outs):
        total = jnp.zeros((256, 256), jnp.float32)
        for o in range(12):
            total = total + jnp.dot(
                dense_ref[group_rows(rep_ref[0], k), o * 256 : (o + 1) * 256],
                feats[o][...],
                preferred_element_type=jnp.float32,
            )
        out[...] = total.astype(out.dtype)


def update_kernel(
    rep_ref, own_ref, sib_ref, far_ref, x_ref, cot_ref, wa_ref, ws_ref, b_ref,
    upd_ref, dagg_ref, base_ref, g0_ref, g1_ref, g2_ref, g3_ref, grads_ref,
):
    agg = own_ref[...] + sib_ref[...].astype(jnp.float32) + far_ref[...].astype(jnp.float32)
    agg_b = agg.astype(jnp.bfloat16)
    x = x_ref[...]
    pre = (
        jnp.dot(agg_b, wa_ref[...], preferred_element_type=jnp.float32)
        + jnp.dot(x, ws_ref[...], preferred_element_type=jnp.float32)
        + b_ref[...]
    )
    s = 1.0 / (1.0 + jnp.exp(-pre))
    upd_ref[...] = (x.astype(jnp.float32) + pre * s).astype(jnp.bfloat16)
    cot = cot_ref[...].astype(jnp.float32)
    dpre = (cot * (s * (1.0 + pre * (1.0 - s)))).astype(jnp.bfloat16)
    dagg_ref[...] = dot_nt(dpre, wa_ref[...]).astype(jnp.bfloat16)
    base_ref[...] = cot + dot_nt(dpre, ws_ref[...])
    scale = 1.0 / 256.0
    for i, a in enumerate((agg_b, x)):
        total = dot_tn(a, dpre) * scale
        grads_ref[2 * i] = total[:, :128]
        grads_ref[2 * i + 1] = total[:, 128:]
    for k, out in enumerate((g0_ref, g1_ref, g2_ref, g3_ref)):
        out[...] = grads_ref[rep_ref[0] ^ k]


def scatter_kernel(rep_ref, dense_ref, d0, d1, d2, d3, *outs):
    turned = [d[...].T for d in (d0, d1, d2, d3)]
    for o in range(12):
        total = jnp.zeros((256, 256), jnp.float32)
        for k in range(4):
            total = total + jnp.dot(
                turned[k],
                dense_ref[group_rows(rep_ref[0], k), o * 256 : (o + 1) * 256],
                preferred_element_type=jnp.float32,
            )
        outs[o][...] = total.astype(outs[o].dtype)


def spread_kernel(pieces_ref, out_ref):
    total = jnp.sum(pieces_ref[...], axis=0)
    out_ref[...] = jnp.broadcast_to(total[None], out_ref.shape)


def join_kernel(rep_ref, q0, q1, q2, q3, out_ref, quarters_ref):
    for k, q in enumerate((q0, q1, q2, q3)):
        quarters_ref[rep_ref[0] ^ k] = q[...]
    for i in range(2):
        out_ref[i, :, :128] = quarters_ref[2 * i]
        out_ref[i, :, 128:] = quarters_ref[2 * i + 1]


def tile_grads_kernel(rep_ref, row_ref, loc_ref, count_ref, d0, d1, d2, d3, *refs):
    feats, out_ref, (grid_ref, zero_ref, sem) = refs[:12], refs[12], refs[13:]
    daggs = (d0, d1, d2, d3)
    rep = rep_ref[0]
    zero_ref[...] = jnp.zeros_like(zero_ref)
    slots = out_ref.shape[0]
    for k in range(4):
        first = (rep ^ k) * 2
        for o in range(12):
            block = (dot_nt(daggs[k][...], feats[o][...]) * (1.0 / 16.0)).astype(jnp.bfloat16)
            for a in range(2):
                for b in range(2):
                    grid_ref[(first + a) * 24 + 2 * o + b] = block[
                        a * 128 : (a + 1) * 128, b * 128 : (b + 1) * 128
                    ]

    def send(k, c):
        pltpu.make_async_copy(grid_ref.at[row_ref[k] * 24 + loc_ref[k]], out_ref.at[k], sem).start()
        return c

    def blank(k, c):
        pltpu.make_async_copy(zero_ref, out_ref.at[k], sem).start()
        return c

    lax.fori_loop(0, count_ref[0], send, 0)
    lax.fori_loop(count_ref[0], slots, blank, 0)

    def wait(k, c):
        pltpu.make_async_copy(zero_ref, out_ref.at[k], sem).wait()
        return c

    lax.fori_loop(0, slots, wait, 0)


def finish_kernel(base_ref, own_ref, *refs):
    terms, out_ref = refs[:-1], refs[-1]
    total = own_ref[...]
    for t in terms:
        total = total + t[...].astype(jnp.float32)
    out_ref[...] = (base_ref[...] + total.T).astype(jnp.bfloat16)


def shape(s, t=jnp.bfloat16):
    return jax.ShapeDtypeStruct(s, t)


def call(kernel, name, outs, ins, flops=0, moved=1 << 20, scratch=(), limit=24):
    return pl.pallas_call(
        kernel,
        out_shape=outs,
        in_specs=ins,
        out_specs=jax.tree.map(lambda _: VMEM, outs),
        scratch_shapes=scratch,
        compiler_params=pltpu.CompilerParams(vmem_limit_bytes=limit << 20),
        cost_estimate=pl.CostEstimate(flops=flops, bytes_accessed=moved, transcendentals=0),
        name=name,
    )


def local(node_feats, tile_vals, tile_row, tile_col, tile_count, w_agg, w_self, bias, cotangent):
    n_blk, n_rep = lax.axis_size("blk"), lax.axis_size("rep")
    group = lax.axis_index("blk")
    half = (group // 4) & 1
    rep = lax.axis_index("rep").reshape(1).astype(jnp.int32)
    row = tile_row[0, 0]
    count = tile_count[0]
    away = (lax.div(tile_col[0, 0], 2) - group + n_blk) & (n_blk - 1)
    place = jnp.zeros_like(away)
    for d in DISTANCES[1:]:
        place = place + (away >= d).astype(jnp.int32)
    place = jnp.where((half == 1) & (away == 4), 9, jnp.where((half == 1) & (away == 60), 3, place))
    loc = (2 * place + lax.rem(tile_col[0, 0], 2)).astype(jnp.int32)

    def move(x, source):
        pairs = [(source(g) * n_rep + r, g * n_rep + r) for g in range(n_blk) for r in range(n_rep)]
        return lax.ppermute(x, ("blk", "rep"), pairs)

    def from_blk(x, d):
        return move(x, lambda g: (g + d) % n_blk)

    def flip(x):
        return move(x, lambda g: g ^ 4)

    def from_plane(x, sign):
        return move(x, lambda g: (g + (8 * sign if g & 4 else -8 * sign)) % n_blk)

    def to_rep(x, k):
        return lax.ppermute(x, "rep", [(i, i ^ k) for i in range(n_rep)])

    def add(a, b):
        return (a.astype(jnp.float32) + b.astype(jnp.float32)).astype(jnp.bfloat16)

    up, down = from_blk(node_feats, 8), from_blk(node_feats, -8)
    right, left = from_blk(node_feats, 1), from_blk(node_feats, -1)
    across = flip(node_feats)
    up2, down2 = from_blk(up, 8), from_blk(down, -8)
    right2, left2 = from_blk(right, 1), from_blk(left, -1)
    across2 = from_plane(across, 1)
    up4 = from_blk(up2, 16)
    feats = [node_feats, right, right2, across, up, up2, up4, down2, down, across2, left2, left]

    dense = call(
        build_kernel, "build", shape((1024, 3072)), [SMEM, SMEM, SMEM, HBM], moved=10 << 20,
        scratch=[
            pltpu.VMEM((192, 128, 128), jnp.float32),
            pltpu.VMEM((128, 128, 128), jnp.bfloat16),
            pltpu.SemaphoreType.DMA((4,)),
        ],
        limit=36,
    )(row, loc, count, pltpu.with_memory_space_constraint(tile_vals[0, 0], pltpu.HBM))

    block = (256, 256)
    work = 2 * 1024 * 3072 * 256

    def forward(ks, types):
        return call(
            functools.partial(forward_kernel, ks), "forward", [shape(block, t) for t in types],
            [SMEM, VMEM] + [VMEM] * 12, flops=work // 2, moved=4 << 20,
        )(rep, dense, *feats)

    near, far = forward((1, 3), (jnp.bfloat16, jnp.bfloat16))
    near, far = to_rep(near, 1), to_rep(far, 1)
    own, other = forward((0, 2), (jnp.float32, jnp.float32))
    far = to_rep(add(other, far), 2)

    quarter = shape((256, 128), jnp.float32)
    updated, dagg, base, g0, g1, g2, g3 = call(
        update_kernel, "update",
        [shape(block), shape(block), shape(block, jnp.float32)] + [quarter] * 4,
        [SMEM] + [VMEM] * 8, flops=12 * 256**3, moved=2 << 20,
        scratch=[pltpu.VMEM((4, 256, 128), jnp.float32)],
    )(rep, own, near, far, node_feats, cotangent, w_agg, w_self, bias.reshape(1, 256))

    def gather_rep(x):
        x2, x1 = to_rep(x, 2), to_rep(x, 1)
        return [x, x1, x2, to_rep(x2, 1)]

    daggs = gather_rep(dagg)
    terms = call(
        scatter_kernel, "scatter", [shape(block, jnp.float32)] + [shape(block)] * 11,
        [SMEM] + [VMEM] * 5, flops=work, moved=8 << 20,
    )(rep, dense, *daggs)

    up2_sum = add(terms[5], from_blk(terms[6], -16))
    up_sum = add(terms[4], from_blk(up2_sum, -8))
    down_sum = add(terms[8], from_blk(terms[7], 8))
    right_sum = add(terms[1], from_blk(terms[2], -1))
    left_sum = add(terms[11], from_blk(terms[10], 1))
    across_sum = add(terms[3], from_plane(terms[9], -1))
    arrived = [
        from_blk(up_sum, -8), from_blk(down_sum, 8), from_blk(right_sum, -1), from_blk(left_sum, 1), flip(across_sum)
    ]

    tile_grads = pl.pallas_call(
        tile_grads_kernel,
        out_shape=shape((128, 128, 128)),
        in_specs=[SMEM] * 4 + [VMEM] * 16,
        out_specs=ANY,
        scratch_shapes=[
            pltpu.VMEM((192, 128, 128), jnp.bfloat16),
            pltpu.VMEM((128, 128), jnp.bfloat16),
            pltpu.SemaphoreType.DMA,
        ],
        compiler_params=pltpu.CompilerParams(vmem_limit_bytes=24 << 20),
        cost_estimate=pl.CostEstimate(flops=work, bytes_accessed=8 << 20, transcendentals=0),
        name="tile_grads",
    )(rep, row, loc, count, *daggs, *feats)

    feat_grad = call(finish_kernel, "finish", shape(block), [VMEM] * 7)(base, terms[0], *arrived)

    mine = g0 + to_rep(g1, 1)
    theirs = g2 + to_rep(g3, 1)
    mine = mine + to_rep(theirs, 2)
    pieces = lax.all_to_all(mine.reshape(n_blk, 4, 128), "blk", 0, 0, tiled=True)
    spread = call(spread_kernel, "spread", shape((n_blk, 4, 128), jnp.float32), [VMEM])(pieces)
    whole = lax.all_to_all(spread, "blk", 0, 0, tiled=True).reshape(256, 128)
    weight_grads = call(
        join_kernel, "join", shape((2, 256, 256), jnp.float32), [SMEM] + [VMEM] * 4,
        scratch=[pltpu.VMEM((4, 256, 128), jnp.float32)],
    )(rep, *gather_rep(whole))
    return updated, feat_grad, tile_grads.reshape(1, 1, 128, 128, 128), weight_grads


def solution(mesh):
    in_specs = (
        P(("blk", "rep"), None),
        P("blk", "rep", None, None, None),
        P("blk", "rep", None),
        P("blk", "rep", None),
        P("blk", "rep"),
        P(),
        P(),
        P(),
        P(("blk", "rep"), None),
    )
    out_specs = (
        P(("blk", "rep"), None),
        P(("blk", "rep"), None),
        P("blk", "rep", None, None, None),
        P(),
    )
    return jax.shard_map(local, mesh=mesh, in_specs=in_specs, out_specs=out_specs, check_vma=False)
```

time: 156 us -> 119 us (0.76)
  the two profiles are of different devices: /device:TPU:60 before, /device:TPU:1 now
where the time goes in v2:
time: 119 us
  starting transfers between devices  84.9 us (71%)
  Pallas kernels  16.3 us (14%)
  other arithmetic  7.87 us (7%)
  waiting for transfers between devices  7.38 us (6%)
  between operations  1.53 us (1%)
    ppermute x22, starting transfers between devices, move(): return lax.ppermute(x, ('blk', 'rep'), pairs)  48.4 us
    ppermute x12, starting transfers between devices, to_rep(): return lax.ppermute(x, 'rep', [(i, i ^ k) for i in range(n_rep)])  19.4 us
    all_to_all x1, starting transfers between devices, local(): whole = lax.all_to_all(spread, 'blk', 0, 0, tiled=True).reshape(256, 128)  9.84 us
    all_to_all x1, starting transfers between devices, local(): lax.all_to_all(mine.reshape(n_blk, 4, 128), 'blk', 0, 0, tiled=True)  7.28 us
    convert_element_type x7, other arithmetic, add(): return (a.astype(jnp.float32) + b.astype(jnp.float32)).astype(jnp.bfloat16)  6.49 us
    ppermute x12, waiting for transfers between devices, to_rep(): return lax.ppermute(x, 'rep', [(i, i ^ k) for i in range(n_rep)])  5.73 us
    pallas_call x1, Pallas kernels, local(): pl.pallas_call(tile_grads_kernel, out_shape=shape((128, 128, 128)), in_sp...  4.35 us
    pallas_call x1, Pallas kernels, local(): call(build_kernel, 'build', shape((1024, 3072)), [SMEM, SMEM, SMEM, HBM],...  4.04 us
  transfers between devices with their start and end apart: 36, of which 4 were waited for; matrix products, arithmetic and copies ran while one was open for 7% of the time, Pallas kernels for 11%

profile of v2, /device:TPU:1, one launch (start us, length us, event | category | flops | bytes accessed | tf_op | source)
XLA Modules:
  0.0 118.7 jit_solution(5162089869093372638)
XLA Ops:
  0.6 6.5 %collective-permute-start.3 = (bf16[256,256]{1,0:T(8,128)(2,1)}, bf16[256,256]{1,0:T(8,128)(2,1)S(1)}, u32[]{:S(2)}, u32[]{:S(2)}) collective-permute-start(bf16[256,256]{1,0:T(8,128)(2,1)} %refs_0_.5), channel_id=1, source_target_pairs={{32,0},{33,1},{34,2},{35,3},{36,4},{37,5},{38,6},{39,7},{40,8},{41... | collective-permute-start | bytes 393224 | tf_op jit(solution)/shard_map/ppermute | solution.py:208
  8.4 2.7 %collective-permute-start.2 = (bf16[256,256]{1,0:T(8,128)(2,1)}, bf16[256,256]{1,0:T(8,128)(2,1)S(1)}, u32[]{:S(2)}, u32[]{:S(2)}) collective-permute-start(bf16[256,256]{1,0:T(8,128)(2,1)} %refs_0_.5), channel_id=1, source_target_pairs={{16,0},{17,1},{18,2},{19,3},{20,4},{21,5},{22,6},{23,7},{24,8},{25... | collective-permute-start | bytes 393224 | tf_op jit(solution)/shard_map/ppermute | solution.py:208
  11.2 6.2 %collective-permute-start = (bf16[256,256]{1,0:T(8,128)(2,1)}, bf16[256,256]{1,0:T(8,128)(2,1)S(1)}, u32[]{:S(2)}, u32[]{:S(2)}) collective-permute-start(bf16[256,256]{1,0:T(8,128)(2,1)} %refs_0_.5), channel_id=1, source_target_pairs={{4,0},{5,1},{6,2},{7,3},{8,4},{9,5},{10,6},{11,7},{12,8},{13,9},{1... | collective-permute-start | bytes 393224 | tf_op jit(solution)/shard_map/ppermute | solution.py:208
  18.1 1.5 %collective-permute-start.7 = (bf16[256,256]{1,0:T(8,128)(2,1)S(1)}, bf16[256,256]{1,0:T(8,128)(2,1)S(1)}, u32[]{:S(2)}, u32[]{:S(2)}) collective-permute-start(bf16[256,256]{1,0:T(8,128)(2,1)S(1)} %collective-permute-done.6.refs_8_), channel_id=1, source_target_pairs={{224,0},{225,1},{226,2},{227,3},{228,4},{229,5},{230,6},{231,7},{2... | collective-permute-start | bytes 393224 | tf_op jit(solution)/shard_map/ppermute | solution.py:208
  19.7 7.3 %collective-permute-start.1 = (bf16[256,256]{1,0:T(8,128)(2,1)S(1)}, bf16[256,256]{1,0:T(8,128)(2,1)S(1)}, u32[]{:S(2)}, u32[]{:S(2)}) collective-permute-start(bf16[256,256]{1,0:T(8,128)(2,1)S(1)} %collective-permute-done.refs_1_), channel_id=1, source_target_pairs={{4,0},{5,1},{6,2},{7,3},{8,4},{9,5},{10,6},{11,7},{12,8},{13,9},{1... | collective-permute-start | bytes 393224 | tf_op jit(solution)/shard_map/ppermute | solution.py:208
  28.4 4.0 %build.1.dense_ref = bf16[1024,3072]{1,0:T(8,128)(2,1)S(1)} custom-call(s32[128]{0:T(128)S(1)} %bitcast.21, s32[128]{0:T(128)S(1)} %fusion.loc_ref, s32[1]{0:T(128)} %bitcast.16.count_ref, bf16[128,128,128]{2,1,0:T(8,128)(2,1)} %bitcast.24), custom_call_target="tpu_custom_call" | custom-call | bytes 10485760 | tf_op jit(solution)/shard_map/build/pallas_call | solution.py:234
  33.5 4.7 %collective-permute-start.12 = (bf16[256,256]{1,0:T(8,128)(2,1)S(1)}, bf16[256,256]{1,0:T(8,128)(2,1)S(1)}, u32[]{:S(2)}, u32[]{:S(2)}) collective-permute-start(bf16[256,256]{1,0:T(8,128)(2,1)S(1)} %get-tuple-element.30), channel_id=1, source_target_pairs={{0,1},{1,0},{2,3},{3,2},{4,5},{5,4},{6,7},{7,6},{8,9},{9,8},{10,11... | collective-permute-start | bytes 393224 | tf_op jit(solution)/shard_map/ppermute | solution.py:220
  40.1 3.9 %collective-permute-done.13.far_ref = bf16[256,256]{1,0:T(8,128)(2,1)S(1)} collective-permute-done((bf16[256,256]{1,0:T(8,128)(2,1)S(1)}, bf16[256,256]{1,0:T(8,128)(2,1)S(1)}, u32[]{:S(2)}, u32[]{:S(2)}) %collective-permute-start.13) | collective-permute-done | bytes 131104 | tf_op jit(solution)/shard_map/ppermute | solution.py:220
  46.0 1.6 %collective-permute-start.29 = (f32[256,128]{1,0:T(8,128)S(1)}, f32[256,128]{1,0:T(8,128)S(1)}, u32[]{:S(2)}, u32[]{:S(2)}) collective-permute-start(f32[256,128]{1,0:T(8,128)S(1)} %get-tuple-element.49), channel_id=1, source_target_pairs={{0,1},{1,0},{2,3},{3,2},{4,5},{5,4},{6,7},{7,6},{8,9},{9,8},{10,11... | collective-permute-start | bytes 393224 | tf_op jit(solution)/shard_map/ppermute | solution.py:220
  47.6 1.6 %collective-permute-done.15.d2 = bf16[256,256]{1,0:T(8,128)(2,1)S(1)} collective-permute-done((bf16[256,256]{1,0:T(8,128)(2,1)S(1)}, bf16[256,256]{1,0:T(8,128)(2,1)S(1)}, u32[]{:S(2)}, u32[]{:S(2)}) %collective-permute-start.15) | collective-permute-done | bytes 131104 | tf_op jit(solution)/shard_map/ppermute | solution.py:220
  49.1 2.5 %collective-permute-start.16 = (bf16[256,256]{1,0:T(8,128)(2,1)S(1)}, bf16[256,256]{1,0:T(8,128)(2,1)S(1)}, u32[]{:S(2)}, u32[]{:S(2)}) collective-permute-start(bf16[256,256]{1,0:T(8,128)(2,1)S(1)} %collective-permute-done.15.d2), channel_id=1, source_target_pairs={{0,1},{1,0},{2,3},{3,2},{4,5},{5,4},{6,7},{7,6},{8,9},{9,8},{10,11... | collective-permute-start | bytes 393224 | tf_op jit(solution)/shard_map/ppermute | solution.py:220
  52.6 2.3 %scatter.1 = (f32[256,256]{1,0:T(8,128)S(1)}, bf16[256,256]{1,0:T(8,128)(2,1)S(1)}, bf16[256,256]{1,0:T(8,128)(2,1)S(1)}, bf16[256,256]{1,0:T(8,128)(2,1)S(1)}, ...) custom-call(s32[1]{0:T(128)} %bitcast.rep_ref, ...), custom_call_target="tpu_custom_call" | custom-call | flops 1610612736 | bytes 8388608 | tf_op jit(solution)/shard_map/scatter/pallas_call | solution.py:271
  54.8 2.5 %collective-permute-start.17 = (bf16[256,256]{1,0:T(8,128)(2,1)}, bf16[256,256]{1,0:T(8,128)(2,1)}, u32[]{:S(2)}, u32[]{:S(2)}) collective-permute-start(bf16[256,256]{1,0:T(8,128)(2,1)} %get-tuple-element.37), channel_id=1, source_target_pairs={{192,0},{193,1},{194,2},{195,3},{196,4},{197,5},{198,6},{199,7},{2... | collective-permute-start | bytes 393224 | tf_op jit(solution)/shard_map/ppermute | solution.py:208
  58.0 7.3 %all-to-all-start = ((f32[64,4,128]{2,1,0:T(4,128)}), f32[64,4,128]{2,1,0:T(4,128)S(1)}, u32[]{:S(2)}, u32[]{:S(2)}) async-start(f32[64,4,128]{2,1,0:T(4,128)} %bitcast.26), calls=%async_computation | async-start | bytes 262144 | tf_op jit(solution)/shard_map/all_to_all | solution.py:306
  65.3 2.6 %collective-permute-start.20 = (bf16[256,256]{1,0:T(8,128)(2,1)}, bf16[256,256]{1,0:T(8,128)(2,1)S(1)}, u32[]{:S(2)}, u32[]{:S(2)}) collective-permute-start(bf16[256,256]{1,0:T(8,128)(2,1)} %copy-done.10), channel_id=1, source_target_pairs={{32,0},{33,1},{34,2},{35,3},{36,4},{37,5},{38,6},{39,7},{40,8},{41... | collective-permute-start | bytes 393224 | tf_op jit(solution)/shard_map/ppermute | solution.py:208
  69.0 6.0 %collective-permute-start.24 = (bf16[256,256]{1,0:T(8,128)(2,1)}, bf16[256,256]{1,0:T(8,128)(2,1)}, u32[]{:S(2)}, u32[]{:S(2)}) collective-permute-start(bf16[256,256]{1,0:T(8,128)(2,1)} %copy-done.8), channel_id=1, source_target_pairs={{4,0},{5,1},{6,2},{7,3},{8,4},{9,5},{10,6},{11,7},{12,8},{13,9},{1... | collective-permute-start | bytes 393224 | tf_op jit(solution)/shard_map/ppermute | solution.py:208
  75.1 1.6 %add_convert_fusion.5 = bf16[256,256]{1,0:T(8,128)(2,1)} fusion(bf16[256,256]{1,0:T(8,128)(2,1)} %collective-permute-done.17, bf16[256,256]{1,0:T(8,128)(2,1)S(1)} %get-tuple-element.36), kind=kLoop, calls=%fused_computation.5 | loop fusion | flops 262144 | bytes 393216 | tf_op jit(solution)/shard_map/convert_element_type | solution.py:223
  81.5 9.8 %all-to-all-start.1 = ((f32[64,4,128]{2,1,0:T(4,128)}), f32[64,4,128]{2,1,0:T(4,128)S(1)}, u32[]{:S(2)}, u32[]{:S(2)}) async-start(f32[64,4,128]{2,1,0:T(4,128)} %spread.1), calls=%async_computation.1 | async-start | bytes 262144 | tf_op jit(solution)/shard_map/all_to_all | solution.py:308
  92.3 7.1 %collective-permute-start.25 = (bf16[256,256]{1,0:T(8,128)(2,1)S(1)}, bf16[256,256]{1,0:T(8,128)(2,1)S(1)}, u32[]{:S(2)}, u32[]{:S(2)}) collective-permute-start(bf16[256,256]{1,0:T(8,128)(2,1)S(1)} %add_convert_fusion.1), channel_id=1, source_target_pairs={{4,0},{5,1},{6,2},{7,3},{8,4},{9,5},{10,6},{11,7},{12,8},{13,9},{1... | collective-permute-start | bytes 393224 | tf_op jit(solution)/shard_map/ppermute | solution.py:208
  99.4 1.6 %add_convert_fusion = bf16[256,256]{1,0:T(8,128)(2,1)} fusion(bf16[256,256]{1,0:T(8,128)(2,1)} %collective-permute-done.26, bf16[256,256]{1,0:T(8,128)(2,1)S(1)} %get-tuple-element.44), kind=kLoop, calls=%fused_computation | loop fusion | flops 262144 | bytes 393216 | tf_op jit(solution)/shard_map/convert_element_type | solution.py:223
  101.0 1.6 %all-to-all-done.1 = f32[64,4,128]{2,1,0:T(4,128)S(1)} async-done(((f32[64,4,128]{2,1,0:T(4,128)}), f32[64,4,128]{2,1,0:T(4,128)S(1)}, u32[]{:S(2)}, u32[]{:S(2)}) %all-to-all-start.1) | async-done | bytes 131104 | tf_op jit(solution)/shard_map/all_to_all | solution.py:308
  104.4 5.6 %collective-permute-start.31 = (f32[256,128]{1,0:T(8,128)S(1)}, f32[256,128]{1,0:T(8,128)S(1)}, u32[]{:S(2)}, u32[]{:S(2)}) collective-permute-start(f32[256,128]{1,0:T(8,128)S(1)} %bitcast.19), channel_id=1, source_target_pairs={{0,1},{1,0},{2,3},{3,2},{4,5},{5,4},{6,7},{7,6},{8,9},{9,8},{10,11... | collective-permute-start | bytes 393224 | tf_op jit(solution)/shard_map/ppermute | solution.py:220
  110.0 2.6 %collective-permute-start.33 = (f32[256,128]{1,0:T(8,128)S(1)}, f32[256,128]{1,0:T(8,128)S(1)}, u32[]{:S(2)}, u32[]{:S(2)}) collective-permute-start(f32[256,128]{1,0:T(8,128)S(1)} %collective-permute-done.32.q2), channel_id=1, source_target_pairs={{0,1},{1,0},{2,3},{3,2},{4,5},{5,4},{6,7},{7,6},{8,9},{9,8},{10,11... | collective-permute-start | bytes 393224 | tf_op jit(solution)/shard_map/ppermute | solution.py:220
  112.6 4.4 %tile_grads.1 = bf16[128,128,128]{2,1,0:T(8,128)(2,1)} custom-call(s32[1]{0:T(128)} %bitcast.rep_ref, s32[128]{0:T(128)S(1)} %bitcast.22, s32[128]{0:T(128)S(1)} %fusion.loc_ref, s32[1]{0:T(128)} %bitcast.17.count_ref, bf16[256,256]{1,0:T(8,128)(2,1)S(1)} %get-tuple-element.33.d0, bf16[256,256]{1,0:T(8,128)(2,1)S(1)} %collective-permute-done.14.d1, ...), custom_call_target="tpu_custom_call" | custom-call | flops 1610612736 | bytes 8388608 | tf_op jit(solution)/shard_map/tile_grads/pallas_call | solution.py:286
  (89 shorter events, 19.8 us)
Async XLA Ops:
  0.6 16.7 %collective-permute-start.3 = (bf16[256,256]{1,0:T(8,128)(2,1)}, bf16[256,256]{1,0:T(8,128)(2,1)S(1)}, u32[]{:S(2)}, u32[]{:S(2)}) collective-permute-start(bf16[256,256]{1,0:T(8,128)(2,1)} %refs_0_.5), channel_id=1, source_target_pairs={{32,0},{33,1},{34,2},{35,3},{36,4},{37,5},{38,6},{39,7},{40,8},{41... | collective-permute-start | bytes 393224 | tf_op jit(solution)/shard_map/ppermute | solution.py:208
  7.1 10.9 %collective-permute-start.9 = (bf16[256,256]{1,0:T(8,128)(2,1)}, bf16[256,256]{1,0:T(8,128)(2,1)S(1)}, u32[]{:S(2)}, u32[]{:S(2)}) collective-permute-start(bf16[256,256]{1,0:T(8,128)(2,1)} %refs_0_.5), channel_id=1, source_target_pairs={{252,0},{253,1},{254,2},{255,3},{0,4},{1,5},{2,6},{3,7},{4,8},{5,9... | collective-permute-start | bytes 393224 | tf_op jit(solution)/shard_map/ppermute | solution.py:208
  8.4 9.7 %collective-permute-start.6 = (bf16[256,256]{1,0:T(8,128)(2,1)}, bf16[256,256]{1,0:T(8,128)(2,1)S(1)}, u32[]{:S(2)}, u32[]{:S(2)}) collective-permute-start(bf16[256,256]{1,0:T(8,128)(2,1)} %refs_0_.5), channel_id=1, source_target_pairs={{224,0},{225,1},{226,2},{227,3},{228,4},{229,5},{230,6},{231,7},{2... | collective-permute-start | bytes 393224 | tf_op jit(solution)/shard_map/ppermute | solution.py:208
  8.4 11.2 %collective-permute-start.2 = (bf16[256,256]{1,0:T(8,128)(2,1)}, bf16[256,256]{1,0:T(8,128)(2,1)S(1)}, u32[]{:S(2)}, u32[]{:S(2)}) collective-permute-start(bf16[256,256]{1,0:T(8,128)(2,1)} %refs_0_.5), channel_id=1, source_target_pairs={{16,0},{17,1},{18,2},{19,3},{20,4},{21,5},{22,6},{23,7},{24,8},{25... | collective-permute-start | bytes 393224 | tf_op jit(solution)/shard_map/ppermute | solution.py:208
  11.2 8.6 %collective-permute-start = (bf16[256,256]{1,0:T(8,128)(2,1)}, bf16[256,256]{1,0:T(8,128)(2,1)S(1)}, u32[]{:S(2)}, u32[]{:S(2)}) collective-permute-start(bf16[256,256]{1,0:T(8,128)(2,1)} %refs_0_.5), channel_id=1, source_target_pairs={{4,0},{5,1},{6,2},{7,3},{8,4},{9,5},{10,6},{11,7},{12,8},{13,9},{1... | collective-permute-start | bytes 393224 | tf_op jit(solution)/shard_map/ppermute | solution.py:208
  17.3 9.8 %collective-permute-start.4 = (bf16[256,256]{1,0:T(8,128)(2,1)S(1)}, bf16[256,256]{1,0:T(8,128)(2,1)S(1)}, u32[]{:S(2)}, u32[]{:S(2)}) collective-permute-start(bf16[256,256]{1,0:T(8,128)(2,1)S(1)} %collective-permute-done.3.refs_4_), channel_id=1, source_target_pairs={{32,0},{33,1},{34,2},{35,3},{36,4},{37,5},{38,6},{39,7},{40,8},{41... | collective-permute-start | bytes 393224 | tf_op jit(solution)/shard_map/ppermute | solution.py:208
  18.0 14.5 %collective-permute-start.10 = (bf16[256,256]{1,0:T(8,128)(2,1)S(1)}, bf16[256,256]{1,0:T(8,128)(2,1)S(1)}, u32[]{:S(2)}, u32[]{:S(2)}) collective-permute-start(bf16[256,256]{1,0:T(8,128)(2,1)S(1)} %collective-permute-done.9.refs_11_), channel_id=1, source_target_pairs={{252,0},{253,1},{254,2},{255,3},{0,4},{1,5},{2,6},{3,7},{4,8},{5,9... | collective-permute-start | bytes 393224 | tf_op jit(solution)/shard_map/ppermute | solution.py:208
  18.1 14.4 %collective-permute-start.7 = (bf16[256,256]{1,0:T(8,128)(2,1)S(1)}, bf16[256,256]{1,0:T(8,128)(2,1)S(1)}, u32[]{:S(2)}, u32[]{:S(2)}) collective-permute-start(bf16[256,256]{1,0:T(8,128)(2,1)S(1)} %collective-permute-done.6.refs_8_), channel_id=1, source_target_pairs={{224,0},{225,1},{226,2},{227,3},{228,4},{229,5},{230,6},{231,7},{2... | collective-permute-start | bytes 393224 | tf_op jit(solution)/shard_map/ppermute | solution.py:208
  19.6 12.9 %collective-permute-start.8 = (bf16[256,256]{1,0:T(8,128)(2,1)S(1)}, bf16[256,256]{1,0:T(8,128)(2,1)S(1)}, u32[]{:S(2)}, u32[]{:S(2)}) collective-permute-start(bf16[256,256]{1,0:T(8,128)(2,1)S(1)} %collective-permute-done.2.refs_3_), channel_id=1, source_target_pairs={{224,0},{225,1},{226,2},{227,3},{228,4},{229,5},{230,6},{231,7},{2... | collective-permute-start | bytes 393224 | tf_op jit(solution)/shard_map/ppermute | solution.py:208
  19.7 12.8 %collective-permute-start.1 = (bf16[256,256]{1,0:T(8,128)(2,1)S(1)}, bf16[256,256]{1,0:T(8,128)(2,1)S(1)}, u32[]{:S(2)}, u32[]{:S(2)}) collective-permute-start(bf16[256,256]{1,0:T(8,128)(2,1)S(1)} %collective-permute-done.refs_1_), channel_id=1, source_target_pairs={{4,0},{5,1},{6,2},{7,3},{8,4},{9,5},{10,6},{11,7},{12,8},{13,9},{1... | collective-permute-start | bytes 393224 | tf_op jit(solution)/shard_map/ppermute | solution.py:208
  54.8 20.2 %collective-permute-start.17 = (bf16[256,256]{1,0:T(8,128)(2,1)}, bf16[256,256]{1,0:T(8,128)(2,1)}, u32[]{:S(2)}, u32[]{:S(2)}) collective-permute-start(bf16[256,256]{1,0:T(8,128)(2,1)} %get-tuple-element.37), channel_id=1, source_target_pairs={{192,0},{193,1},{194,2},{195,3},{196,4},{197,5},{198,6},{199,7},{2... | collective-permute-start | bytes 393224 | tf_op jit(solution)/shard_map/ppermute | solution.py:208
  58.0 22.7 %all-to-all-start = ((f32[64,4,128]{2,1,0:T(4,128)}), f32[64,4,128]{2,1,0:T(4,128)S(1)}, u32[]{:S(2)}, u32[]{:S(2)}) async-start(f32[64,4,128]{2,1,0:T(4,128)} %bitcast.26), calls=%async_computation | async-start | bytes 262144 | tf_op jit(solution)/shard_map/all_to_all | solution.py:306
  65.3 12.8 %collective-permute-start.20 = (bf16[256,256]{1,0:T(8,128)(2,1)}, bf16[256,256]{1,0:T(8,128)(2,1)S(1)}, u32[]{:S(2)}, u32[]{:S(2)}) collective-permute-start(bf16[256,256]{1,0:T(8,128)(2,1)} %copy-done.10), channel_id=1, source_target_pairs={{32,0},{33,1},{34,2},{35,3},{36,4},{37,5},{38,6},{39,7},{40,8},{41... | collective-permute-start | bytes 393224 | tf_op jit(solution)/shard_map/ppermute | solution.py:208
  67.9 12.2 %collective-permute-start.22 = (bf16[256,256]{1,0:T(8,128)(2,1)}, bf16[256,256]{1,0:T(8,128)(2,1)S(1)}, u32[]{:S(2)}, u32[]{:S(2)}) collective-permute-start(bf16[256,256]{1,0:T(8,128)(2,1)} %copy-done.9), channel_id=1, source_target_pairs={{252,0},{253,1},{254,2},{255,3},{0,4},{1,5},{2,6},{3,7},{4,8},{5,9... | collective-permute-start | bytes 393224 | tf_op jit(solution)/shard_map/ppermute | solution.py:208
  69.0 22.3 %collective-permute-start.24 = (bf16[256,256]{1,0:T(8,128)(2,1)}, bf16[256,256]{1,0:T(8,128)(2,1)}, u32[]{:S(2)}, u32[]{:S(2)}) collective-permute-start(bf16[256,256]{1,0:T(8,128)(2,1)} %copy-done.8), channel_id=1, source_target_pairs={{4,0},{5,1},{6,2},{7,3},{8,4},{9,5},{10,6},{11,7},{12,8},{13,9},{1... | collective-permute-start | bytes 393224 | tf_op jit(solution)/shard_map/ppermute | solution.py:208
  75.0 24.3 %collective-permute-start.26 = (bf16[256,256]{1,0:T(8,128)(2,1)}, bf16[256,256]{1,0:T(8,128)(2,1)}, u32[]{:S(2)}, u32[]{:S(2)}) collective-permute-start(bf16[256,256]{1,0:T(8,128)(2,1)} %copy-done.7), channel_id=1, source_target_pairs={{32,0},{33,1},{34,2},{35,3},{36,4},{37,5},{38,6},{39,7},{40,8},{41... | collective-permute-start | bytes 393224 | tf_op jit(solution)/shard_map/ppermute | solution.py:208
  76.7 24.3 %collective-permute-start.18 = (bf16[256,256]{1,0:T(8,128)(2,1)}, bf16[256,256]{1,0:T(8,128)(2,1)}, u32[]{:S(2)}, u32[]{:S(2)}) collective-permute-start(bf16[256,256]{1,0:T(8,128)(2,1)} %add_convert_fusion.5), channel_id=1, source_target_pairs={{224,0},{225,1},{226,2},{227,3},{228,4},{229,5},{230,6},{231,7},{2... | collective-permute-start | bytes 393224 | tf_op jit(solution)/shard_map/ppermute | solution.py:208
  78.8 24.9 %collective-permute-start.21 = (bf16[256,256]{1,0:T(8,128)(2,1)}, bf16[256,256]{1,0:T(8,128)(2,1)S(1)}, u32[]{:S(2)}, u32[]{:S(2)}) collective-permute-start(bf16[256,256]{1,0:T(8,128)(2,1)} %add_convert_fusion.3), channel_id=1, source_target_pairs={{32,0},{33,1},{34,2},{35,3},{36,4},{37,5},{38,6},{39,7},{40,8},{41... | collective-permute-start | bytes 393224 | tf_op jit(solution)/shard_map/ppermute | solution.py:208
  80.7 23.7 %collective-permute-start.23 = (bf16[256,256]{1,0:T(8,128)(2,1)}, bf16[256,256]{1,0:T(8,128)(2,1)S(1)}, u32[]{:S(2)}, u32[]{:S(2)}) collective-permute-start(bf16[256,256]{1,0:T(8,128)(2,1)} %add_convert_fusion.2), channel_id=1, source_target_pairs={{252,0},{253,1},{254,2},{255,3},{0,4},{1,5},{2,6},{3,7},{4,8},{5,9... | collective-permute-start | bytes 393224 | tf_op jit(solution)/shard_map/ppermute | solution.py:208
  81.5 21.1 %all-to-all-start.1 = ((f32[64,4,128]{2,1,0:T(4,128)}), f32[64,4,128]{2,1,0:T(4,128)S(1)}, u32[]{:S(2)}, u32[]{:S(2)}) async-start(f32[64,4,128]{2,1,0:T(4,128)} %spread.1), calls=%async_computation.1 | async-start | bytes 262144 | tf_op jit(solution)/shard_map/all_to_all | solution.py:308
  92.3 24.7 %collective-permute-start.25 = (bf16[256,256]{1,0:T(8,128)(2,1)S(1)}, bf16[256,256]{1,0:T(8,128)(2,1)S(1)}, u32[]{:S(2)}, u32[]{:S(2)}) collective-permute-start(bf16[256,256]{1,0:T(8,128)(2,1)S(1)} %add_convert_fusion.1), channel_id=1, source_target_pairs={{4,0},{5,1},{6,2},{7,3},{8,4},{9,5},{10,6},{11,7},{12,8},{13,9},{1... | collective-permute-start | bytes 393224 | tf_op jit(solution)/shard_map/ppermute | solution.py:208
  101.0 16.0 %collective-permute-start.27 = (bf16[256,256]{1,0:T(8,128)(2,1)}, bf16[256,256]{1,0:T(8,128)(2,1)S(1)}, u32[]{:S(2)}, u32[]{:S(2)}) collective-permute-start(bf16[256,256]{1,0:T(8,128)(2,1)} %add_convert_fusion), channel_id=1, source_target_pairs={{16,0},{17,1},{18,2},{19,3},{20,4},{21,5},{22,6},{23,7},{24,8},{25... | collective-permute-start | bytes 393224 | tf_op jit(solution)/shard_map/ppermute | solution.py:208
  103.8 13.2 %collective-permute-start.19 = (bf16[256,256]{1,0:T(8,128)(2,1)S(1)}, bf16[256,256]{1,0:T(8,128)(2,1)S(1)}, u32[]{:S(2)}, u32[]{:S(2)}) collective-permute-start(bf16[256,256]{1,0:T(8,128)(2,1)S(1)} %add_convert_fusion.4), channel_id=1, source_target_pairs={{224,0},{225,1},{226,2},{227,3},{228,4},{229,5},{230,6},{231,7},{2... | collective-permute-start | bytes 393224 | tf_op jit(solution)/shard_map/ppermute | solution.py:208
  104.4 13.4 %collective-permute-start.31 = (f32[256,128]{1,0:T(8,128)S(1)}, f32[256,128]{1,0:T(8,128)S(1)}, u32[]{:S(2)}, u32[]{:S(2)}) collective-permute-start(f32[256,128]{1,0:T(8,128)S(1)} %bitcast.19), channel_id=1, source_target_pairs={{0,1},{1,0},{2,3},{3,2},{4,5},{5,4},{6,7},{7,6},{8,9},{9,8},{10,11... | collective-permute-start | bytes 393224 | tf_op jit(solution)/shard_map/ppermute | solution.py:220
  (23 other events, 164.1 us)

commit v3 on v2

--- a/solution.py
+++ b/solution.py
@@ -104,14 +104,21 @@
         out[...] = grads_ref[rep_ref[0] ^ k]
 
 
-def scatter_kernel(rep_ref, dense_ref, d0, d1, d2, d3, *outs):
+def scatter_kernel(rep_ref, group_ref, dense_ref, d0, d1, d2, d3, *outs):
     turned = [d[...].T for d in (d0, d1, d2, d3)]
+    group = group_ref[0]
+    line, half = group & 3, (group // 4) & 1
+    swaps = (line >= 2, (line >= 2) ^ (half == 1))
     for o in range(12):
+        columns = pl.ds(o * 256, 256)
+        if o in (2, 3, 9, 10):
+            place = jnp.where(swaps[o & 1], 12 - o, o)
+            columns = pl.ds(pl.multiple_of(place * 256, 256), 256)
         total = jnp.zeros((256, 256), jnp.float32)
         for k in range(4):
             total = total + jnp.dot(
                 turned[k],
-                dense_ref[group_rows(rep_ref[0], k), o * 256 : (o + 1) * 256],
+                dense_ref[group_rows(rep_ref[0], k), columns],
                 preferred_element_type=jnp.float32,
             )
         outs[o][...] = total.astype(outs[o].dtype)
@@ -131,20 +138,18 @@
 
 
 def tile_grads_kernel(rep_ref, row_ref, loc_ref, count_ref, d0, d1, d2, d3, *refs):
-    feats, out_ref, (grid_ref, zero_ref, sem) = refs[:12], refs[12], refs[13:]
+    feats, out_ref, (grid_ref, all_ref, zero_ref, sem) = refs[:12], refs[12], refs[13:]
     daggs = (d0, d1, d2, d3)
     rep = rep_ref[0]
     zero_ref[...] = jnp.zeros_like(zero_ref)
     slots = out_ref.shape[0]
     for k in range(4):
-        first = (rep ^ k) * 2
-        for o in range(12):
-            block = (dot_nt(daggs[k][...], feats[o][...]) * (1.0 / 16.0)).astype(jnp.bfloat16)
-            for a in range(2):
-                for b in range(2):
-                    grid_ref[(first + a) * 24 + 2 * o + b] = block[
-                        a * 128 : (a + 1) * 128, b * 128 : (b + 1) * 128
-                    ]
+        all_ref[group_rows(rep, k)] = daggs[k][...]
+    for o in range(12):
+        block = (dot_nt(all_ref[...], feats[o][...]) * (1.0 / 16.0)).astype(jnp.bfloat16)
+        for q in range(8):
+            for b in range(2):
+                grid_ref[q * 24 + 2 * o + b] = block[q * 128 : (q + 1) * 128, b * 128 : (b + 1) * 128]
 
     def send(k, c):
         pltpu.make_async_copy(grid_ref.at[row_ref[k] * 24 + loc_ref[k]], out_ref.at[k], sem).start()
@@ -157,11 +162,7 @@
     lax.fori_loop(0, count_ref[0], send, 0)
     lax.fori_loop(count_ref[0], slots, blank, 0)
 
-    def wait(k, c):
-        pltpu.make_async_copy(zero_ref, out_ref.at[k], sem).wait()
-        return c
-
-    lax.fori_loop(0, slots, wait, 0)
+    pltpu.make_async_copy(out_ref, out_ref, sem).wait()
 
 
 def finish_kernel(base_ref, own_ref, *refs):
@@ -192,15 +193,17 @@
 def local(node_feats, tile_vals, tile_row, tile_col, tile_count, w_agg, w_self, bias, cotangent):
     n_blk, n_rep = lax.axis_size("blk"), lax.axis_size("rep")
     group = lax.axis_index("blk")
-    half = (group // 4) & 1
+    half, line = (group // 4) & 1, group & 3
     rep = lax.axis_index("rep").reshape(1).astype(jnp.int32)
+    ring = group.reshape(1).astype(jnp.int32)
     row = tile_row[0, 0]
     count = tile_count[0]
     away = (lax.div(tile_col[0, 0], 2) - group + n_blk) & (n_blk - 1)
     place = jnp.zeros_like(away)
     for d in DISTANCES[1:]:
         place = place + (away >= d).astype(jnp.int32)
-    place = jnp.where((half == 1) & (away == 4), 9, jnp.where((half == 1) & (away == 60), 3, place))
+    swapped = (line >= 2) & ((away == 4) | (away == 60) | (away == 2) | (away == 62))
+    place = jnp.where(swapped, 12 - place, place)
     loc = (2 * place + lax.rem(tile_col[0, 0], 2)).astype(jnp.int32)
 
     def move(x, source):
@@ -222,14 +225,22 @@
     def add(a, b):
         return (a.astype(jnp.float32) + b.astype(jnp.float32)).astype(jnp.bfloat16)
 
+    def cross(g):
+        return (g + 4 if g & 3 < 2 else g - 4) % n_blk
+
+    def other(g):
+        return (g - 4 if g & 3 < 2 else g + 4) % n_blk
+
+    crossing = move(node_feats, cross)
     up, down = from_blk(node_feats, 8), from_blk(node_feats, -8)
-    right, left = from_blk(node_feats, 1), from_blk(node_feats, -1)
-    across = flip(node_feats)
+    over2 = move(node_feats, lambda g: g ^ 2)
     up2, down2 = from_blk(up, 8), from_blk(down, -8)
-    right2, left2 = from_blk(right, 1), from_blk(left, -1)
-    across2 = from_plane(across, 1)
+    right = move(jnp.where(line == 0, crossing, node_feats), lambda g: g & ~3 | (g + 1) & 3)
+    left = move(jnp.where(line == 3, crossing, node_feats), lambda g: g & ~3 | (g - 1) & 3)
+    cross2 = move(crossing, lambda g: g ^ 2)
+    rest = move(node_feats, other)
     up4 = from_blk(up2, 16)
-    feats = [node_feats, right, right2, across, up, up2, up4, down2, down, across2, left2, left]
+    feats = [node_feats, right, over2, crossing, up, up2, up4, down2, down, rest, cross2, left]
 
     dense = call(
         build_kernel, "build", shape((1024, 3072)), [SMEM, SMEM, SMEM, HBM], moved=10 << 20,
@@ -270,8 +281,8 @@
     daggs = gather_rep(dagg)
     terms = call(
         scatter_kernel, "scatter", [shape(block, jnp.float32)] + [shape(block)] * 11,
-        [SMEM] + [VMEM] * 5, flops=work, moved=8 << 20,
-    )(rep, dense, *daggs)
+        [SMEM] * 2 + [VMEM] * 5, flops=work, moved=8 << 20,
+    )(rep, ring, dense, *daggs)
 
     up2_sum = add(terms[5], from_blk(terms[6], -16))
     up_sum = add(terms[4], from_blk(up2_sum, -8))
@@ -290,6 +301,7 @@
         out_specs=ANY,
         scratch_shapes=[
             pltpu.VMEM((192, 128, 128), jnp.bfloat16),
+            pltpu.VMEM((1024, 256), jnp.bfloat16),
             pltpu.VMEM((128, 128), jnp.bfloat16),
             pltpu.SemaphoreType.DMA,
         ],

time: 119 us -> 116 us (0.975)
  starting transfers between devices: 84.9 us -> 82 us
    ppermute x22, starting transfers between devices: 48.4 us -> 42.3 us  [move(): return lax.ppermute(x, ('blk', 'rep'), pairs)]
    all_to_all x1, starting transfers between devices: 7.28 us -> 9.79 us  [local(): lax.all_to_all(mine.reshape(n_blk, 4, 128), 'blk', 0, 0, tiled=True)]
  transfers between devices with their start and end apart: 36 -> 36, of which waited for: 4 -> 3; matrix products, arithmetic and copies ran while one was open for 7% -> 8% of each run, Pallas kernels for 11% -> 11%
where the time goes in v3:
time: 116 us; the launch traced here: 115 us
  starting transfers between devices  82 us (71%)
  Pallas kernels  16.3 us (14%)
  other arithmetic  8.79 us (8%)
  waiting for transfers between devices  6.22 us (5%)
  between operations  1.54 us (1%)
    ppermute x22, starting transfers between devices, move(): return lax.ppermute(x, ('blk', 'rep'), pairs)  42.3 us
    ppermute x12, starting transfers between devices, to_rep(): return lax.ppermute(x, 'rep', [(i, i ^ k) for i in range(n_rep)])  20.1 us
    all_to_all x1, starting transfers between devices, local(): whole = lax.all_to_all(spread, 'blk', 0, 0, tiled=True).reshape(256, 128)  9.84 us
    all_to_all x1, starting transfers between devices, local(): lax.all_to_all(mine.reshape(n_blk, 4, 128), 'blk', 0, 0, tiled=True)  9.79 us
    convert_element_type x7, other arithmetic, add(): return (a.astype(jnp.float32) + b.astype(jnp.float32)).astype(jnp.bfloat16)  6.5 us
    ppermute x12, waiting for transfers between devices, to_rep(): return lax.ppermute(x, 'rep', [(i, i ^ k) for i in range(n_rep)])  4.59 us
    pallas_call x1, Pallas kernels, local(): pl.pallas_call(tile_grads_kernel, out_shape=shape((128, 128, 128)), in_sp...  4.34 us
    pallas_call x1, Pallas kernels, local(): call(build_kernel, 'build', shape((1024, 3072)), [SMEM, SMEM, SMEM, HBM],...  4.04 us
  transfers between devices with their start and end apart: 36, of which 3 were waited for; matrix products, arithmetic and copies ran while one was open for 8% of the time, Pallas kernels for 11%

profile of v3, /device:TPU:1, one launch (start us, length us, event | category | flops | bytes accessed | tf_op | source)
XLA Modules:
  0.0 115.5 jit_solution(4906112639232204084)
XLA Ops:
  0.6 6.5 %collective-permute-start.3 = (bf16[256,256]{1,0:T(8,128)(2,1)}, bf16[256,256]{1,0:T(8,128)(2,1)S(1)}, u32[]{:S(2)}, u32[]{:S(2)}) collective-permute-start(bf16[256,256]{1,0:T(8,128)(2,1)} %refs_0_.5), channel_id=1, source_target_pairs={{32,0},{33,1},{34,2},{35,3},{36,4},{37,5},{38,6},{39,7},{40,8},{41... | collective-permute-start | bytes 393224 | tf_op jit(solution)/shard_map/ppermute | solution.py:211
  7.1 3.2 %collective-permute-start = (bf16[256,256]{1,0:T(8,128)(2,1)}, bf16[256,256]{1,0:T(8,128)(2,1)S(1)}, u32[]{:S(2)}, u32[]{:S(2)}) collective-permute-start(bf16[256,256]{1,0:T(8,128)(2,1)} %refs_0_.5), channel_id=1, source_target_pairs={{16,0},{17,1},{18,2},{19,3},{20,4},{21,5},{22,6},{23,7},{248,8},{2... | collective-permute-start | bytes 393224 | tf_op jit(solution)/shard_map/ppermute | solution.py:211
  11.0 4.1 %collective-permute-start.2 = (bf16[256,256]{1,0:T(8,128)(2,1)}, bf16[256,256]{1,0:T(8,128)(2,1)S(1)}, u32[]{:S(2)}, u32[]{:S(2)}) collective-permute-start(bf16[256,256]{1,0:T(8,128)(2,1)} %refs_0_.5), channel_id=1, source_target_pairs={{8,0},{9,1},{10,2},{11,3},{12,4},{13,5},{14,6},{15,7},{0,8},{1,9},... | collective-permute-start | bytes 393224 | tf_op jit(solution)/shard_map/ppermute | solution.py:211
  15.8 2.8 %collective-permute-start.4 = (bf16[256,256]{1,0:T(8,128)(2,1)S(1)}, bf16[256,256]{1,0:T(8,128)(2,1)S(1)}, u32[]{:S(2)}, u32[]{:S(2)}) collective-permute-start(bf16[256,256]{1,0:T(8,128)(2,1)S(1)} %collective-permute-done.3.refs_4_), channel_id=1, source_target_pairs={{32,0},{33,1},{34,2},{35,3},{36,4},{37,5},{38,6},{39,7},{40,8},{41... | collective-permute-start | bytes 393224 | tf_op jit(solution)/shard_map/ppermute | solution.py:211
  19.9 2.3 %collective-permute-start.1 = (bf16[256,256]{1,0:T(8,128)(2,1)S(1)}, bf16[256,256]{1,0:T(8,128)(2,1)S(1)}, u32[]{:S(2)}, u32[]{:S(2)}) collective-permute-start(bf16[256,256]{1,0:T(8,128)(2,1)S(1)} %get-tuple-element.51), channel_id=1, source_target_pairs={{4,0},{5,1},{6,2},{7,3},{8,4},{9,5},{10,6},{11,7},{12,8},{13,9},{1... | collective-permute-start | bytes 393224 | tf_op jit(solution)/shard_map/ppermute | solution.py:211
  24.9 4.0 %build.1.dense_ref = bf16[1024,3072]{1,0:T(8,128)(2,1)S(1)} custom-call(s32[128]{0:T(128)S(1)} %bitcast.22, s32[128]{0:T(128)S(1)} %fusion.loc_ref, s32[1]{0:T(128)} %bitcast.17.count_ref, bf16[128,128,128]{2,1,0:T(8,128)(2,1)} %bitcast.25), custom_call_target="tpu_custom_call" | custom-call | bytes 10485760 | tf_op jit(solution)/shard_map/build/pallas_call | solution.py:245
  29.9 3.3 %collective-permute-start.12 = (bf16[256,256]{1,0:T(8,128)(2,1)S(1)}, bf16[256,256]{1,0:T(8,128)(2,1)S(1)}, u32[]{:S(2)}, u32[]{:S(2)}) collective-permute-start(bf16[256,256]{1,0:T(8,128)(2,1)S(1)} %get-tuple-element.30), channel_id=1, source_target_pairs={{0,1},{1,0},{2,3},{3,2},{4,5},{5,4},{6,7},{7,6},{8,9},{9,8},{10,11... | collective-permute-start | bytes 393224 | tf_op jit(solution)/shard_map/ppermute | solution.py:223
  34.4 1.8 %collective-permute-start.13 = (bf16[256,256]{1,0:T(8,128)(2,1)S(1)}, bf16[256,256]{1,0:T(8,128)(2,1)S(1)}, u32[]{:S(2)}, u32[]{:S(2)}) collective-permute-start(bf16[256,256]{1,0:T(8,128)(2,1)S(1)} %add_convert_fusion.6), channel_id=1, source_target_pairs={{0,2},{1,3},{2,0},{3,1},{4,6},{5,7},{6,4},{7,5},{8,10},{9,11},{10,... | collective-permute-start | bytes 393224 | tf_op jit(solution)/shard_map/ppermute | solution.py:223
  36.2 3.5 %collective-permute-done.13.far_ref = bf16[256,256]{1,0:T(8,128)(2,1)S(1)} collective-permute-done((bf16[256,256]{1,0:T(8,128)(2,1)S(1)}, bf16[256,256]{1,0:T(8,128)(2,1)S(1)}, u32[]{:S(2)}, u32[]{:S(2)}) %collective-permute-start.13) | collective-permute-done | bytes 131104 | tf_op jit(solution)/shard_map/ppermute | solution.py:223
  42.1 1.6 %collective-permute-start.29 = (f32[256,128]{1,0:T(8,128)S(1)}, f32[256,128]{1,0:T(8,128)S(1)}, u32[]{:S(2)}, u32[]{:S(2)}) collective-permute-start(f32[256,128]{1,0:T(8,128)S(1)} %get-tuple-element.49), channel_id=1, source_target_pairs={{0,1},{1,0},{2,3},{3,2},{4,5},{5,4},{6,7},{7,6},{8,9},{9,8},{10,11... | collective-permute-start | bytes 393224 | tf_op jit(solution)/shard_map/ppermute | solution.py:223
  44.8 2.1 %collective-permute-start.16 = (bf16[256,256]{1,0:T(8,128)(2,1)S(1)}, bf16[256,256]{1,0:T(8,128)(2,1)S(1)}, u32[]{:S(2)}, u32[]{:S(2)}) collective-permute-start(bf16[256,256]{1,0:T(8,128)(2,1)S(1)} %collective-permute-done.15.d2), channel_id=1, source_target_pairs={{0,1},{1,0},{2,3},{3,2},{4,5},{5,4},{6,7},{7,6},{8,9},{9,8},{10,11... | collective-permute-start | bytes 393224 | tf_op jit(solution)/shard_map/ppermute | solution.py:223
  46.9 1.5 %collective-permute-start.30 = (f32[256,128]{1,0:T(8,128)S(1)}, f32[256,128]{1,0:T(8,128)S(1)}, u32[]{:S(2)}, u32[]{:S(2)}) collective-permute-start(f32[256,128]{1,0:T(8,128)S(1)} %add.90), channel_id=1, source_target_pairs={{0,2},{1,3},{2,0},{3,1},{4,6},{5,7},{6,4},{7,5},{8,10},{9,11},{10,... | collective-permute-start | bytes 393224 | tf_op jit(solution)/shard_map/ppermute | solution.py:223
  48.5 2.3 %scatter.1 = (f32[256,256]{1,0:T(8,128)S(1)}, bf16[256,256]{1,0:T(8,128)(2,1)S(1)}, bf16[256,256]{1,0:T(8,128)(2,1)S(1)}, bf16[256,256]{1,0:T(8,128)(2,1)S(1)}, ...) custom-call(s32[1]{0:T(128)} %bitcast.rep_ref, ...), custom_call_target="tpu_custom_call" | custom-call | flops 1610612736 | bytes 8388608 | tf_op jit(solution)/shard_map/scatter/pallas_call | solution.py:282
  52.3 9.8 %all-to-all-start = ((f32[64,4,128]{2,1,0:T(4,128)}), f32[64,4,128]{2,1,0:T(4,128)S(1)}, u32[]{:S(2)}, u32[]{:S(2)}) async-start(f32[64,4,128]{2,1,0:T(4,128)} %bitcast.27), calls=%async_computation | async-start | bytes 262144 | tf_op jit(solution)/shard_map/all_to_all | solution.py:318
  62.1 2.6 %collective-permute-start.20 = (bf16[256,256]{1,0:T(8,128)(2,1)}, bf16[256,256]{1,0:T(8,128)(2,1)S(1)}, u32[]{:S(2)}, u32[]{:S(2)}) collective-permute-start(bf16[256,256]{1,0:T(8,128)(2,1)} %copy-done.10), channel_id=1, source_target_pairs={{32,0},{33,1},{34,2},{35,3},{36,4},{37,5},{38,6},{39,7},{40,8},{41... | collective-permute-start | bytes 393224 | tf_op jit(solution)/shard_map/ppermute | solution.py:211
  65.8 6.0 %collective-permute-start.24 = (bf16[256,256]{1,0:T(8,128)(2,1)}, bf16[256,256]{1,0:T(8,128)(2,1)}, u32[]{:S(2)}, u32[]{:S(2)}) collective-permute-start(bf16[256,256]{1,0:T(8,128)(2,1)} %copy-done.8), channel_id=1, source_target_pairs={{4,0},{5,1},{6,2},{7,3},{8,4},{9,5},{10,6},{11,7},{12,8},{13,9},{1... | collective-permute-start | bytes 393224 | tf_op jit(solution)/shard_map/ppermute | solution.py:211
  71.8 1.6 %add_convert_fusion.5 = bf16[256,256]{1,0:T(8,128)(2,1)} fusion(bf16[256,256]{1,0:T(8,128)(2,1)} %collective-permute-done.17, bf16[256,256]{1,0:T(8,128)(2,1)S(1)} %get-tuple-element.36), kind=kLoop, calls=%fused_computation.5 | loop fusion | flops 262144 | bytes 393216 | tf_op jit(solution)/shard_map/convert_element_type | solution.py:226
  78.2 9.8 %all-to-all-start.1 = ((f32[64,4,128]{2,1,0:T(4,128)}), f32[64,4,128]{2,1,0:T(4,128)S(1)}, u32[]{:S(2)}, u32[]{:S(2)}) async-start(f32[64,4,128]{2,1,0:T(4,128)} %spread.1), calls=%async_computation.1 | async-start | bytes 262144 | tf_op jit(solution)/shard_map/all_to_all | solution.py:320
  89.0 7.1 %collective-permute-start.25 = (bf16[256,256]{1,0:T(8,128)(2,1)S(1)}, bf16[256,256]{1,0:T(8,128)(2,1)S(1)}, u32[]{:S(2)}, u32[]{:S(2)}) collective-permute-start(bf16[256,256]{1,0:T(8,128)(2,1)S(1)} %add_convert_fusion.1), channel_id=1, source_target_pairs={{4,0},{5,1},{6,2},{7,3},{8,4},{9,5},{10,6},{11,7},{12,8},{13,9},{1... | collective-permute-start | bytes 393224 | tf_op jit(solution)/shard_map/ppermute | solution.py:211
  96.2 1.6 %add_convert_fusion = bf16[256,256]{1,0:T(8,128)(2,1)} fusion(bf16[256,256]{1,0:T(8,128)(2,1)} %collective-permute-done.26, bf16[256,256]{1,0:T(8,128)(2,1)S(1)} %get-tuple-element.44), kind=kLoop, calls=%fused_computation | loop fusion | flops 262144 | bytes 393216 | tf_op jit(solution)/shard_map/convert_element_type | solution.py:226
  97.8 1.6 %all-to-all-done.1 = f32[64,4,128]{2,1,0:T(4,128)S(1)} async-done(((f32[64,4,128]{2,1,0:T(4,128)}), f32[64,4,128]{2,1,0:T(4,128)S(1)}, u32[]{:S(2)}, u32[]{:S(2)}) %all-to-all-start.1) | async-done | bytes 131104 | tf_op jit(solution)/shard_map/all_to_all | solution.py:320
  101.9 5.0 %collective-permute-start.31 = (f32[256,128]{1,0:T(8,128)S(1)}, f32[256,128]{1,0:T(8,128)S(1)}, u32[]{:S(2)}, u32[]{:S(2)}) collective-permute-start(f32[256,128]{1,0:T(8,128)S(1)} %bitcast.20), channel_id=1, source_target_pairs={{0,1},{1,0},{2,3},{3,2},{4,5},{5,4},{6,7},{7,6},{8,9},{9,8},{10,11... | collective-permute-start | bytes 393224 | tf_op jit(solution)/shard_map/ppermute | solution.py:223
  106.9 2.5 %collective-permute-start.33 = (f32[256,128]{1,0:T(8,128)S(1)}, f32[256,128]{1,0:T(8,128)S(1)}, u32[]{:S(2)}, u32[]{:S(2)}) collective-permute-start(f32[256,128]{1,0:T(8,128)S(1)} %collective-permute-done.32.q2), channel_id=1, source_target_pairs={{0,1},{1,0},{2,3},{3,2},{4,5},{5,4},{6,7},{7,6},{8,9},{9,8},{10,11... | collective-permute-start | bytes 393224 | tf_op jit(solution)/shard_map/ppermute | solution.py:223
  109.4 4.3 %tile_grads.1 = bf16[128,128,128]{2,1,0:T(8,128)(2,1)} custom-call(s32[1]{0:T(128)} %bitcast.rep_ref, s32[128]{0:T(128)S(1)} %bitcast.23, s32[128]{0:T(128)S(1)} %fusion.loc_ref, s32[1]{0:T(128)} %bitcast.18.count_ref, bf16[256,256]{1,0:T(8,128)(2,1)S(1)} %get-tuple-element.33.d0, bf16[256,256]{1,0:T(8,128)(2,1)S(1)} %collective-permute-done.14.d1, ...), custom_call_target="tpu_custom_call" | custom-call | flops 1610612736 | bytes 8388608 | tf_op jit(solution)/shard_map/tile_grads/pallas_call | solution.py:297
  (90 shorter events, 23.1 us)
Async XLA Ops:
  0.6 15.1 %collective-permute-start.3 = (bf16[256,256]{1,0:T(8,128)(2,1)}, bf16[256,256]{1,0:T(8,128)(2,1)S(1)}, u32[]{:S(2)}, u32[]{:S(2)}) collective-permute-start(bf16[256,256]{1,0:T(8,128)(2,1)} %refs_0_.5), channel_id=1, source_target_pairs={{32,0},{33,1},{34,2},{35,3},{36,4},{37,5},{38,6},{39,7},{40,8},{41... | collective-permute-start | bytes 393224 | tf_op jit(solution)/shard_map/ppermute | solution.py:211
  7.1 11.4 %collective-permute-start = (bf16[256,256]{1,0:T(8,128)(2,1)}, bf16[256,256]{1,0:T(8,128)(2,1)S(1)}, u32[]{:S(2)}, u32[]{:S(2)}) collective-permute-start(bf16[256,256]{1,0:T(8,128)(2,1)} %refs_0_.5), channel_id=1, source_target_pairs={{16,0},{17,1},{18,2},{19,3},{20,4},{21,5},{22,6},{23,7},{248,8},{2... | collective-permute-start | bytes 393224 | tf_op jit(solution)/shard_map/ppermute | solution.py:211
  10.3 9.6 %collective-permute-start.8 = (bf16[256,256]{1,0:T(8,128)(2,1)}, bf16[256,256]{1,0:T(8,128)(2,1)S(1)}, u32[]{:S(2)}, u32[]{:S(2)}) collective-permute-start(bf16[256,256]{1,0:T(8,128)(2,1)} %refs_0_.5), channel_id=1, source_target_pairs={{240,0},{241,1},{242,2},{243,3},{244,4},{245,5},{246,6},{247,7},{2... | collective-permute-start | bytes 393224 | tf_op jit(solution)/shard_map/ppermute | solution.py:211
  10.3 11.9 %collective-permute-start.6 = (bf16[256,256]{1,0:T(8,128)(2,1)}, bf16[256,256]{1,0:T(8,128)(2,1)S(1)}, u32[]{:S(2)}, u32[]{:S(2)}) collective-permute-start(bf16[256,256]{1,0:T(8,128)(2,1)} %refs_0_.5), channel_id=1, source_target_pairs={{224,0},{225,1},{226,2},{227,3},{228,4},{229,5},{230,6},{231,7},{2... | collective-permute-start | bytes 393224 | tf_op jit(solution)/shard_map/ppermute | solution.py:211
  11.0 11.2 %collective-permute-start.2 = (bf16[256,256]{1,0:T(8,128)(2,1)}, bf16[256,256]{1,0:T(8,128)(2,1)S(1)}, u32[]{:S(2)}, u32[]{:S(2)}) collective-permute-start(bf16[256,256]{1,0:T(8,128)(2,1)} %refs_0_.5), channel_id=1, source_target_pairs={{8,0},{9,1},{10,2},{11,3},{12,4},{13,5},{14,6},{15,7},{0,8},{1,9},... | collective-permute-start | bytes 393224 | tf_op jit(solution)/shard_map/ppermute | solution.py:211
  19.5 9.5 %collective-permute-start.10 = (bf16[256,256]{1,0:T(8,128)(2,1)S(1)}, bf16[256,256]{1,0:T(8,128)(2,1)S(1)}, u32[]{:S(2)}, u32[]{:S(2)}) collective-permute-start(bf16[256,256]{1,0:T(8,128)(2,1)S(1)} %get-tuple-element.50), channel_id=1, source_target_pairs={{12,0},{13,1},{14,2},{15,3},{0,4},{1,5},{2,6},{3,7},{4,8},{5,9},{6... | collective-permute-start | bytes 393224 | tf_op jit(solution)/shard_map/ppermute | solution.py:211
  19.9 9.0 %collective-permute-start.1 = (bf16[256,256]{1,0:T(8,128)(2,1)S(1)}, bf16[256,256]{1,0:T(8,128)(2,1)S(1)}, u32[]{:S(2)}, u32[]{:S(2)}) collective-permute-start(bf16[256,256]{1,0:T(8,128)(2,1)S(1)} %get-tuple-element.51), channel_id=1, source_target_pairs={{4,0},{5,1},{6,2},{7,3},{8,4},{9,5},{10,6},{11,7},{12,8},{13,9},{1... | collective-permute-start | bytes 393224 | tf_op jit(solution)/shard_map/ppermute | solution.py:211
  22.2 6.7 %collective-permute-start.9 = (bf16[256,256]{1,0:T(8,128)(2,1)S(1)}, bf16[256,256]{1,0:T(8,128)(2,1)S(1)}, u32[]{:S(2)}, u32[]{:S(2)}) collective-permute-start(bf16[256,256]{1,0:T(8,128)(2,1)S(1)} %collective-permute-done.refs_3_), channel_id=1, source_target_pairs={{8,0},{9,1},{10,2},{11,3},{12,4},{13,5},{14,6},{15,7},{0,8},{1,9},... | collective-permute-start | bytes 393224 | tf_op jit(solution)/shard_map/ppermute | solution.py:211
  50.8 21.0 %collective-permute-start.17 = (bf16[256,256]{1,0:T(8,128)(2,1)}, bf16[256,256]{1,0:T(8,128)(2,1)}, u32[]{:S(2)}, u32[]{:S(2)}) collective-permute-start(bf16[256,256]{1,0:T(8,128)(2,1)} %get-tuple-element.37), channel_id=1, source_target_pairs={{192,0},{193,1},{194,2},{195,3},{196,4},{197,5},{198,6},{199,7},{2... | collective-permute-start | bytes 393224 | tf_op jit(solution)/shard_map/ppermute | solution.py:211
  52.3 25.2 %all-to-all-start = ((f32[64,4,128]{2,1,0:T(4,128)}), f32[64,4,128]{2,1,0:T(4,128)S(1)}, u32[]{:S(2)}, u32[]{:S(2)}) async-start(f32[64,4,128]{2,1,0:T(4,128)} %bitcast.27), calls=%async_computation | async-start | bytes 262144 | tf_op jit(solution)/shard_map/all_to_all | solution.py:318
  62.1 12.8 %collective-permute-start.20 = (bf16[256,256]{1,0:T(8,128)(2,1)}, bf16[256,256]{1,0:T(8,128)(2,1)S(1)}, u32[]{:S(2)}, u32[]{:S(2)}) collective-permute-start(bf16[256,256]{1,0:T(8,128)(2,1)} %copy-done.10), channel_id=1, source_target_pairs={{32,0},{33,1},{34,2},{35,3},{36,4},{37,5},{38,6},{39,7},{40,8},{41... | collective-permute-start | bytes 393224 | tf_op jit(solution)/shard_map/ppermute | solution.py:211
  64.6 12.2 %collective-permute-start.22 = (bf16[256,256]{1,0:T(8,128)(2,1)}, bf16[256,256]{1,0:T(8,128)(2,1)S(1)}, u32[]{:S(2)}, u32[]{:S(2)}) collective-permute-start(bf16[256,256]{1,0:T(8,128)(2,1)} %copy-done.9), channel_id=1, source_target_pairs={{252,0},{253,1},{254,2},{255,3},{0,4},{1,5},{2,6},{3,7},{4,8},{5,9... | collective-permute-start | bytes 393224 | tf_op jit(solution)/shard_map/ppermute | solution.py:211
  65.8 22.3 %collective-permute-start.24 = (bf16[256,256]{1,0:T(8,128)(2,1)}, bf16[256,256]{1,0:T(8,128)(2,1)}, u32[]{:S(2)}, u32[]{:S(2)}) collective-permute-start(bf16[256,256]{1,0:T(8,128)(2,1)} %copy-done.8), channel_id=1, source_target_pairs={{4,0},{5,1},{6,2},{7,3},{8,4},{9,5},{10,6},{11,7},{12,8},{13,9},{1... | collective-permute-start | bytes 393224 | tf_op jit(solution)/shard_map/ppermute | solution.py:211
  71.8 24.3 %collective-permute-start.26 = (bf16[256,256]{1,0:T(8,128)(2,1)}, bf16[256,256]{1,0:T(8,128)(2,1)}, u32[]{:S(2)}, u32[]{:S(2)}) collective-permute-start(bf16[256,256]{1,0:T(8,128)(2,1)} %copy-done.7), channel_id=1, source_target_pairs={{32,0},{33,1},{34,2},{35,3},{36,4},{37,5},{38,6},{39,7},{40,8},{41... | collective-permute-start | bytes 393224 | tf_op jit(solution)/shard_map/ppermute | solution.py:211
  73.4 24.3 %collective-permute-start.18 = (bf16[256,256]{1,0:T(8,128)(2,1)}, bf16[256,256]{1,0:T(8,128)(2,1)}, u32[]{:S(2)}, u32[]{:S(2)}) collective-permute-start(bf16[256,256]{1,0:T(8,128)(2,1)} %add_convert_fusion.5), channel_id=1, source_target_pairs={{224,0},{225,1},{226,2},{227,3},{228,4},{229,5},{230,6},{231,7},{2... | collective-permute-start | bytes 393224 | tf_op jit(solution)/shard_map/ppermute | solution.py:211
  75.6 25.6 %collective-permute-start.21 = (bf16[256,256]{1,0:T(8,128)(2,1)}, bf16[256,256]{1,0:T(8,128)(2,1)S(1)}, u32[]{:S(2)}, u32[]{:S(2)}) collective-permute-start(bf16[256,256]{1,0:T(8,128)(2,1)} %add_convert_fusion.3), channel_id=1, source_target_pairs={{32,0},{33,1},{34,2},{35,3},{36,4},{37,5},{38,6},{39,7},{40,8},{41... | collective-permute-start | bytes 393224 | tf_op jit(solution)/shard_map/ppermute | solution.py:211
  77.5 24.4 %collective-permute-start.23 = (bf16[256,256]{1,0:T(8,128)(2,1)}, bf16[256,256]{1,0:T(8,128)(2,1)S(1)}, u32[]{:S(2)}, u32[]{:S(2)}) collective-permute-start(bf16[256,256]{1,0:T(8,128)(2,1)} %add_convert_fusion.2), channel_id=1, source_target_pairs={{252,0},{253,1},{254,2},{255,3},{0,4},{1,5},{2,6},{3,7},{4,8},{5,9... | collective-permute-start | bytes 393224 | tf_op jit(solution)/shard_map/ppermute | solution.py:211
  78.2 21.1 %all-to-all-start.1 = ((f32[64,4,128]{2,1,0:T(4,128)}), f32[64,4,128]{2,1,0:T(4,128)S(1)}, u32[]{:S(2)}, u32[]{:S(2)}) async-start(f32[64,4,128]{2,1,0:T(4,128)} %spread.1), calls=%async_computation.1 | async-start | bytes 262144 | tf_op jit(solution)/shard_map/all_to_all | solution.py:320
  89.0 24.7 %collective-permute-start.25 = (bf16[256,256]{1,0:T(8,128)(2,1)S(1)}, bf16[256,256]{1,0:T(8,128)(2,1)S(1)}, u32[]{:S(2)}, u32[]{:S(2)}) collective-permute-start(bf16[256,256]{1,0:T(8,128)(2,1)S(1)} %add_convert_fusion.1), channel_id=1, source_target_pairs={{4,0},{5,1},{6,2},{7,3},{8,4},{9,5},{10,6},{11,7},{12,8},{13,9},{1... | collective-permute-start | bytes 393224 | tf_op jit(solution)/shard_map/ppermute | solution.py:211
  97.8 16.0 %collective-permute-start.27 = (bf16[256,256]{1,0:T(8,128)(2,1)}, bf16[256,256]{1,0:T(8,128)(2,1)S(1)}, u32[]{:S(2)}, u32[]{:S(2)}) collective-permute-start(bf16[256,256]{1,0:T(8,128)(2,1)} %add_convert_fusion), channel_id=1, source_target_pairs={{16,0},{17,1},{18,2},{19,3},{20,4},{21,5},{22,6},{23,7},{24,8},{25... | collective-permute-start | bytes 393224 | tf_op jit(solution)/shard_map/ppermute | solution.py:211
  99.3 7.6 %collective-permute-start.32 = (f32[256,128]{1,0:T(8,128)S(1)}, f32[256,128]{1,0:T(8,128)S(1)}, u32[]{:S(2)}, u32[]{:S(2)}) collective-permute-start(f32[256,128]{1,0:T(8,128)S(1)} %bitcast.19), channel_id=1, source_target_pairs={{0,2},{1,3},{2,0},{3,1},{4,6},{5,7},{6,4},{7,5},{8,10},{9,11},{10,... | collective-permute-start | bytes 393224 | tf_op jit(solution)/shard_map/ppermute | solution.py:223
  101.2 12.6 %collective-permute-start.19 = (bf16[256,256]{1,0:T(8,128)(2,1)S(1)}, bf16[256,256]{1,0:T(8,128)(2,1)S(1)}, u32[]{:S(2)}, u32[]{:S(2)}) collective-permute-start(bf16[256,256]{1,0:T(8,128)(2,1)S(1)} %add_convert_fusion.4), channel_id=1, source_target_pairs={{224,0},{225,1},{226,2},{227,3},{228,4},{229,5},{230,6},{231,7},{2... | collective-permute-start | bytes 393224 | tf_op jit(solution)/shard_map/ppermute | solution.py:211
  101.9 12.7 %collective-permute-start.31 = (f32[256,128]{1,0:T(8,128)S(1)}, f32[256,128]{1,0:T(8,128)S(1)}, u32[]{:S(2)}, u32[]{:S(2)}) collective-permute-start(f32[256,128]{1,0:T(8,128)S(1)} %bitcast.20), channel_id=1, source_target_pairs={{0,1},{1,0},{2,3},{3,2},{4,5},{5,4},{6,7},{7,6},{8,9},{9,8},{10,11... | collective-permute-start | bytes 393224 | tf_op jit(solution)/shard_map/ppermute | solution.py:223
  106.9 7.7 %collective-permute-start.33 = (f32[256,128]{1,0:T(8,128)S(1)}, f32[256,128]{1,0:T(8,128)S(1)}, u32[]{:S(2)}, u32[]{:S(2)}) collective-permute-start(f32[256,128]{1,0:T(8,128)S(1)} %collective-permute-done.32.q2), channel_id=1, source_target_pairs={{0,1},{1,0},{2,3},{3,2},{4,5},{5,4},{6,7},{7,6},{8,9},{9,8},{10,11... | collective-permute-start | bytes 393224 | tf_op jit(solution)/shard_map/ppermute | solution.py:223
  (23 other events, 156.6 us)

commit v4 on v3

--- a/solution.py
+++ b/solution.py
@@ -22,7 +22,7 @@
     return lax.dot_general(a, b, (((0,), (0,)), ((), ())), preferred_element_type=jnp.float32)
 
 
-def build_kernel(row_ref, loc_ref, count_ref, vals_ref, dense_ref, acc_ref, held_ref, sems):
+def build_kernel(at_ref, count_ref, vals_ref, dense_ref, acc_ref, held_ref, sems):
     parts = sems.shape[0]
     share = held_ref.shape[0] // parts
     copies = [
@@ -43,7 +43,7 @@
     lax.fori_loop(0, row_tiles * col_tiles, clear, 0)
 
     def add(k, c):
-        at = row_ref[k] * col_tiles + loc_ref[k]
+        at = at_ref[k]
         acc_ref[at] = acc_ref[at] + held_ref[k].astype(jnp.float32)
         return c
 
@@ -129,15 +129,7 @@
     out_ref[...] = jnp.broadcast_to(total[None], out_ref.shape)
 
 
-def join_kernel(rep_ref, q0, q1, q2, q3, out_ref, quarters_ref):
-    for k, q in enumerate((q0, q1, q2, q3)):
-        quarters_ref[rep_ref[0] ^ k] = q[...]
-    for i in range(2):
-        out_ref[i, :, :128] = quarters_ref[2 * i]
-        out_ref[i, :, 128:] = quarters_ref[2 * i + 1]
-
-
-def tile_grads_kernel(rep_ref, row_ref, loc_ref, count_ref, d0, d1, d2, d3, *refs):
+def tile_grads_kernel(rep_ref, at_ref, count_ref, d0, d1, d2, d3, *refs):
     feats, out_ref, (grid_ref, all_ref, zero_ref, sem) = refs[:12], refs[12], refs[13:]
     daggs = (d0, d1, d2, d3)
     rep = rep_ref[0]
@@ -152,7 +144,7 @@
                 grid_ref[q * 24 + 2 * o + b] = block[q * 128 : (q + 1) * 128, b * 128 : (b + 1) * 128]
 
     def send(k, c):
-        pltpu.make_async_copy(grid_ref.at[row_ref[k] * 24 + loc_ref[k]], out_ref.at[k], sem).start()
+        pltpu.make_async_copy(grid_ref.at[at_ref[k]], out_ref.at[k], sem).start()
         return c
 
     def blank(k, c):
@@ -165,12 +157,17 @@
     pltpu.make_async_copy(out_ref, out_ref, sem).wait()
 
 
-def finish_kernel(base_ref, own_ref, *refs):
-    terms, out_ref = refs[:-1], refs[-1]
+def finish_kernel(rep_ref, base_ref, own_ref, *refs):
+    terms, quarters, (out_ref, grads_ref, held_ref) = refs[:5], refs[5:9], refs[9:]
     total = own_ref[...]
     for t in terms:
         total = total + t[...].astype(jnp.float32)
     out_ref[...] = (base_ref[...] + total.T).astype(jnp.bfloat16)
+    for k, q in enumerate(quarters):
+        held_ref[rep_ref[0] ^ k] = q[...]
+    for i in range(2):
+        grads_ref[i, :, :128] = held_ref[2 * i]
+        grads_ref[i, :, 128:] = held_ref[2 * i + 1]
 
 
 def shape(s, t=jnp.bfloat16):
@@ -196,7 +193,6 @@
     half, line = (group // 4) & 1, group & 3
     rep = lax.axis_index("rep").reshape(1).astype(jnp.int32)
     ring = group.reshape(1).astype(jnp.int32)
-    row = tile_row[0, 0]
     count = tile_count[0]
     away = (lax.div(tile_col[0, 0], 2) - group + n_blk) & (n_blk - 1)
     place = jnp.zeros_like(away)
@@ -204,7 +200,7 @@
         place = place + (away >= d).astype(jnp.int32)
     swapped = (line >= 2) & ((away == 4) | (away == 60) | (away == 2) | (away == 62))
     place = jnp.where(swapped, 12 - place, place)
-    loc = (2 * place + lax.rem(tile_col[0, 0], 2)).astype(jnp.int32)
+    at = (24 * tile_row[0, 0] + 2 * place + lax.rem(tile_col[0, 0], 2)).astype(jnp.int32)
 
     def move(x, source):
         pairs = [(source(g) * n_rep + r, g * n_rep + r) for g in range(n_blk) for r in range(n_rep)]
@@ -243,14 +239,14 @@
     feats = [node_feats, right, over2, crossing, up, up2, up4, down2, down, rest, cross2, left]
 
     dense = call(
-        build_kernel, "build", shape((1024, 3072)), [SMEM, SMEM, SMEM, HBM], moved=10 << 20,
+        build_kernel, "build", shape((1024, 3072)), [SMEM, SMEM, HBM], moved=10 << 20,
         scratch=[
             pltpu.VMEM((192, 128, 128), jnp.float32),
             pltpu.VMEM((128, 128, 128), jnp.bfloat16),
             pltpu.SemaphoreType.DMA((4,)),
         ],
         limit=36,
-    )(row, loc, count, pltpu.with_memory_space_constraint(tile_vals[0, 0], pltpu.HBM))
+    )(at, count, pltpu.with_memory_space_constraint(tile_vals[0, 0], pltpu.HBM))
 
     block = (256, 256)
     work = 2 * 1024 * 3072 * 256
@@ -297,7 +293,7 @@
     tile_grads = pl.pallas_call(
         tile_grads_kernel,
         out_shape=shape((128, 128, 128)),
-        in_specs=[SMEM] * 4 + [VMEM] * 16,
+        in_specs=[SMEM] * 3 + [VMEM] * 16,
         out_specs=ANY,
         scratch_shapes=[
             pltpu.VMEM((192, 128, 128), jnp.bfloat16),
@@ -308,9 +304,7 @@
         compiler_params=pltpu.CompilerParams(vmem_limit_bytes=24 << 20),
         cost_estimate=pl.CostEstimate(flops=work, bytes_accessed=8 << 20, transcendentals=0),
         name="tile_grads",
-    )(rep, row, loc, count, *daggs, *feats)
-
-    feat_grad = call(finish_kernel, "finish", shape(block), [VMEM] * 7)(base, terms[0], *arrived)
+    )(rep, at, count, *daggs, *feats)
 
     mine = g0 + to_rep(g1, 1)
     theirs = g2 + to_rep(g3, 1)
@@ -318,10 +312,10 @@
     pieces = lax.all_to_all(mine.reshape(n_blk, 4, 128), "blk", 0, 0, tiled=True)
     spread = call(spread_kernel, "spread", shape((n_blk, 4, 128), jnp.float32), [VMEM])(pieces)
     whole = lax.all_to_all(spread, "blk", 0, 0, tiled=True).reshape(256, 128)
-    weight_grads = call(
-        join_kernel, "join", shape((2, 256, 256), jnp.float32), [SMEM] + [VMEM] * 4,
+    feat_grad, weight_grads = call(
+        finish_kernel, "finish", [shape(block), shape((2, 256, 256), jnp.float32)], [SMEM] + [VMEM] * 11,
         scratch=[pltpu.VMEM((4, 256, 128), jnp.float32)],
-    )(rep, *gather_rep(whole))
+    )(rep, base, terms[0], *arrived, *gather_rep(whole))
     return updated, feat_grad, tile_grads.reshape(1, 1, 128, 128, 128), weight_grads
 
 

time: 116 us -> 115 us (level)
    pallas_call x3 -> x2, Pallas kernels: 5.73 us -> 5.03 us  [the longest x1 4.04 us: local(): call(build_kernel, 'build', shape((1024, 3072)), [SMEM, SMEM, HBM], moved...]
where the time goes in v4:
time: 115 us; the launch traced here: 114 us
  starting transfers between devices  82 us (71%)
  Pallas kernels  15.6 us (14%)
  other arithmetic  8.81 us (8%)
  waiting for transfers between devices  6.26 us (5%)
  between operations  1.55 us (1%)
    ppermute x22, starting transfers between devices, move(): return lax.ppermute(x, ('blk', 'rep'), pairs)  43.1 us
    ppermute x12, starting transfers between devices, to_rep(): return lax.ppermute(x, 'rep', [(i, i ^ k) for i in range(n_rep)])  19.6 us
    all_to_all x1, starting transfers between devices, local(): whole = lax.all_to_all(spread, 'blk', 0, 0, tiled=True).reshape(256, 128)  9.84 us
    all_to_all x1, starting transfers between devices, local(): lax.all_to_all(mine.reshape(n_blk, 4, 128), 'blk', 0, 0, tiled=True)  9.56 us
    convert_element_type x7, other arithmetic, add(): return (a.astype(jnp.float32) + b.astype(jnp.float32)).astype(jnp.bfloat16)  6.5 us
    ppermute x12, waiting for transfers between devices, to_rep(): return lax.ppermute(x, 'rep', [(i, i ^ k) for i in range(n_rep)])  4.61 us
    pallas_call x1, Pallas kernels, local(): pl.pallas_call(tile_grads_kernel, out_shape=shape((128, 128, 128)), in_sp...  4.34 us
    pallas_call x1, Pallas kernels, local(): call(build_kernel, 'build', shape((1024, 3072)), [SMEM, SMEM, HBM], moved...  4.04 us
  transfers between devices with their start and end apart: 36, of which 3 were waited for; matrix products, arithmetic and copies ran while one was open for 8% of the time, Pallas kernels for 11%

profile of v4, /device:TPU:1, one launch (start us, length us, event | category | flops | bytes accessed | tf_op | source)
XLA Modules:
  0.0 114.3 jit_solution(5274126384840758684)
XLA Ops:
  0.6 6.5 %collective-permute-start.3 = (bf16[256,256]{1,0:T(8,128)(2,1)}, bf16[256,256]{1,0:T(8,128)(2,1)S(1)}, u32[]{:S(2)}, u32[]{:S(2)}) collective-permute-start(bf16[256,256]{1,0:T(8,128)(2,1)} %refs_0_.5), channel_id=1, source_target_pairs={{32,0},{33,1},{34,2},{35,3},{36,4},{37,5},{38,6},{39,7},{40,8},{41... | collective-permute-start | bytes 393224 | tf_op jit(solution)/shard_map/ppermute | solution.py:207
  7.1 3.2 %collective-permute-start = (bf16[256,256]{1,0:T(8,128)(2,1)}, bf16[256,256]{1,0:T(8,128)(2,1)S(1)}, u32[]{:S(2)}, u32[]{:S(2)}) collective-permute-start(bf16[256,256]{1,0:T(8,128)(2,1)} %refs_0_.5), channel_id=1, source_target_pairs={{16,0},{17,1},{18,2},{19,3},{20,4},{21,5},{22,6},{23,7},{248,8},{2... | collective-permute-start | bytes 393224 | tf_op jit(solution)/shard_map/ppermute | solution.py:207
  11.0 4.1 %collective-permute-start.2 = (bf16[256,256]{1,0:T(8,128)(2,1)}, bf16[256,256]{1,0:T(8,128)(2,1)S(1)}, u32[]{:S(2)}, u32[]{:S(2)}) collective-permute-start(bf16[256,256]{1,0:T(8,128)(2,1)} %refs_0_.5), channel_id=1, source_target_pairs={{8,0},{9,1},{10,2},{11,3},{12,4},{13,5},{14,6},{15,7},{0,8},{1,9},... | collective-permute-start | bytes 393224 | tf_op jit(solution)/shard_map/ppermute | solution.py:207
  15.8 2.8 %collective-permute-start.4 = (bf16[256,256]{1,0:T(8,128)(2,1)S(1)}, bf16[256,256]{1,0:T(8,128)(2,1)S(1)}, u32[]{:S(2)}, u32[]{:S(2)}) collective-permute-start(bf16[256,256]{1,0:T(8,128)(2,1)S(1)} %collective-permute-done.3.refs_4_), channel_id=1, source_target_pairs={{32,0},{33,1},{34,2},{35,3},{36,4},{37,5},{38,6},{39,7},{40,8},{41... | collective-permute-start | bytes 393224 | tf_op jit(solution)/shard_map/ppermute | solution.py:207
  19.9 2.3 %collective-permute-start.1 = (bf16[256,256]{1,0:T(8,128)(2,1)S(1)}, bf16[256,256]{1,0:T(8,128)(2,1)S(1)}, u32[]{:S(2)}, u32[]{:S(2)}) collective-permute-start(bf16[256,256]{1,0:T(8,128)(2,1)S(1)} %get-tuple-element.55), channel_id=1, source_target_pairs={{4,0},{5,1},{6,2},{7,3},{8,4},{9,5},{10,6},{11,7},{12,8},{13,9},{1... | collective-permute-start | bytes 393224 | tf_op jit(solution)/shard_map/ppermute | solution.py:207
  24.2 4.0 %build.1.dense_ref = bf16[1024,3072]{1,0:T(8,128)(2,1)S(1)} custom-call(s32[128]{0:T(128)S(1)} %fusion.at_ref, s32[1]{0:T(128)} %bitcast.20.count_ref, bf16[128,128,128]{2,1,0:T(8,128)(2,1)} %bitcast.26), custom_call_target="tpu_custom_call" | custom-call | bytes 10485760 | tf_op jit(solution)/shard_map/build/pallas_call | solution.py:241
  29.3 3.5 %collective-permute-start.12 = (bf16[256,256]{1,0:T(8,128)(2,1)S(1)}, bf16[256,256]{1,0:T(8,128)(2,1)S(1)}, u32[]{:S(2)}, u32[]{:S(2)}) collective-permute-start(bf16[256,256]{1,0:T(8,128)(2,1)S(1)} %get-tuple-element.32), channel_id=1, source_target_pairs={{0,1},{1,0},{2,3},{3,2},{4,5},{5,4},{6,7},{7,6},{8,9},{9,8},{10,11... | collective-permute-start | bytes 393224 | tf_op jit(solution)/shard_map/ppermute | solution.py:219
  35.2 3.5 %collective-permute-done.13.far_ref = bf16[256,256]{1,0:T(8,128)(2,1)S(1)} collective-permute-done((bf16[256,256]{1,0:T(8,128)(2,1)S(1)}, bf16[256,256]{1,0:T(8,128)(2,1)S(1)}, u32[]{:S(2)}, u32[]{:S(2)}) %collective-permute-start.13) | collective-permute-done | bytes 131104 | tf_op jit(solution)/shard_map/ppermute | solution.py:219
  41.1 1.6 %collective-permute-start.29 = (f32[256,128]{1,0:T(8,128)S(1)}, f32[256,128]{1,0:T(8,128)S(1)}, u32[]{:S(2)}, u32[]{:S(2)}) collective-permute-start(f32[256,128]{1,0:T(8,128)S(1)} %get-tuple-element.51), channel_id=1, source_target_pairs={{0,1},{1,0},{2,3},{3,2},{4,5},{5,4},{6,7},{7,6},{8,9},{9,8},{10,11... | collective-permute-start | bytes 393224 | tf_op jit(solution)/shard_map/ppermute | solution.py:219
  43.7 2.5 %collective-permute-start.16 = (bf16[256,256]{1,0:T(8,128)(2,1)S(1)}, bf16[256,256]{1,0:T(8,128)(2,1)S(1)}, u32[]{:S(2)}, u32[]{:S(2)}) collective-permute-start(bf16[256,256]{1,0:T(8,128)(2,1)S(1)} %collective-permute-done.15.d2), channel_id=1, source_target_pairs={{0,1},{1,0},{2,3},{3,2},{4,5},{5,4},{6,7},{7,6},{8,9},{9,8},{10,11... | collective-permute-start | bytes 393224 | tf_op jit(solution)/shard_map/ppermute | solution.py:219
  47.4 2.3 %scatter.1 = (f32[256,256]{1,0:T(8,128)S(1)}, bf16[256,256]{1,0:T(8,128)(2,1)S(1)}, bf16[256,256]{1,0:T(8,128)(2,1)S(1)}, bf16[256,256]{1,0:T(8,128)(2,1)S(1)}, ...) custom-call(s32[1]{0:T(128)} %bitcast.rep_ref, ...), custom_call_target="tpu_custom_call" | custom-call | flops 1610612736 | bytes 8388608 | tf_op jit(solution)/shard_map/scatter/pallas_call | solution.py:278
  49.7 1.6 %collective-permute-start.17 = (bf16[256,256]{1,0:T(8,128)(2,1)}, bf16[256,256]{1,0:T(8,128)(2,1)}, u32[]{:S(2)}, u32[]{:S(2)}) collective-permute-start(bf16[256,256]{1,0:T(8,128)(2,1)} %get-tuple-element.39), channel_id=1, source_target_pairs={{192,0},{193,1},{194,2},{195,3},{196,4},{197,5},{198,6},{199,7},{2... | collective-permute-start | bytes 393224 | tf_op jit(solution)/shard_map/ppermute | solution.py:207
  52.0 9.6 %all-to-all-start = ((f32[64,4,128]{2,1,0:T(4,128)}), f32[64,4,128]{2,1,0:T(4,128)S(1)}, u32[]{:S(2)}, u32[]{:S(2)}) async-start(f32[64,4,128]{2,1,0:T(4,128)} %bitcast.28), calls=%async_computation | async-start | bytes 262144 | tf_op jit(solution)/shard_map/all_to_all | solution.py:312
  61.6 2.6 %collective-permute-start.20 = (bf16[256,256]{1,0:T(8,128)(2,1)}, bf16[256,256]{1,0:T(8,128)(2,1)S(1)}, u32[]{:S(2)}, u32[]{:S(2)}) collective-permute-start(bf16[256,256]{1,0:T(8,128)(2,1)} %copy-done.8), channel_id=1, source_target_pairs={{32,0},{33,1},{34,2},{35,3},{36,4},{37,5},{38,6},{39,7},{40,8},{41... | collective-permute-start | bytes 393224 | tf_op jit(solution)/shard_map/ppermute | solution.py:207
  65.3 6.0 %collective-permute-start.24 = (bf16[256,256]{1,0:T(8,128)(2,1)}, bf16[256,256]{1,0:T(8,128)(2,1)}, u32[]{:S(2)}, u32[]{:S(2)}) collective-permute-start(bf16[256,256]{1,0:T(8,128)(2,1)} %copy-done.6), channel_id=1, source_target_pairs={{4,0},{5,1},{6,2},{7,3},{8,4},{9,5},{10,6},{11,7},{12,8},{13,9},{1... | collective-permute-start | bytes 393224 | tf_op jit(solution)/shard_map/ppermute | solution.py:207
  71.3 1.6 %add_convert_fusion.5 = bf16[256,256]{1,0:T(8,128)(2,1)} fusion(bf16[256,256]{1,0:T(8,128)(2,1)} %collective-permute-done.17, bf16[256,256]{1,0:T(8,128)(2,1)S(1)} %get-tuple-element.38), kind=kLoop, calls=%fused_computation.5 | loop fusion | flops 262144 | bytes 393216 | tf_op jit(solution)/shard_map/convert_element_type | solution.py:222
  72.9 1.5 %collective-permute-start.18 = (bf16[256,256]{1,0:T(8,128)(2,1)}, bf16[256,256]{1,0:T(8,128)(2,1)}, u32[]{:S(2)}, u32[]{:S(2)}) collective-permute-start(bf16[256,256]{1,0:T(8,128)(2,1)} %add_convert_fusion.5), channel_id=1, source_target_pairs={{224,0},{225,1},{226,2},{227,3},{228,4},{229,5},{230,6},{231,7},{2... | collective-permute-start | bytes 393224 | tf_op jit(solution)/shard_map/ppermute | solution.py:207
  77.7 9.8 %all-to-all-start.1 = ((f32[64,4,128]{2,1,0:T(4,128)}), f32[64,4,128]{2,1,0:T(4,128)S(1)}, u32[]{:S(2)}, u32[]{:S(2)}) async-start(f32[64,4,128]{2,1,0:T(4,128)} %spread.1), calls=%async_computation.1 | async-start | bytes 262144 | tf_op jit(solution)/shard_map/all_to_all | solution.py:314
  88.5 7.1 %collective-permute-start.25 = (bf16[256,256]{1,0:T(8,128)(2,1)S(1)}, bf16[256,256]{1,0:T(8,128)(2,1)S(1)}, u32[]{:S(2)}, u32[]{:S(2)}) collective-permute-start(bf16[256,256]{1,0:T(8,128)(2,1)S(1)} %add_convert_fusion.1), channel_id=1, source_target_pairs={{4,0},{5,1},{6,2},{7,3},{8,4},{9,5},{10,6},{11,7},{12,8},{13,9},{1... | collective-permute-start | bytes 393224 | tf_op jit(solution)/shard_map/ppermute | solution.py:207
  95.7 1.6 %add_convert_fusion = bf16[256,256]{1,0:T(8,128)(2,1)} fusion(bf16[256,256]{1,0:T(8,128)(2,1)} %collective-permute-done.26, bf16[256,256]{1,0:T(8,128)(2,1)S(1)} %get-tuple-element.46), kind=kLoop, calls=%fused_computation | loop fusion | flops 262144 | bytes 393216 | tf_op jit(solution)/shard_map/convert_element_type | solution.py:222
  97.3 1.6 %all-to-all-done.1 = f32[64,4,128]{2,1,0:T(4,128)S(1)} async-done(((f32[64,4,128]{2,1,0:T(4,128)}), f32[64,4,128]{2,1,0:T(4,128)S(1)}, u32[]{:S(2)}, u32[]{:S(2)}) %all-to-all-start.1) | async-done | bytes 131104 | tf_op jit(solution)/shard_map/all_to_all | solution.py:314
  101.3 5.1 %collective-permute-start.31 = (f32[256,128]{1,0:T(8,128)S(1)}, f32[256,128]{1,0:T(8,128)S(1)}, u32[]{:S(2)}, u32[]{:S(2)}) collective-permute-start(f32[256,128]{1,0:T(8,128)S(1)} %bitcast.23), channel_id=1, source_target_pairs={{0,1},{1,0},{2,3},{3,2},{4,5},{5,4},{6,7},{7,6},{8,9},{9,8},{10,11... | collective-permute-start | bytes 393224 | tf_op jit(solution)/shard_map/ppermute | solution.py:219
  106.4 2.5 %collective-permute-start.33 = (f32[256,128]{1,0:T(8,128)S(1)}, f32[256,128]{1,0:T(8,128)S(1)}, u32[]{:S(2)}, u32[]{:S(2)}) collective-permute-start(f32[256,128]{1,0:T(8,128)S(1)} %collective-permute-done.32.refs_7_), channel_id=1, source_target_pairs={{0,1},{1,0},{2,3},{3,2},{4,5},{5,4},{6,7},{7,6},{8,9},{9,8},{10,11... | collective-permute-start | bytes 393224 | tf_op jit(solution)/shard_map/ppermute | solution.py:219
  108.9 4.3 %tile_grads.1 = bf16[128,128,128]{2,1,0:T(8,128)(2,1)} custom-call(s32[1]{0:T(128)} %bitcast.rep_ref, s32[128]{0:T(128)S(1)} %fusion.at_ref, s32[1]{0:T(128)} %bitcast.21.count_ref, bf16[256,256]{1,0:T(8,128)(2,1)S(1)} %get-tuple-element.35.d0, bf16[256,256]{1,0:T(8,128)(2,1)S(1)} %collective-permute-done.14.d1, ...), custom_call_target="tpu_custom_call" | custom-call | flops 1610612736 | bytes 8388608 | tf_op jit(solution)/shard_map/tile_grads/pallas_call | solution.py:293
  (85 shorter events, 21.8 us)
Async XLA Ops:
  0.6 15.1 %collective-permute-start.3 = (bf16[256,256]{1,0:T(8,128)(2,1)}, bf16[256,256]{1,0:T(8,128)(2,1)S(1)}, u32[]{:S(2)}, u32[]{:S(2)}) collective-permute-start(bf16[256,256]{1,0:T(8,128)(2,1)} %refs_0_.5), channel_id=1, source_target_pairs={{32,0},{33,1},{34,2},{35,3},{36,4},{37,5},{38,6},{39,7},{40,8},{41... | collective-permute-start | bytes 393224 | tf_op jit(solution)/shard_map/ppermute | solution.py:207
  7.1 11.4 %collective-permute-start = (bf16[256,256]{1,0:T(8,128)(2,1)}, bf16[256,256]{1,0:T(8,128)(2,1)S(1)}, u32[]{:S(2)}, u32[]{:S(2)}) collective-permute-start(bf16[256,256]{1,0:T(8,128)(2,1)} %refs_0_.5), channel_id=1, source_target_pairs={{16,0},{17,1},{18,2},{19,3},{20,4},{21,5},{22,6},{23,7},{248,8},{2... | collective-permute-start | bytes 393224 | tf_op jit(solution)/shard_map/ppermute | solution.py:207
  10.3 9.6 %collective-permute-start.8 = (bf16[256,256]{1,0:T(8,128)(2,1)}, bf16[256,256]{1,0:T(8,128)(2,1)S(1)}, u32[]{:S(2)}, u32[]{:S(2)}) collective-permute-start(bf16[256,256]{1,0:T(8,128)(2,1)} %refs_0_.5), channel_id=1, source_target_pairs={{240,0},{241,1},{242,2},{243,3},{244,4},{245,5},{246,6},{247,7},{2... | collective-permute-start | bytes 393224 | tf_op jit(solution)/shard_map/ppermute | solution.py:207
  10.3 11.9 %collective-permute-start.6 = (bf16[256,256]{1,0:T(8,128)(2,1)}, bf16[256,256]{1,0:T(8,128)(2,1)S(1)}, u32[]{:S(2)}, u32[]{:S(2)}) collective-permute-start(bf16[256,256]{1,0:T(8,128)(2,1)} %refs_0_.5), channel_id=1, source_target_pairs={{224,0},{225,1},{226,2},{227,3},{228,4},{229,5},{230,6},{231,7},{2... | collective-permute-start | bytes 393224 | tf_op jit(solution)/shard_map/ppermute | solution.py:207
  11.0 11.2 %collective-permute-start.2 = (bf16[256,256]{1,0:T(8,128)(2,1)}, bf16[256,256]{1,0:T(8,128)(2,1)S(1)}, u32[]{:S(2)}, u32[]{:S(2)}) collective-permute-start(bf16[256,256]{1,0:T(8,128)(2,1)} %refs_0_.5), channel_id=1, source_target_pairs={{8,0},{9,1},{10,2},{11,3},{12,4},{13,5},{14,6},{15,7},{0,8},{1,9},... | collective-permute-start | bytes 393224 | tf_op jit(solution)/shard_map/ppermute | solution.py:207
  15.8 6.5 %collective-permute-start.4 = (bf16[256,256]{1,0:T(8,128)(2,1)S(1)}, bf16[256,256]{1,0:T(8,128)(2,1)S(1)}, u32[]{:S(2)}, u32[]{:S(2)}) collective-permute-start(bf16[256,256]{1,0:T(8,128)(2,1)S(1)} %collective-permute-done.3.refs_4_), channel_id=1, source_target_pairs={{32,0},{33,1},{34,2},{35,3},{36,4},{37,5},{38,6},{39,7},{40,8},{41... | collective-permute-start | bytes 393224 | tf_op jit(solution)/shard_map/ppermute | solution.py:207
  19.5 8.8 %collective-permute-start.10 = (bf16[256,256]{1,0:T(8,128)(2,1)S(1)}, bf16[256,256]{1,0:T(8,128)(2,1)S(1)}, u32[]{:S(2)}, u32[]{:S(2)}) collective-permute-start(bf16[256,256]{1,0:T(8,128)(2,1)S(1)} %get-tuple-element.54), channel_id=1, source_target_pairs={{12,0},{13,1},{14,2},{15,3},{0,4},{1,5},{2,6},{3,7},{4,8},{5,9},{6... | collective-permute-start | bytes 393224 | tf_op jit(solution)/shard_map/ppermute | solution.py:207
  19.9 8.4 %collective-permute-start.1 = (bf16[256,256]{1,0:T(8,128)(2,1)S(1)}, bf16[256,256]{1,0:T(8,128)(2,1)S(1)}, u32[]{:S(2)}, u32[]{:S(2)}) collective-permute-start(bf16[256,256]{1,0:T(8,128)(2,1)S(1)} %get-tuple-element.55), channel_id=1, source_target_pairs={{4,0},{5,1},{6,2},{7,3},{8,4},{9,5},{10,6},{11,7},{12,8},{13,9},{1... | collective-permute-start | bytes 393224 | tf_op jit(solution)/shard_map/ppermute | solution.py:207
  49.7 21.6 %collective-permute-start.17 = (bf16[256,256]{1,0:T(8,128)(2,1)}, bf16[256,256]{1,0:T(8,128)(2,1)}, u32[]{:S(2)}, u32[]{:S(2)}) collective-permute-start(bf16[256,256]{1,0:T(8,128)(2,1)} %get-tuple-element.39), channel_id=1, source_target_pairs={{192,0},{193,1},{194,2},{195,3},{196,4},{197,5},{198,6},{199,7},{2... | collective-permute-start | bytes 393224 | tf_op jit(solution)/shard_map/ppermute | solution.py:207
  52.0 25.0 %all-to-all-start = ((f32[64,4,128]{2,1,0:T(4,128)}), f32[64,4,128]{2,1,0:T(4,128)S(1)}, u32[]{:S(2)}, u32[]{:S(2)}) async-start(f32[64,4,128]{2,1,0:T(4,128)} %bitcast.28), calls=%async_computation | async-start | bytes 262144 | tf_op jit(solution)/shard_map/all_to_all | solution.py:312
  61.6 12.8 %collective-permute-start.20 = (bf16[256,256]{1,0:T(8,128)(2,1)}, bf16[256,256]{1,0:T(8,128)(2,1)S(1)}, u32[]{:S(2)}, u32[]{:S(2)}) collective-permute-start(bf16[256,256]{1,0:T(8,128)(2,1)} %copy-done.8), channel_id=1, source_target_pairs={{32,0},{33,1},{34,2},{35,3},{36,4},{37,5},{38,6},{39,7},{40,8},{41... | collective-permute-start | bytes 393224 | tf_op jit(solution)/shard_map/ppermute | solution.py:207
  64.1 12.2 %collective-permute-start.22 = (bf16[256,256]{1,0:T(8,128)(2,1)}, bf16[256,256]{1,0:T(8,128)(2,1)S(1)}, u32[]{:S(2)}, u32[]{:S(2)}) collective-permute-start(bf16[256,256]{1,0:T(8,128)(2,1)} %copy-done.7), channel_id=1, source_target_pairs={{252,0},{253,1},{254,2},{255,3},{0,4},{1,5},{2,6},{3,7},{4,8},{5,9... | collective-permute-start | bytes 393224 | tf_op jit(solution)/shard_map/ppermute | solution.py:207
  65.3 22.3 %collective-permute-start.24 = (bf16[256,256]{1,0:T(8,128)(2,1)}, bf16[256,256]{1,0:T(8,128)(2,1)}, u32[]{:S(2)}, u32[]{:S(2)}) collective-permute-start(bf16[256,256]{1,0:T(8,128)(2,1)} %copy-done.6), channel_id=1, source_target_pairs={{4,0},{5,1},{6,2},{7,3},{8,4},{9,5},{10,6},{11,7},{12,8},{13,9},{1... | collective-permute-start | bytes 393224 | tf_op jit(solution)/shard_map/ppermute | solution.py:207
  71.3 24.3 %collective-permute-start.26 = (bf16[256,256]{1,0:T(8,128)(2,1)}, bf16[256,256]{1,0:T(8,128)(2,1)}, u32[]{:S(2)}, u32[]{:S(2)}) collective-permute-start(bf16[256,256]{1,0:T(8,128)(2,1)} %copy-done.5), channel_id=1, source_target_pairs={{32,0},{33,1},{34,2},{35,3},{36,4},{37,5},{38,6},{39,7},{40,8},{41... | collective-permute-start | bytes 393224 | tf_op jit(solution)/shard_map/ppermute | solution.py:207
  72.9 24.3 %collective-permute-start.18 = (bf16[256,256]{1,0:T(8,128)(2,1)}, bf16[256,256]{1,0:T(8,128)(2,1)}, u32[]{:S(2)}, u32[]{:S(2)}) collective-permute-start(bf16[256,256]{1,0:T(8,128)(2,1)} %add_convert_fusion.5), channel_id=1, source_target_pairs={{224,0},{225,1},{226,2},{227,3},{228,4},{229,5},{230,6},{231,7},{2... | collective-permute-start | bytes 393224 | tf_op jit(solution)/shard_map/ppermute | solution.py:207
  75.1 25.5 %collective-permute-start.21 = (bf16[256,256]{1,0:T(8,128)(2,1)}, bf16[256,256]{1,0:T(8,128)(2,1)S(1)}, u32[]{:S(2)}, u32[]{:S(2)}) collective-permute-start(bf16[256,256]{1,0:T(8,128)(2,1)} %add_convert_fusion.3), channel_id=1, source_target_pairs={{32,0},{33,1},{34,2},{35,3},{36,4},{37,5},{38,6},{39,7},{40,8},{41... | collective-permute-start | bytes 393224 | tf_op jit(solution)/shard_map/ppermute | solution.py:207
  77.0 24.3 %collective-permute-start.23 = (bf16[256,256]{1,0:T(8,128)(2,1)}, bf16[256,256]{1,0:T(8,128)(2,1)S(1)}, u32[]{:S(2)}, u32[]{:S(2)}) collective-permute-start(bf16[256,256]{1,0:T(8,128)(2,1)} %add_convert_fusion.2), channel_id=1, source_target_pairs={{252,0},{253,1},{254,2},{255,3},{0,4},{1,5},{2,6},{3,7},{4,8},{5,9... | collective-permute-start | bytes 393224 | tf_op jit(solution)/shard_map/ppermute | solution.py:207
  77.7 21.1 %all-to-all-start.1 = ((f32[64,4,128]{2,1,0:T(4,128)}), f32[64,4,128]{2,1,0:T(4,128)S(1)}, u32[]{:S(2)}, u32[]{:S(2)}) async-start(f32[64,4,128]{2,1,0:T(4,128)} %spread.1), calls=%async_computation.1 | async-start | bytes 262144 | tf_op jit(solution)/shard_map/all_to_all | solution.py:314
  88.5 24.7 %collective-permute-start.25 = (bf16[256,256]{1,0:T(8,128)(2,1)S(1)}, bf16[256,256]{1,0:T(8,128)(2,1)S(1)}, u32[]{:S(2)}, u32[]{:S(2)}) collective-permute-start(bf16[256,256]{1,0:T(8,128)(2,1)S(1)} %add_convert_fusion.1), channel_id=1, source_target_pairs={{4,0},{5,1},{6,2},{7,3},{8,4},{9,5},{10,6},{11,7},{12,8},{13,9},{1... | collective-permute-start | bytes 393224 | tf_op jit(solution)/shard_map/ppermute | solution.py:207
  97.3 16.0 %collective-permute-start.27 = (bf16[256,256]{1,0:T(8,128)(2,1)}, bf16[256,256]{1,0:T(8,128)(2,1)S(1)}, u32[]{:S(2)}, u32[]{:S(2)}) collective-permute-start(bf16[256,256]{1,0:T(8,128)(2,1)} %add_convert_fusion), channel_id=1, source_target_pairs={{16,0},{17,1},{18,2},{19,3},{20,4},{21,5},{22,6},{23,7},{24,8},{25... | collective-permute-start | bytes 393224 | tf_op jit(solution)/shard_map/ppermute | solution.py:207
  98.8 7.5 %collective-permute-start.32 = (f32[256,128]{1,0:T(8,128)S(1)}, f32[256,128]{1,0:T(8,128)S(1)}, u32[]{:S(2)}, u32[]{:S(2)}) collective-permute-start(f32[256,128]{1,0:T(8,128)S(1)} %bitcast.22), channel_id=1, source_target_pairs={{0,2},{1,3},{2,0},{3,1},{4,6},{5,7},{6,4},{7,5},{8,10},{9,11},{10,... | collective-permute-start | bytes 393224 | tf_op jit(solution)/shard_map/ppermute | solution.py:219
  100.6 12.6 %collective-permute-start.19 = (bf16[256,256]{1,0:T(8,128)(2,1)S(1)}, bf16[256,256]{1,0:T(8,128)(2,1)S(1)}, u32[]{:S(2)}, u32[]{:S(2)}) collective-permute-start(bf16[256,256]{1,0:T(8,128)(2,1)S(1)} %add_convert_fusion.4), channel_id=1, source_target_pairs={{224,0},{225,1},{226,2},{227,3},{228,4},{229,5},{230,6},{231,7},{2... | collective-permute-start | bytes 393224 | tf_op jit(solution)/shard_map/ppermute | solution.py:207
  101.3 11.9 %collective-permute-start.31 = (f32[256,128]{1,0:T(8,128)S(1)}, f32[256,128]{1,0:T(8,128)S(1)}, u32[]{:S(2)}, u32[]{:S(2)}) collective-permute-start(f32[256,128]{1,0:T(8,128)S(1)} %bitcast.23), channel_id=1, source_target_pairs={{0,1},{1,0},{2,3},{3,2},{4,5},{5,4},{6,7},{7,6},{8,9},{9,8},{10,11... | collective-permute-start | bytes 393224 | tf_op jit(solution)/shard_map/ppermute | solution.py:219
  106.4 6.9 %collective-permute-start.33 = (f32[256,128]{1,0:T(8,128)S(1)}, f32[256,128]{1,0:T(8,128)S(1)}, u32[]{:S(2)}, u32[]{:S(2)}) collective-permute-start(f32[256,128]{1,0:T(8,128)S(1)} %collective-permute-done.32.refs_7_), channel_id=1, source_target_pairs={{0,1},{1,0},{2,3},{3,2},{4,5},{5,4},{6,7},{7,6},{8,9},{9,8},{10,11... | collective-permute-start | bytes 393224 | tf_op jit(solution)/shard_map/ppermute | solution.py:219
  (21 other events, 94.1 us)

commit v5 on v4

--- a/solution.py
+++ b/solution.py
@@ -124,7 +124,16 @@
         outs[o][...] = total.astype(outs[o].dtype)
 
 
-def spread_kernel(pieces_ref, out_ref):
+def late_sum_kernel(a_ref, b_ref, after_ref, out_ref):
+    out_ref[...] = (a_ref[...].astype(jnp.float32) + b_ref[...].astype(jnp.float32)).astype(jnp.bfloat16)
+
+
+def fold_kernel(a_ref, b_ref, c_ref, after_ref, out_ref):
+    out_ref[...] = a_ref[...] + b_ref[...] + c_ref[...]
+
+
+def spread_kernel(pieces_ref, *refs):
+    out_ref = refs[-1]
     total = jnp.sum(pieces_ref[...], axis=0)
     out_ref[...] = jnp.broadcast_to(total[None], out_ref.shape)
 
@@ -280,12 +289,20 @@
         [SMEM] * 2 + [VMEM] * 5, flops=work, moved=8 << 20,
     )(rep, ring, dense, *daggs)
 
+    firsts = [from_blk(terms[7], 8), from_blk(terms[2], -1), from_blk(terms[10], 1), from_plane(terms[9], -1)]
+    theirs = to_rep(g2 + to_rep(g3, 1), 2)
+    mine = call(fold_kernel, "fold", quarter, [VMEM] * 3 + [ANY])(g0, to_rep(g1, 1), theirs, terms[0])
+    pieces = lax.all_to_all(mine.reshape(n_blk, 4, 128), "blk", 0, 0, tiled=True)
+    spread = call(spread_kernel, "spread", shape((n_blk, 4, 128), jnp.float32), [VMEM] + [ANY] * 4)(pieces, *firsts)
+    def late(a, b):
+        return call(late_sum_kernel, "late_sum", shape(block), [VMEM, VMEM, ANY])(a, b, spread)
+
     up2_sum = add(terms[5], from_blk(terms[6], -16))
-    up_sum = add(terms[4], from_blk(up2_sum, -8))
-    down_sum = add(terms[8], from_blk(terms[7], 8))
-    right_sum = add(terms[1], from_blk(terms[2], -1))
-    left_sum = add(terms[11], from_blk(terms[10], 1))
-    across_sum = add(terms[3], from_plane(terms[9], -1))
+    up_sum = late(terms[4], from_blk(up2_sum, -8))
+    down_sum = late(terms[8], firsts[0])
+    right_sum = late(terms[1], firsts[1])
+    left_sum = late(terms[11], firsts[2])
+    across_sum = late(terms[3], firsts[3])
     arrived = [
         from_blk(up_sum, -8), from_blk(down_sum, 8), from_blk(right_sum, -1), from_blk(left_sum, 1), flip(across_sum)
     ]
@@ -306,11 +323,6 @@
         name="tile_grads",
     )(rep, at, count, *daggs, *feats)
 
-    mine = g0 + to_rep(g1, 1)
-    theirs = g2 + to_rep(g3, 1)
-    mine = mine + to_rep(theirs, 2)
-    pieces = lax.all_to_all(mine.reshape(n_blk, 4, 128), "blk", 0, 0, tiled=True)
-    spread = call(spread_kernel, "spread", shape((n_blk, 4, 128), jnp.float32), [VMEM])(pieces)
     whole = lax.all_to_all(spread, "blk", 0, 0, tiled=True).reshape(256, 128)
     feat_grad, weight_grads = call(
         finish_kernel, "finish", [shape(block), shape((2, 256, 256), jnp.float32)], [SMEM] + [VMEM] * 11,

time: 115 us -> 118 us (1.026)
  starting transfers between devices: 82 us -> 75 us
  waiting for transfers between devices: 6.26 us -> 12.6 us
  local copies, waits for them, and re-layouts: 0.03 us -> 6.27 us
  other arithmetic: 8.81 us -> 3.27 us
  Pallas kernels: 15.6 us -> 19.3 us
    unnamed x18 -> x30, local copies, waits for them, and re-layouts: 0.03 us -> 6.27 us
    ppermute x22, waiting for transfers between devices: 0.06 us -> 5.21 us  [move(): return lax.ppermute(x, ('blk', 'rep'), pairs)]
    convert_element_type x7 -> x2, other arithmetic: 6.5 us -> 1.64 us  [add(): return (a.astype(jnp.float32) + b.astype(jnp.float32)).astype(jnp.bfloat16)]
    ppermute x22, starting transfers between devices: 43.1 us -> 39.5 us  [move(): return lax.ppermute(x, ('blk', 'rep'), pairs)]
    pallas_call x1 -> x7, Pallas kernels: 0.73 us -> 3.86 us  [the longest x5 2.39 us: late(): call(late_sum_kernel, 'late_sum', shape(block), [VMEM, VMEM, ANY])]
    all_to_all x1, starting transfers between devices: 9.84 us -> 7.22 us  [local(): whole = lax.all_to_all(spread, 'blk', 0, 0, tiled=True).reshape(256, 128)]
    all_to_all x1, waiting for transfers between devices: 1.58 us -> 2.78 us  [local(): whole = lax.all_to_all(spread, 'blk', 0, 0, tiled=True).reshape(256, 128)]
  transfers between devices with their start and end apart: 36 -> 36, of which waited for: 3 -> 5; matrix products, arithmetic and copies ran while one was open for 8% -> 3% of each run, Pallas kernels for 11% -> 13%
where the time goes in v5:
time: 118 us
  starting transfers between devices  75 us (64%)
  Pallas kernels  19.3 us (16%)
  waiting for transfers between devices  12.6 us (11%)
  local copies, waits for them, and re-layouts  6.27 us (5%)
  other arithmetic  3.27 us (3%)
  between operations  1.57 us (1%)
    ppermute x22, starting transfers between devices, move(): return lax.ppermute(x, ('blk', 'rep'), pairs)  39.5 us
    ppermute x12, starting transfers between devices, to_rep(): return lax.ppermute(x, 'rep', [(i, i ^ k) for i in range(n_rep)])  19.3 us
    all_to_all x1, starting transfers between devices, local(): lax.all_to_all(mine.reshape(n_blk, 4, 128), 'blk', 0, 0, tiled=True)  8.97 us
    all_to_all x1, starting transfers between devices, local(): whole = lax.all_to_all(spread, 'blk', 0, 0, tiled=True).reshape(256, 128)  7.22 us
    unnamed x30, local copies, waits for them, and re-layouts  6.27 us
    ppermute x22, waiting for transfers between devices, move(): return lax.ppermute(x, ('blk', 'rep'), pairs)  5.21 us
    ppermute x12, waiting for transfers between devices, to_rep(): return lax.ppermute(x, 'rep', [(i, i ^ k) for i in range(n_rep)])  4.62 us
    pallas_call x1, Pallas kernels, local(): call(build_kernel, 'build', shape((1024, 3072)), [SMEM, SMEM, HBM], moved...  4.39 us
  transfers between devices with their start and end apart: 36, of which 5 were waited for; matrix products, arithmetic and copies ran while one was open for 3% of the time, Pallas kernels for 13%

profile of v5, /device:TPU:1, one launch (start us, length us, event | category | flops | bytes accessed | tf_op | source)
XLA Modules:
  0.0 118.0 jit_solution(1688381991918870701)
XLA Ops:
  0.6 6.5 %collective-permute-start.3 = (bf16[256,256]{1,0:T(8,128)(2,1)}, bf16[256,256]{1,0:T(8,128)(2,1)S(1)}, u32[]{:S(2)}, u32[]{:S(2)}) collective-permute-start(bf16[256,256]{1,0:T(8,128)(2,1)} %refs_0_.5), channel_id=1, source_target_pairs={{32,0},{33,1},{34,2},{35,3},{36,4},{37,5},{38,6},{39,7},{40,8},{41... | collective-permute-start | bytes 393224 | tf_op jit(solution)/shard_map/ppermute | solution.py:216
  7.1 3.2 %collective-permute-start = (bf16[256,256]{1,0:T(8,128)(2,1)}, bf16[256,256]{1,0:T(8,128)(2,1)S(1)}, u32[]{:S(2)}, u32[]{:S(2)}) collective-permute-start(bf16[256,256]{1,0:T(8,128)(2,1)} %refs_0_.5), channel_id=1, source_target_pairs={{16,0},{17,1},{18,2},{19,3},{20,4},{21,5},{22,6},{23,7},{248,8},{2... | collective-permute-start | bytes 393224 | tf_op jit(solution)/shard_map/ppermute | solution.py:216
  11.0 4.1 %collective-permute-start.2 = (bf16[256,256]{1,0:T(8,128)(2,1)}, bf16[256,256]{1,0:T(8,128)(2,1)S(1)}, u32[]{:S(2)}, u32[]{:S(2)}) collective-permute-start(bf16[256,256]{1,0:T(8,128)(2,1)} %refs_0_.5), channel_id=1, source_target_pairs={{8,0},{9,1},{10,2},{11,3},{12,4},{13,5},{14,6},{15,7},{0,8},{1,9},... | collective-permute-start | bytes 393224 | tf_op jit(solution)/shard_map/ppermute | solution.py:216
  15.8 2.8 %collective-permute-start.4 = (bf16[256,256]{1,0:T(8,128)(2,1)S(1)}, bf16[256,256]{1,0:T(8,128)(2,1)S(1)}, u32[]{:S(2)}, u32[]{:S(2)}) collective-permute-start(bf16[256,256]{1,0:T(8,128)(2,1)S(1)} %collective-permute-done.3.refs_4_), channel_id=1, source_target_pairs={{32,0},{33,1},{34,2},{35,3},{36,4},{37,5},{38,6},{39,7},{40,8},{41... | collective-permute-start | bytes 393224 | tf_op jit(solution)/shard_map/ppermute | solution.py:216
  19.9 2.3 %collective-permute-start.1 = (bf16[256,256]{1,0:T(8,128)(2,1)S(1)}, bf16[256,256]{1,0:T(8,128)(2,1)S(1)}, u32[]{:S(2)}, u32[]{:S(2)}) collective-permute-start(bf16[256,256]{1,0:T(8,128)(2,1)S(1)} %get-tuple-element.55), channel_id=1, source_target_pairs={{4,0},{5,1},{6,2},{7,3},{8,4},{9,5},{10,6},{11,7},{12,8},{13,9},{1... | collective-permute-start | bytes 393224 | tf_op jit(solution)/shard_map/ppermute | solution.py:216
  24.2 4.4 %build.1.dense_ref = bf16[1024,3072]{1,0:T(8,128)(2,1)S(1)} custom-call(s32[128]{0:T(128)S(1)} %fusion.at_ref, s32[1]{0:T(128)} %bitcast.20.count_ref, bf16[128,128,128]{2,1,0:T(8,128)(2,1)} %bitcast.26), custom_call_target="tpu_custom_call" | custom-call | bytes 10485760 | tf_op jit(solution)/shard_map/build/pallas_call | solution.py:250
  29.7 3.1 %collective-permute-start.12 = (bf16[256,256]{1,0:T(8,128)(2,1)S(1)}, bf16[256,256]{1,0:T(8,128)(2,1)S(1)}, u32[]{:S(2)}, u32[]{:S(2)}) collective-permute-start(bf16[256,256]{1,0:T(8,128)(2,1)S(1)} %get-tuple-element.32), channel_id=1, source_target_pairs={{0,1},{1,0},{2,3},{3,2},{4,5},{5,4},{6,7},{7,6},{8,9},{9,8},{10,11... | collective-permute-start | bytes 393224 | tf_op jit(solution)/shard_map/ppermute | solution.py:228
  35.2 3.5 %collective-permute-done.13.far_ref = bf16[256,256]{1,0:T(8,128)(2,1)S(1)} collective-permute-done((bf16[256,256]{1,0:T(8,128)(2,1)S(1)}, bf16[256,256]{1,0:T(8,128)(2,1)S(1)}, u32[]{:S(2)}, u32[]{:S(2)}) %collective-permute-start.13) | collective-permute-done | bytes 131104 | tf_op jit(solution)/shard_map/ppermute | solution.py:228
  38.7 1.2 %update.1 = (bf16[256,256]{1,0:T(8,128)(2,1)}, bf16[256,256]{1,0:T(8,128)(2,1)S(1)}, f32[256,256]{1,0:T(8,128)S(1)}, f32[256,128]{1,0:T(8,128)S(1)}, f32[256,128...) custom-call(s32[1]{0:T(128)} %bitcast.rep_ref, f32[256,256]{1,0:T(8,128)S(1)} %get-tuple-element.29.own_ref, ...), custom_call_target="tpu_custom_call" | custom-call | flops 201326592 | bytes 2097152 | tf_op jit(solution)/shard_map/update/pallas_call | solution.py:275
  41.0 1.6 %collective-permute-start.20 = (f32[256,128]{1,0:T(8,128)S(1)}, f32[256,128]{1,0:T(8,128)S(1)}, u32[]{:S(2)}, u32[]{:S(2)}) collective-permute-start(f32[256,128]{1,0:T(8,128)S(1)} %get-tuple-element.43), channel_id=1, source_target_pairs={{0,1},{1,0},{2,3},{3,2},{4,5},{5,4},{6,7},{7,6},{8,9},{9,8},{10,11... | collective-permute-start | bytes 393224 | tf_op jit(solution)/shard_map/ppermute | solution.py:228
  43.7 2.5 %collective-permute-start.16 = (bf16[256,256]{1,0:T(8,128)(2,1)S(1)}, bf16[256,256]{1,0:T(8,128)(2,1)S(1)}, u32[]{:S(2)}, u32[]{:S(2)}) collective-permute-start(bf16[256,256]{1,0:T(8,128)(2,1)S(1)} %collective-permute-done.15.d2), channel_id=1, source_target_pairs={{0,1},{1,0},{2,3},{3,2},{4,5},{5,4},{6,7},{7,6},{8,9},{9,8},{10,11... | collective-permute-start | bytes 393224 | tf_op jit(solution)/shard_map/ppermute | solution.py:228
  47.4 2.5 %scatter.1 = (f32[256,256]{1,0:T(8,128)S(1)}, bf16[256,256]{1,0:T(8,128)(2,1)S(1)}, bf16[256,256]{1,0:T(8,128)(2,1)}, bf16[256,256]{1,0:T(8,128)(2,1)S(1)}, bf16...) custom-call(s32[1]{0:T(128)} %bitcast.rep_ref, ...), custom_call_target="tpu_custom_call" | custom-call | flops 1610612736 | bytes 8388608 | tf_op jit(solution)/shard_map/scatter/pallas_call | solution.py:287
  53.3 9.0 %all-to-all-start = ((f32[64,4,128]{2,1,0:T(4,128)}), f32[64,4,128]{2,1,0:T(4,128)S(1)}, u32[]{:S(2)}, u32[]{:S(2)}) async-start(f32[64,4,128]{2,1,0:T(4,128)} %bitcast.7), calls=%async_computation | async-start | bytes 262144 | tf_op jit(solution)/shard_map/all_to_all | solution.py:295
  62.3 2.6 %collective-permute-start.22 = (bf16[256,256]{1,0:T(8,128)(2,1)}, bf16[256,256]{1,0:T(8,128)(2,1)S(1)}, u32[]{:S(2)}, u32[]{:S(2)}) collective-permute-start(bf16[256,256]{1,0:T(8,128)(2,1)} %get-tuple-element.44), channel_id=1, source_target_pairs={{32,0},{33,1},{34,2},{35,3},{36,4},{37,5},{38,6},{39,7},{40,8},{41... | collective-permute-start | bytes 393224 | tf_op jit(solution)/shard_map/ppermute | solution.py:216
  66.1 6.0 %collective-permute-start.24 = (bf16[256,256]{1,0:T(8,128)(2,1)}, bf16[256,256]{1,0:T(8,128)(2,1)S(1)}, u32[]{:S(2)}, u32[]{:S(2)}) collective-permute-start(bf16[256,256]{1,0:T(8,128)(2,1)} %get-tuple-element.46), channel_id=1, source_target_pairs={{4,0},{5,1},{6,2},{7,3},{8,4},{9,5},{10,6},{11,7},{12,8},{13,9},{1... | collective-permute-start | bytes 393224 | tf_op jit(solution)/shard_map/ppermute | solution.py:216
  72.1 3.3 %collective-permute-done.23.refs_1_.b_ref = bf16[256,256]{1,0:T(8,128)(2,1)S(1)} collective-permute-done((bf16[256,256]{1,0:T(8,128)(2,1)}, bf16[256,256]{1,0:T(8,128)(2,1)S(1)}, u32[]{:S(2)}, u32[]{:S(2)}) %collective-permute-start.23) | collective-permute-done | bytes 131104 | tf_op jit(solution)/shard_map/ppermute | solution.py:216
  75.4 1.9 %collective-permute-done.25.refs_3_.b_ref = bf16[256,256]{1,0:T(8,128)(2,1)S(1)} collective-permute-done((bf16[256,256]{1,0:T(8,128)(2,1)}, bf16[256,256]{1,0:T(8,128)(2,1)S(1)}, u32[]{:S(2)}, u32[]{:S(2)}) %collective-permute-start.25) | collective-permute-done | bytes 131104 | tf_op jit(solution)/shard_map/ppermute | solution.py:216
  78.0 7.2 %all-to-all-start.1 = ((f32[64,4,128]{2,1,0:T(4,128)}), f32[64,4,128]{2,1,0:T(4,128)S(1)}, u32[]{:S(2)}, u32[]{:S(2)}) async-start(f32[64,4,128]{2,1,0:T(4,128)} %spread.1.after_ref), calls=%async_computation.1 | async-start | bytes 262144 | tf_op jit(solution)/shard_map/all_to_all | solution.py:326
  85.2 1.6 %add_convert_fusion = bf16[256,256]{1,0:T(8,128)(2,1)} fusion(bf16[256,256]{1,0:T(8,128)(2,1)} %collective-permute-done.17, bf16[256,256]{1,0:T(8,128)(2,1)S(1)} %get-tuple-element.38), kind=kLoop, calls=%fused_computation | loop fusion | flops 262144 | bytes 393216 | tf_op jit(solution)/shard_map/convert_element_type | solution.py:231
  89.4 1.7 %collective-permute-start.27 = (bf16[256,256]{1,0:T(8,128)(2,1)}, bf16[256,256]{1,0:T(8,128)(2,1)S(1)}, u32[]{:S(2)}, u32[]{:S(2)}) collective-permute-start(bf16[256,256]{1,0:T(8,128)(2,1)} %late_sum.6), channel_id=1, source_target_pairs={{32,0},{33,1},{34,2},{35,3},{36,4},{37,5},{38,6},{39,7},{40,8},{41... | collective-permute-start | bytes 393224 | tf_op jit(solution)/shard_map/ppermute | solution.py:216
  93.7 2.8 %all-to-all-done.1 = f32[64,4,128]{2,1,0:T(4,128)S(1)} async-done(((f32[64,4,128]{2,1,0:T(4,128)}), f32[64,4,128]{2,1,0:T(4,128)S(1)}, u32[]{:S(2)}, u32[]{:S(2)}) %all-to-all-start.1) | async-done | bytes 131104 | tf_op jit(solution)/shard_map/all_to_all | solution.py:326
  98.3 4.1 %collective-permute-start.29 = (bf16[256,256]{1,0:T(8,128)(2,1)S(1)}, bf16[256,256]{1,0:T(8,128)(2,1)S(1)}, u32[]{:S(2)}, u32[]{:S(2)}) collective-permute-start(bf16[256,256]{1,0:T(8,128)(2,1)S(1)} %late_sum.8), channel_id=1, source_target_pairs={{4,0},{5,1},{6,2},{7,3},{8,4},{9,5},{10,6},{11,7},{12,8},{13,9},{1... | collective-permute-start | bytes 393224 | tf_op jit(solution)/shard_map/ppermute | solution.py:216
  105.0 7.5 %collective-permute-start.31 = (f32[256,128]{1,0:T(8,128)S(1)}, f32[256,128]{1,0:T(8,128)S(1)}, u32[]{:S(2)}, u32[]{:S(2)}) collective-permute-start(f32[256,128]{1,0:T(8,128)S(1)} %bitcast.23), channel_id=1, source_target_pairs={{0,1},{1,0},{2,3},{3,2},{4,5},{5,4},{6,7},{7,6},{8,9},{9,8},{10,11... | collective-permute-start | bytes 393224 | tf_op jit(solution)/shard_map/ppermute | solution.py:228
  112.6 4.3 %tile_grads.1 = bf16[128,128,128]{2,1,0:T(8,128)(2,1)} custom-call(s32[1]{0:T(128)} %bitcast.rep_ref, s32[128]{0:T(128)S(1)} %fusion.at_ref, s32[1]{0:T(128)} %bitcast.21.count_ref, bf16[256,256]{1,0:T(8,128)(2,1)S(1)} %get-tuple-element.35.d0, bf16[256,256]{1,0:T(8,128)(2,1)S(1)} %collective-permute-done.14.d1, ...), custom_call_target="tpu_custom_call" | custom-call | flops 1610612736 | bytes 8388608 | tf_op jit(solution)/shard_map/tile_grads/pallas_call | solution.py:310
  (97 shorter events, 27.0 us)
Async XLA Ops:
  0.6 15.1 %collective-permute-start.3 = (bf16[256,256]{1,0:T(8,128)(2,1)}, bf16[256,256]{1,0:T(8,128)(2,1)S(1)}, u32[]{:S(2)}, u32[]{:S(2)}) collective-permute-start(bf16[256,256]{1,0:T(8,128)(2,1)} %refs_0_.5), channel_id=1, source_target_pairs={{32,0},{33,1},{34,2},{35,3},{36,4},{37,5},{38,6},{39,7},{40,8},{41... | collective-permute-start | bytes 393224 | tf_op jit(solution)/shard_map/ppermute | solution.py:216
  7.1 11.4 %collective-permute-start = (bf16[256,256]{1,0:T(8,128)(2,1)}, bf16[256,256]{1,0:T(8,128)(2,1)S(1)}, u32[]{:S(2)}, u32[]{:S(2)}) collective-permute-start(bf16[256,256]{1,0:T(8,128)(2,1)} %refs_0_.5), channel_id=1, source_target_pairs={{16,0},{17,1},{18,2},{19,3},{20,4},{21,5},{22,6},{23,7},{248,8},{2... | collective-permute-start | bytes 393224 | tf_op jit(solution)/shard_map/ppermute | solution.py:216
  10.3 9.6 %collective-permute-start.8 = (bf16[256,256]{1,0:T(8,128)(2,1)}, bf16[256,256]{1,0:T(8,128)(2,1)S(1)}, u32[]{:S(2)}, u32[]{:S(2)}) collective-permute-start(bf16[256,256]{1,0:T(8,128)(2,1)} %refs_0_.5), channel_id=1, source_target_pairs={{240,0},{241,1},{242,2},{243,3},{244,4},{245,5},{246,6},{247,7},{2... | collective-permute-start | bytes 393224 | tf_op jit(solution)/shard_map/ppermute | solution.py:216
  10.3 11.9 %collective-permute-start.6 = (bf16[256,256]{1,0:T(8,128)(2,1)}, bf16[256,256]{1,0:T(8,128)(2,1)S(1)}, u32[]{:S(2)}, u32[]{:S(2)}) collective-permute-start(bf16[256,256]{1,0:T(8,128)(2,1)} %refs_0_.5), channel_id=1, source_target_pairs={{224,0},{225,1},{226,2},{227,3},{228,4},{229,5},{230,6},{231,7},{2... | collective-permute-start | bytes 393224 | tf_op jit(solution)/shard_map/ppermute | solution.py:216
  11.0 11.2 %collective-permute-start.2 = (bf16[256,256]{1,0:T(8,128)(2,1)}, bf16[256,256]{1,0:T(8,128)(2,1)S(1)}, u32[]{:S(2)}, u32[]{:S(2)}) collective-permute-start(bf16[256,256]{1,0:T(8,128)(2,1)} %refs_0_.5), channel_id=1, source_target_pairs={{8,0},{9,1},{10,2},{11,3},{12,4},{13,5},{14,6},{15,7},{0,8},{1,9},... | collective-permute-start | bytes 393224 | tf_op jit(solution)/shard_map/ppermute | solution.py:216
  15.8 6.5 %collective-permute-start.4 = (bf16[256,256]{1,0:T(8,128)(2,1)S(1)}, bf16[256,256]{1,0:T(8,128)(2,1)S(1)}, u32[]{:S(2)}, u32[]{:S(2)}) collective-permute-start(bf16[256,256]{1,0:T(8,128)(2,1)S(1)} %collective-permute-done.3.refs_4_), channel_id=1, source_target_pairs={{32,0},{33,1},{34,2},{35,3},{36,4},{37,5},{38,6},{39,7},{40,8},{41... | collective-permute-start | bytes 393224 | tf_op jit(solution)/shard_map/ppermute | solution.py:216
  19.5 9.2 %collective-permute-start.10 = (bf16[256,256]{1,0:T(8,128)(2,1)S(1)}, bf16[256,256]{1,0:T(8,128)(2,1)S(1)}, u32[]{:S(2)}, u32[]{:S(2)}) collective-permute-start(bf16[256,256]{1,0:T(8,128)(2,1)S(1)} %get-tuple-element.54), channel_id=1, source_target_pairs={{12,0},{13,1},{14,2},{15,3},{0,4},{1,5},{2,6},{3,7},{4,8},{5,9},{6... | collective-permute-start | bytes 393224 | tf_op jit(solution)/shard_map/ppermute | solution.py:216
  19.9 8.7 %collective-permute-start.1 = (bf16[256,256]{1,0:T(8,128)(2,1)S(1)}, bf16[256,256]{1,0:T(8,128)(2,1)S(1)}, u32[]{:S(2)}, u32[]{:S(2)}) collective-permute-start(bf16[256,256]{1,0:T(8,128)(2,1)S(1)} %get-tuple-element.55), channel_id=1, source_target_pairs={{4,0},{5,1},{6,2},{7,3},{8,4},{9,5},{10,6},{11,7},{12,8},{13,9},{1... | collective-permute-start | bytes 393224 | tf_op jit(solution)/shard_map/ppermute | solution.py:216
  22.2 6.4 %collective-permute-start.9 = (bf16[256,256]{1,0:T(8,128)(2,1)S(1)}, bf16[256,256]{1,0:T(8,128)(2,1)S(1)}, u32[]{:S(2)}, u32[]{:S(2)}) collective-permute-start(bf16[256,256]{1,0:T(8,128)(2,1)S(1)} %collective-permute-done.refs_3_), channel_id=1, source_target_pairs={{8,0},{9,1},{10,2},{11,3},{12,4},{13,5},{14,6},{15,7},{0,8},{1,9},... | collective-permute-start | bytes 393224 | tf_op jit(solution)/shard_map/ppermute | solution.py:216
  22.2 6.4 %collective-permute-start.7 = (bf16[256,256]{1,0:T(8,128)(2,1)S(1)}, bf16[256,256]{1,0:T(8,128)(2,1)S(1)}, u32[]{:S(2)}, u32[]{:S(2)}) collective-permute-start(bf16[256,256]{1,0:T(8,128)(2,1)S(1)} %collective-permute-done.6.refs_8_), channel_id=1, source_target_pairs={{224,0},{225,1},{226,2},{227,3},{228,4},{229,5},{230,6},{231,7},{2... | collective-permute-start | bytes 393224 | tf_op jit(solution)/shard_map/ppermute | solution.py:216
  53.3 23.9 %all-to-all-start = ((f32[64,4,128]{2,1,0:T(4,128)}), f32[64,4,128]{2,1,0:T(4,128)S(1)}, u32[]{:S(2)}, u32[]{:S(2)}) async-start(f32[64,4,128]{2,1,0:T(4,128)} %bitcast.7), calls=%async_computation | async-start | bytes 262144 | tf_op jit(solution)/shard_map/all_to_all | solution.py:295
  62.3 9.8 %collective-permute-start.22 = (bf16[256,256]{1,0:T(8,128)(2,1)}, bf16[256,256]{1,0:T(8,128)(2,1)S(1)}, u32[]{:S(2)}, u32[]{:S(2)}) collective-permute-start(bf16[256,256]{1,0:T(8,128)(2,1)} %get-tuple-element.44), channel_id=1, source_target_pairs={{32,0},{33,1},{34,2},{35,3},{36,4},{37,5},{38,6},{39,7},{40,8},{41... | collective-permute-start | bytes 393224 | tf_op jit(solution)/shard_map/ppermute | solution.py:216
  64.9 10.5 %collective-permute-start.23 = (bf16[256,256]{1,0:T(8,128)(2,1)}, bf16[256,256]{1,0:T(8,128)(2,1)S(1)}, u32[]{:S(2)}, u32[]{:S(2)}) collective-permute-start(bf16[256,256]{1,0:T(8,128)(2,1)} %get-tuple-element.45), channel_id=1, source_target_pairs={{252,0},{253,1},{254,2},{255,3},{0,4},{1,5},{2,6},{3,7},{4,8},{5,9... | collective-permute-start | bytes 393224 | tf_op jit(solution)/shard_map/ppermute | solution.py:216
  66.1 9.3 %collective-permute-start.24 = (bf16[256,256]{1,0:T(8,128)(2,1)}, bf16[256,256]{1,0:T(8,128)(2,1)S(1)}, u32[]{:S(2)}, u32[]{:S(2)}) collective-permute-start(bf16[256,256]{1,0:T(8,128)(2,1)} %get-tuple-element.46), channel_id=1, source_target_pairs={{4,0},{5,1},{6,2},{7,3},{8,4},{9,5},{10,6},{11,7},{12,8},{13,9},{1... | collective-permute-start | bytes 393224 | tf_op jit(solution)/shard_map/ppermute | solution.py:216
  72.1 13.2 %collective-permute-start.17 = (bf16[256,256]{1,0:T(8,128)(2,1)}, bf16[256,256]{1,0:T(8,128)(2,1)}, u32[]{:S(2)}, u32[]{:S(2)}) collective-permute-start(bf16[256,256]{1,0:T(8,128)(2,1)} %copy-done.13), channel_id=1, source_target_pairs={{192,0},{193,1},{194,2},{195,3},{196,4},{197,5},{198,6},{199,7},{2... | collective-permute-start | bytes 393224 | tf_op jit(solution)/shard_map/ppermute | solution.py:216
  78.0 18.5 %all-to-all-start.1 = ((f32[64,4,128]{2,1,0:T(4,128)}), f32[64,4,128]{2,1,0:T(4,128)S(1)}, u32[]{:S(2)}, u32[]{:S(2)}) async-start(f32[64,4,128]{2,1,0:T(4,128)} %spread.1.after_ref), calls=%async_computation.1 | async-start | bytes 262144 | tf_op jit(solution)/shard_map/all_to_all | solution.py:326
  86.8 16.4 %collective-permute-start.18 = (bf16[256,256]{1,0:T(8,128)(2,1)}, bf16[256,256]{1,0:T(8,128)(2,1)}, u32[]{:S(2)}, u32[]{:S(2)}) collective-permute-start(bf16[256,256]{1,0:T(8,128)(2,1)} %add_convert_fusion), channel_id=1, source_target_pairs={{224,0},{225,1},{226,2},{227,3},{228,4},{229,5},{230,6},{231,7},{2... | collective-permute-start | bytes 393224 | tf_op jit(solution)/shard_map/ppermute | solution.py:216
  89.4 14.9 %collective-permute-start.27 = (bf16[256,256]{1,0:T(8,128)(2,1)}, bf16[256,256]{1,0:T(8,128)(2,1)S(1)}, u32[]{:S(2)}, u32[]{:S(2)}) collective-permute-start(bf16[256,256]{1,0:T(8,128)(2,1)} %late_sum.6), channel_id=1, source_target_pairs={{32,0},{33,1},{34,2},{35,3},{36,4},{37,5},{38,6},{39,7},{40,8},{41... | collective-permute-start | bytes 393224 | tf_op jit(solution)/shard_map/ppermute | solution.py:216
  92.7 12.3 %collective-permute-start.28 = (bf16[256,256]{1,0:T(8,128)(2,1)}, bf16[256,256]{1,0:T(8,128)(2,1)S(1)}, u32[]{:S(2)}, u32[]{:S(2)}) collective-permute-start(bf16[256,256]{1,0:T(8,128)(2,1)} %late_sum.7), channel_id=1, source_target_pairs={{252,0},{253,1},{254,2},{255,3},{0,4},{1,5},{2,6},{3,7},{4,8},{5,9... | collective-permute-start | bytes 393224 | tf_op jit(solution)/shard_map/ppermute | solution.py:216
  96.5 16.0 %collective-permute-start.32 = (f32[256,128]{1,0:T(8,128)S(1)}, f32[256,128]{1,0:T(8,128)S(1)}, u32[]{:S(2)}, u32[]{:S(2)}) collective-permute-start(f32[256,128]{1,0:T(8,128)S(1)} %bitcast.22), channel_id=1, source_target_pairs={{0,2},{1,3},{2,0},{3,1},{4,6},{5,7},{6,4},{7,5},{8,10},{9,11},{10,... | collective-permute-start | bytes 393224 | tf_op jit(solution)/shard_map/ppermute | solution.py:228
  98.3 18.7 %collective-permute-start.29 = (bf16[256,256]{1,0:T(8,128)(2,1)S(1)}, bf16[256,256]{1,0:T(8,128)(2,1)S(1)}, u32[]{:S(2)}, u32[]{:S(2)}) collective-permute-start(bf16[256,256]{1,0:T(8,128)(2,1)S(1)} %late_sum.8), channel_id=1, source_target_pairs={{4,0},{5,1},{6,2},{7,3},{8,4},{9,5},{10,6},{11,7},{12,8},{13,9},{1... | collective-permute-start | bytes 393224 | tf_op jit(solution)/shard_map/ppermute | solution.py:216
  103.3 13.7 %collective-permute-start.30 = (bf16[256,256]{1,0:T(8,128)(2,1)S(1)}, bf16[256,256]{1,0:T(8,128)(2,1)S(1)}, u32[]{:S(2)}, u32[]{:S(2)}) collective-permute-start(bf16[256,256]{1,0:T(8,128)(2,1)S(1)} %late_sum.9), channel_id=1, source_target_pairs={{16,0},{17,1},{18,2},{19,3},{20,4},{21,5},{22,6},{23,7},{24,8},{25... | collective-permute-start | bytes 393224 | tf_op jit(solution)/shard_map/ppermute | solution.py:216
  104.3 12.6 %collective-permute-start.26 = (bf16[256,256]{1,0:T(8,128)(2,1)S(1)}, bf16[256,256]{1,0:T(8,128)(2,1)S(1)}, u32[]{:S(2)}, u32[]{:S(2)}) collective-permute-start(bf16[256,256]{1,0:T(8,128)(2,1)S(1)} %late_sum.5), channel_id=1, source_target_pairs={{224,0},{225,1},{226,2},{227,3},{228,4},{229,5},{230,6},{231,7},{2... | collective-permute-start | bytes 393224 | tf_op jit(solution)/shard_map/ppermute | solution.py:216
  105.0 12.0 %collective-permute-start.31 = (f32[256,128]{1,0:T(8,128)S(1)}, f32[256,128]{1,0:T(8,128)S(1)}, u32[]{:S(2)}, u32[]{:S(2)}) collective-permute-start(f32[256,128]{1,0:T(8,128)S(1)} %bitcast.23), channel_id=1, source_target_pairs={{0,1},{1,0},{2,3},{3,2},{4,5},{5,4},{6,7},{7,6},{8,9},{9,8},{10,11... | collective-permute-start | bytes 393224 | tf_op jit(solution)/shard_map/ppermute | solution.py:228
  (27 other events, 93.3 us)
